TPU v7x, 32 devices: a whole 2x2x4 slice. The times are simulated.
32 devices in a mesh: ctx: 8 (over z, y), head: 4 (over x, core).
Axes of the slice: x: 2, y: 2, z: 4, core: 2. Of those that a mesh axis runs over, the one named last changes fastest.
Arguments:
- queries: bfloat16 [4096, 8192], P('ctx', 'head'), may hold values from -6 to 6
- keys: bfloat16 [4096, 8192], P('ctx', 'head'), may hold values from -6 to 6
- values: bfloat16 [4096, 8192], P('ctx', 'head'), may hold values from -6 to 6
- teacher: bfloat16 [4096, 5120], P('ctx', 'head'), may hold values from -6 to 6
- out_weight: bfloat16 [8192, 5120], P('head'), may hold values from -0.0625 to 0.0625
- valid: int32 [4096], P('ctx'), may hold values from 0 to 1, as said below
Outputs:
- q_grad: float32 [4096, 8192], P('ctx', 'head')
- k_grad: float32 [4096, 8192], P('ctx', 'head')
- v_grad: float32 [4096, 8192], P('ctx', 'head')
Inputs may be any that keep to these rules, and one draw needn't show every extreme that they name: The last token always has valid = 1.
All inputs are finite; a program needn't handle non-finite values.
Results may differ from a plain program's by a relative error of at most 0.012.
Values may be sent and summed in bfloat16 or wider, within the bound.
No kernel may reach another device: no remote copies, remote signals or barrier semaphores. Data moves between devices by JAX's collectives and lax.ppermute only.
A program may use at most 128 MiB of HBM per device.

v0:
```python
import math

import jax
import jax.numpy as jnp
from jax import lax
from jax.sharding import PartitionSpec as P

DH = 128


def on_device(queries, keys, values, teacher, out_weight, valid):
    precise = lax.Precision.HIGHEST
    tok_rows, col_width = queries.shape
    head_count = col_width // DH
    ctx_size = lax.axis_size("ctx")
    attn_scale = 1.0 / math.sqrt(DH * tok_rows * ctx_size)
    blk_rows = math.gcd(tok_rows, 512)
    blk_count = tok_rows // blk_rows
    causal = jnp.tril(jnp.ones((blk_rows, blk_rows), jnp.float32))
    query_b = queries.reshape(blk_count, blk_rows, head_count, DH)
    key_b = keys.reshape(blk_count, blk_rows, head_count, DH)
    value_b = values.reshape(blk_count, blk_rows, head_count, DH)
    query_f = query_b.astype(jnp.float32)
    key_f = key_b.astype(jnp.float32)
    value_f = value_b.astype(jnp.float32)
    block_kv = jnp.einsum("nthd,nthe->nhde", key_b, value_b, preferred_element_type=jnp.float32)
    kv_local = jnp.sum(block_kv, 0)
    count_local = jnp.sum(valid).astype(jnp.float32)
    rank_ids = jnp.arange(ctx_size)
    every_kv, every_count = (
        lax.all_gather(kv_local[None].astype(jnp.bfloat16), "ctx", axis=0, tiled=True).astype(
            jnp.float32
        ),
        lax.all_gather(count_local[None].astype(jnp.bfloat16), "ctx", axis=0, tiled=True).astype(
            jnp.float32
        ),
    )
    before = (rank_ids < lax.axis_index("ctx")).astype(jnp.float32)
    kv_prefix = jnp.einsum("n,nhde->hde", before, every_kv, precision=precise)
    valid_total = jnp.sum(every_count)
    starts = kv_prefix[None] + (jnp.cumsum(block_kv, 0) - block_kv)
    scores = (
        jnp.einsum("nthd,nshd->nhts", query_b, key_b, preferred_element_type=jnp.float32) * causal
    )
    outputs = jnp.einsum("nhts,nshe->nthe", scores, value_f, precision=precise)
    outputs = outputs + jnp.einsum("nthd,nhde->nthe", query_f, starts, precision=precise)
    attn = (attn_scale * outputs).reshape(tok_rows, col_width).astype(jnp.bfloat16)
    terms = jnp.dot(attn, out_weight, preferred_element_type=jnp.float32)
    predicted = lax.psum_scatter(
        terms.astype(jnp.bfloat16), "head", scatter_dimension=1, tiled=True
    ).astype(jnp.float32)
    residual_err = predicted - teacher.astype(jnp.float32)
    factor = tok_rows * ctx_size / valid_total
    error_grad = (valid.astype(jnp.float32)[:, None] * residual_err * factor).astype(jnp.bfloat16)
    attn_grad = lax.dot_general(
        lax.all_gather(error_grad, "head", axis=1, tiled=True),
        out_weight,
        (((1,), (1,)), ((), ())),
        preferred_element_type=jnp.float32,
    )
    grad_f = attn_grad.reshape(blk_count, blk_rows, head_count, DH)
    block_r = jnp.einsum("nthd,nthe->nhde", query_f, grad_f, precision=precise)
    r_local = jnp.sum(block_r, 0)
    every_r = lax.all_gather(r_local[None].astype(jnp.bfloat16), "ctx", axis=0, tiled=True).astype(
        jnp.float32
    )
    behind = (rank_ids > lax.axis_index("ctx")).astype(jnp.float32)
    r_after = jnp.einsum("n,nhde->hde", behind, every_r, precision=precise)
    later = r_after[None] + (r_local[None] - jnp.cumsum(block_r, 0))
    grad_scores = jnp.einsum("nthe,nshe->nhts", grad_f, value_f, precision=precise) * causal
    q_grad = jnp.einsum("nhts,nshd->nthd", grad_scores, key_f, precision=precise)
    q_grad = q_grad + jnp.einsum("nhde,nthe->nthd", starts, grad_f, precision=precise)
    k_grad = jnp.einsum("nhts,nthd->nshd", grad_scores, query_f, precision=precise)
    k_grad = k_grad + jnp.einsum("nhde,nshe->nshd", later, value_f, precision=precise)
    v_grad = jnp.einsum("nhts,nthe->nshe", scores, grad_f, precision=precise)
    v_grad = v_grad + jnp.einsum("nhde,nshd->nshe", later, key_f, precision=precise)
    return (
        (attn_scale * q_grad).reshape(tok_rows, col_width),
        (attn_scale * k_grad).reshape(tok_rows, col_width),
        (attn_scale * v_grad).reshape(tok_rows, col_width),
    )


def solution(mesh):
    in_specs = (
        P("ctx", "head"),
        P("ctx", "head"),
        P("ctx", "head"),
        P("ctx", "head"),
        P("head", None),
        P("ctx"),
    )
    out_specs = (P("ctx", "head"), P("ctx", "head"), P("ctx", "head"))
    return jax.shard_map(
        on_device, mesh=mesh, in_specs=in_specs, out_specs=out_specs, check_vma=False
    )
```

profile of v0, /device:TPU:0, one launch (start us, length us, event | category | flops | bytes accessed | tf_op | source)
XLA Modules:
  0.0 365.6 jit_solution(6640436087515992993)
XLA Ops:
  7.2 0.0 copy-start
  7.2 0.0 all-gather.8.cloned.1.call-start
  7.2 3.7 %copy.63 = bf16[64,8,16,128]{3,2,1,0:T(8,128)(2,1)} copy(bf16[64,8,16,128]{3,1,2,0:T(8,128)(2,1)} %bitcast.153) | data formatting | bytes 4194304
  10.9 4.3 %copy.33 = bf16[512,16,128]{0,2,1:T(8,128)(2,1)} copy(bf16[512,16,128]{2,1,0:T(8,128)(2,1)} %bitcast.159) | data formatting | bytes 4194304 | tf_op jit(solution)/shard_map/reshape.1
  15.2 3.5 fusion.61
  18.6 0.0 all-gather.8.cloned.1.call-update
  18.7 0.0 reduce-scatter.2.cloned.1.call-start
  18.7 0.1 fusion.50
  18.8 10.5 %fusion.32 = f32[16,512,512]{2,1,0:T(8,128)} fusion(bf16[512,2048]{1,0:T(8,128)(2,1)} %param.7, bf16[512,2048]{1,0:T(8,128)(2,1)} %param.6), kind=kOutput, calls=%fused_computation.34 | convolution fusion | flops 1073741824 | bytes 20971520 | tf_op jit(solution)/shard_map/nthd,nshd->nhts/dot_general | solution.py:43
  29.3 65.6 %all-gather.8.cloned.1.call-done = bf16[128,128,128]{2,1,0:T(8,128)(2,1)} async-done(((bf16[16,128,128]{2,1,0:T(8,128)(2,1)}), bf16[128,128,128]{2,1,0:T(8,128)(2,1)}) %all-gather.8.cloned.1.call-update) | async-done | bytes 4194320 | tf_op jit(solution)/shard_map/all_gather | solution.py:31
  94.9 5.1 %fusion.19 = f32[1,16,128,128]{3,0,2,1:T(1,128)S(1)} fusion(bf16[8,16,128,128]{3,2,1,0:T(8,128)(2,1)} %bitcast.161, s32[]{:T(128)S(6)} %axis_index.19), kind=kOutput, calls=%fused_computation.24 | convolution fusion | flops 4194312 | bytes 5242884 | tf_op jit(solution)/shard_map/n,nhde->hde/dot_general | solution.py:39
  100.0 1.9 fusion.38
  102.0 14.3 %fusion.16 = bf16[16,128,512]{2,1,0:T(8,128)(2,1)S(1)} fusion(f32[16,128,512]{2,1,0:T(8,128)S(1)} %fusion.38, f32[16,512,512]{2,1,0:T(8,128)} %fusion.32, f32[512,512]{1,0:T(8,128)S(1)} %fusion.50, bf16[512,2048]{1,0:T(8,128)(2,1)S(1)} %copy-done), kind=kOutput, calls=%fused_computation.21 | convolution fusion | flops 6449790976 | bytes 26214400 | tf_op jit(solution)/shard_map/nhts,nshe->nthe/dot_general | solution.py:45
  116.3 16.9 %convolution_convert_fusion = bf16[512,5120]{1,0:T(8,128)(2,1)} fusion(bf16[512,2048]{0,1:T(8,128)(2,1)S(1)} %bitcast.162, bf16[2048,5120]{1,0:T(8,128)(2,1)} %param.10), kind=kOutput, calls=%fused_computation.12 | convolution fusion | flops 10740039680 | bytes 28311552 | tf_op jit(solution)/shard_map/dot_general | solution.py:48
  133.2 0.0 reduce-scatter.2.cloned.1.call-update
  133.2 0.0 all-gather.6.cloned.1.call-start
  133.2 0.6 copy-done.11
  133.8 0.6 fusion.60
  135.1 0.6 dynamic-slice
  135.7 0.8 dynamic-update-slice
  136.5 18.7 %all-reduce = bf16[8]{0:T(256)(128)(2,1)S(1)} all-reduce(bf16[8]{0:T(256)(128)(2,1)S(1)} %dynamic-update-slice), channel_id=1, replica_groups=mesh['ctx'=8,'head'=4] {'ctx'}, use_global_device_ids=true, to_apply=%add | all-reduce | flops 8 | bytes 32
  155.2 0.6 convert_reduce_fusion
  156.5 26.5 %reduce-scatter.2.cloned.1.call-done = bf16[512,1280]{1,0:T(8,128)(2,1)} async-done(((bf16[512,5120]{1,0:T(8,128)(2,1)}), bf16[512,1280]{1,0:T(8,128)(2,1)}) %reduce-scatter.2.cloned.1.call-update) | async-done | bytes 1310736 | tf_op jit(solution)/shard_map/reduce_scatter | solution.py:49
  183.0 3.2 multiply_convert_fusion
  186.2 0.0 all-gather.6.cloned.1.call-update
  186.3 0.0 all-gather.10.cloned.1.call-start
  186.3 40.5 %all-gather.6.cloned.1.call-done = bf16[512,5120]{1,0:T(8,128)(2,1)} async-done(((bf16[512,1280]{1,0:T(8,128)(2,1)}), bf16[512,5120]{1,0:T(8,128)(2,1)}) %all-gather.6.cloned.1.call-update) | async-done | bytes 5242896 | tf_op jit(solution)/shard_map/all_gather | solution.py:56
  226.9 16.0 %fusion.62 = f32[512,2048]{0,1:T(8,128)S(1)} fusion(bf16[512,5120]{1,0:T(8,128)(2,1)} %all-gather.6.cloned.1.call-done, bf16[2048,5120]{1,0:T(8,128)(2,1)} %param.10), kind=kOutput, calls=%fused_computation.69 | convolution fusion | flops 10737418240 | bytes 30408704 | tf_op jit(solution)/shard_map/dot_general | solution.py:55
  242.8 0.0 copy-start.1
  242.8 2.0 copy-done.1
  244.9 2.3 fusion.35
  247.2 1.0 copy-done.7
  248.2 0.9 convert_bitcast_fusion
  249.1 2.1 copy.44
  251.1 0.0 all-gather.10.cloned.1.call-update
  251.2 6.6 %fusion.51 = f32[16,512,128]{1,2,0:T(8,128)S(1)} fusion(f32[512,16,128]{0,2,1:T(8,128)} %bitcast.150, f32[16,128,128]{2,1,0:T(8,128)} %bitcast.158, f32[16,128,128]{2,1,0:T(8,128)} %get-tuple-element.12), kind=kOutput, calls=%fused_computation.57 | convolution fusion | flops 1611137024 | bytes 10485760 | tf_op jit(solution)/shard_map/nhde,nthe->nthd/dot_general | solution.py:72
  257.8 10.5 %fusion.27 = f32[16,512,512]{2,1,0:T(8,128)} fusion(f32[512,16,128]{0,2,1:T(8,128)S(1)} %bitcast.152, bf16[512,2048]{1,0:T(8,128)(2,1)S(1)} %copy-done), kind=kOutput, calls=%fused_computation.29 | convolution fusion | flops 6442450944 | bytes 23068672 | tf_op jit(solution)/shard_map/nthe,nshe->nhts/dot_general | solution.py:70
  268.4 16.8 %fusion.14 = f32[1,512,16,128]{1,3,2,0:T(8,128)} fusion(f32[16,512,128]{1,2,0:T(8,128)S(1)} %fusion.51, bf16[512,16,128]{0,2,1:T(8,128)(2,1)S(1)} %copy-done.6, f32[16,512,512]{2,1,0:T(8,128)} %fusion.27, f32[512,512]{1,0:T(8,128)S(1)} %fusion.50), kind=kOutput, calls=%fused_computation.18 | convolution fusion | flops 6448742400 | bytes 28311552 | tf_op jit(solution)/shard_map/nhts,nshd->nthd/dot_general | solution.py:71
  285.2 5.4 %copy.49 = f32[512,2048]{1,0:T(8,128)} copy(f32[512,2048]{0,1:T(8,128)} %bitcast.155) | data formatting | bytes 8388608
  290.7 17.2 %fusion.4 = f32[16,128,512]{2,1,0:T(8,128)} fusion(f32[512,16,128]{0,2,1:T(8,128)} %bitcast.151, f32[16,512,512]{2,1,0:T(8,128)} %fusion.32, f32[512,512]{1,0:T(8,128)S(1)} %fusion.50), kind=kOutput, calls=%fused_computation.4 | convolution fusion | flops 6446645248 | bytes 26214400 | tf_op jit(solution)/shard_map/nhts,nthe->nshe/dot_general | solution.py:75
  307.8 12.0 %fusion = f32[16,512,128]{1,2,0:T(8,128)} fusion(f32[16,512,512]{2,1,0:T(8,128)} %fusion.27, f32[512,512]{1,0:T(8,128)S(1)} %fusion.50, bf16[512,2048]{1,0:T(8,128)(2,1)S(1)} %copy-done.5), kind=kOutput, calls=%fused_computation | convolution fusion | flops 6446645248 | bytes 24117248 | tf_op jit(solution)/shard_map/nhts,nthd->nshd/dot_general | solution.py:73
  319.8 4.9 %all-gather.10.cloned.1.call-done = bf16[128,128,128]{2,1,0:T(8,128)(2,1)} async-done(((bf16[16,128,128]{2,1,0:T(8,128)(2,1)}), bf16[128,128,128]{2,1,0:T(8,128)(2,1)}) %all-gather.10.cloned.1.call-update) | async-done | bytes 4194320 | tf_op jit(solution)/shard_map/all_gather | solution.py:64
  324.7 5.9 %fusion.17 = f32[1,16,128,128]{3,0,2,1:T(1,128)} fusion(bf16[8,16,128,128]{3,2,1,0:T(8,128)(2,1)} %bitcast.160, s32[]{:T(128)S(6)} %axis_index.19), kind=kOutput, calls=%fused_computation.22 | convolution fusion | flops 4194312 | bytes 5242884 | tf_op jit(solution)/shard_map/n,nhde->hde/dot_general | solution.py:68
  330.6 3.6 copy.58
  334.2 7.2 %fusion.12 = f32[1,512,16,128]{1,3,2,0:T(8,128)} fusion(f32[16,128,512]{2,1,0:T(8,128)} %fusion.4, f32[1,16,128,128]{2,3,1,0:T(8,128)} %copy.58, f32[16,128,128]{2,1,0:T(8,128)S(1)} %copy-done.8, bf16[512,2048]{1,0:T(8,128)(2,1)} %param.7), kind=kOutput, calls=%fused_computation.14 | convolution fusion | flops 1613234176 | bytes 12582912 | tf_op jit(solution)/shard_map/nhde,nshd->nshe/dot_general | solution.py:76
  341.5 5.3 %copy.51 = f32[512,2048]{1,0:T(8,128)} copy(f32[512,2048]{0,1:T(8,128)} %bitcast.156) | data formatting | bytes 8388608
  346.8 6.5 %fusion.13 = f32[1,512,16,128]{1,3,2,0:T(8,128)} fusion(f32[16,512,128]{1,2,0:T(8,128)} %fusion, f32[1,16,128,128]{2,3,1,0:T(8,128)} %copy.58, f32[16,128,128]{2,1,0:T(8,128)S(1)} %copy-done.8, bf16[512,2048]{1,0:T(8,128)(2,1)S(1)} %copy-done), kind=kOutput, calls=%fused_computation.16 | convolution fusion | flops 1613234176 | bytes 12582912 | tf_op jit(solution)/shard_map/nhde,nshe->nshd/dot_general | solution.py:74
  353.3 5.3 %copy.50 = f32[512,2048]{1,0:T(8,128)} copy(f32[512,2048]{0,1:T(8,128)} %bitcast.154) | data formatting | bytes 8388608
  (22 shorter events, 0.0 us)
Async XLA Ops:
  7.2 8.0 %copy-start = (bf16[512,2048]{1,0:T(8,128)(2,1)S(1)}, bf16[512,2048]{1,0:T(8,128)(2,1)}, u32[]{:S(2)}) copy-start(bf16[512,2048]{1,0:T(8,128)(2,1)} %param.8) | copy-start | bytes 6291460
  7.2 87.7 %all-gather.8.cloned.1.call-start = ((), (), s32[]{:S(2)}) async-start(), calls=%async_computation.3 | async-start | bytes 4718592 | tf_op jit(solution)/shard_map/all_gather | solution.py:31
  18.7 164.3 %reduce-scatter.2.cloned.1.call-start = ((), (), s32[]{:S(2)}) async-start(), calls=%async_computation.1 | async-start | bytes 6553600 | tf_op jit(solution)/shard_map/reduce_scatter | solution.py:49
  94.9 5.1 %copy-start.3 = (bf16[512,2048]{1,0:T(8,128)(2,1)S(1)}, bf16[512,2048]{1,0:T(8,128)(2,1)}, u32[]{:S(2)}) copy-start(bf16[512,2048]{1,0:T(8,128)(2,1)} %param.6) | copy-start | bytes 6291460
  94.9 5.1 %copy-start.9 = (f32[16,128,128]{2,1,0:T(8,128)S(1)}, f32[16,128,128]{2,1,0:T(8,128)}, u32[]{:S(2)}) copy-start(f32[16,128,128]{2,1,0:T(8,128)} %get-tuple-element.12) | copy-start | bytes 3145732
  100.0 2.0 copy-start.10
  133.2 0.7 copy-start.11
  133.2 2.0 copy-start.12
  133.2 93.7 %all-gather.6.cloned.1.call-start = ((), (), s32[]{:S(2)}) async-start(), calls=%async_computation.2 | async-start | bytes 6553600 | tf_op jit(solution)/shard_map/all_gather | solution.py:56
  186.3 138.5 %all-gather.10.cloned.1.call-start = ((), (), s32[]{:S(2)}) async-start(), calls=%async_computation.4 | async-start | bytes 4718592 | tf_op jit(solution)/shard_map/all_gather | solution.py:64
  226.9 18.0 %copy-start.4 = (bf16[512,2048]{1,0:T(8,128)(2,1)S(1)}, bf16[512,2048]{1,0:T(8,128)(2,1)}, u32[]{:S(2)}) copy-start(bf16[512,2048]{1,0:T(8,128)(2,1)} %param.6) | copy-start | bytes 6291460
  242.8 2.0 copy-start.1
  247.2 1.0 copy-start.7
  251.2 6.7 %copy-start.2 = (f32[512,2048]{0,1:T(8,128)S(1)}, f32[512,2048]{0,1:T(8,128)}, u32[]{:S(2)}) copy-start(f32[512,2048]{0,1:T(8,128)} %copy-done.1) | copy-start | bytes 12582916
  257.8 10.6 %copy-start.6 = (bf16[512,16,128]{0,2,1:T(8,128)(2,1)S(1)}, bf16[512,16,128]{0,2,1:T(8,128)(2,1)}, u32[]{:S(2)}) copy-start(bf16[512,16,128]{0,2,1:T(8,128)(2,1)} %copy.33) | copy-start | bytes 6291460
  290.6 17.2 %copy-start.5 = (bf16[512,2048]{1,0:T(8,128)(2,1)S(1)}, bf16[512,2048]{1,0:T(8,128)(2,1)}, u32[]{:S(2)}) copy-start(bf16[512,2048]{1,0:T(8,128)(2,1)} %param.6) | copy-start | bytes 6291460
  319.8 14.4 %copy-start.8 = (f32[16,128,128]{2,1,0:T(8,128)S(1)}, f32[16,128,128]{2,1,0:T(8,128)}, u32[]{:S(2)}) copy-start(f32[16,128,128]{2,1,0:T(8,128)} %copy-done.7) | copy-start | bytes 3145732
Sparse Core Ops, SparseCore 0:
  18.8 76.0 all-gather.7
  133.3 49.6 reduce-scatter.1
  186.4 40.4 all-gather.5
  251.3 73.3 all-gather.9
where the time goes:
time: 373 us; the launch traced here: 366 us
  matrix products  153 us (41%)
  waiting for transfers between devices  138 us (37%)
  local copies, waits for them, and re-layouts  34.7 us (9%)
  blocking collectives  18.7 us (5%)
  between operations  15.7 us (4%)
  other arithmetic  5.47 us (1%)
    all_gather x1, waiting for transfers between devices, on_device(): lax.all_gather(kv_local[None].astype(jnp.bfloat16), 'ctx', axis=0, tiled=...  65.6 us
    all_gather x1, waiting for transfers between devices, on_device(): lax.all_gather(error_grad, 'head', axis=1, tiled=True)  40.5 us
    reduce_scatter x1, waiting for transfers between devices, on_device(): lax.psum_scatter(terms.astype(jnp.bfloat16), 'head', scatter_dimension=1,...  26.5 us
    unnamed x33, local copies, waits for them, and re-layouts  24.8 us
    unnamed x1, blocking collectives  18.7 us
    dot_general x1, matrix products, on_device(): v_grad = jnp.einsum('nhts,nthe->nshe', scores, grad_f, precision=precise)  17.2 us
    dot_general x1, matrix products, on_device(): terms = jnp.dot(attn, out_weight, preferred_element_type=jnp.float32)  16.9 us
    dot_general x1, matrix products, on_device(): jnp.einsum('nhts,nshd->nthd', grad_scores, key_f, precision=precise)  16.8 us
  transfers between devices with their start and end apart: 4, of which 4 were waited for; matrix products, arithmetic and copies ran while one was open for 22% of the time, Pallas kernels for 0%

commit v1 on v0

v1 whole, which is shorter than its diff:
```python
import functools
import math

import jax
import jax.numpy as jnp
from jax import lax
from jax.experimental import pallas as pl
from jax.experimental.pallas import tpu as pltpu
from jax.sharding import PartitionSpec as P

DH = 128
PAIR = 2
VMEM_LIMIT = 40 * 1024 * 1024
NT = (((1,), (1,)), ((), ()))
TN = (((0,), (0,)), ((), ()))
F32 = jnp.float32
BF16 = jnp.bfloat16


def dot(a, b, dims=(((1,), (0,)), ((), ()))):
    return lax.dot_general(a, b, dims, preferred_element_type=F32)


def call(body, grid, in_specs, out_specs, out_shape, flops, moved, aliases=None):
    return pl.pallas_call(
        body,
        grid_spec=pltpu.PrefetchScalarGridSpec(
            num_scalar_prefetch=1, grid=grid, in_specs=in_specs, out_specs=out_specs
        ),
        out_shape=out_shape,
        input_output_aliases=aliases or {},
        compiler_params=pltpu.CompilerParams(vmem_limit_bytes=VMEM_LIMIT),
        cost_estimate=pl.CostEstimate(flops=flops, bytes_accessed=moved, transcendentals=0),
    )


def sds(shape, dtype):
    return jax.ShapeDtypeStruct(shape, dtype)


def lower_mask(n):
    rows = lax.broadcasted_iota(jnp.int32, (n, n), 0)
    cols = lax.broadcasted_iota(jnp.int32, (n, n), 1)
    return rows >= cols


def kv_body(idx, k, v, out):
    for i in range(PAIR):
        c = slice(i * DH, (i + 1) * DH)
        out[i] = dot(k[:, c], v[:, c], TN).astype(BF16)


def kv_states(half, k, v, half_heads):
    rows = k.shape[0]
    steps = half_heads // PAIR
    blk = pl.BlockSpec((rows, PAIR * DH), lambda i, s: (0, s[0] * steps + i))
    return call(
        kv_body,
        (steps,),
        [blk, blk],
        pl.BlockSpec((PAIR, DH, DH), lambda i, s: (i, 0, 0)),
        sds((half_heads, DH, DH), BF16),
        2 * rows * DH * DH * half_heads,
        rows * DH * half_heads * 4,
    )(half, k, v)


def intra_body(block, idx, q, k, v, out):
    mask = lower_mask(block)
    n = q.shape[0] // block
    for i in range(PAIR):
        c = slice(i * DH, (i + 1) * DH)
        state = None
        for b in range(n):
            r = slice(b * block, (b + 1) * block)
            qb, kb, vb = q[r, c], k[r, c], v[r, c]
            s = jnp.where(mask, dot(qb, kb, NT), 0.0).astype(BF16)
            o = dot(s, vb)
            if state is not None:
                o = o + dot(qb, state.astype(BF16))
            if b < n - 1:
                kv = dot(kb, vb, TN)
                state = kv if state is None else state + kv
            out[r, c] = o


def intra(half, q, k, v, half_heads):
    rows = k.shape[0]
    block = math.gcd(rows, 256)
    steps = half_heads // PAIR
    blk = pl.BlockSpec((rows, PAIR * DH), lambda i, s: (0, s[0] * steps + i))
    return call(
        functools.partial(intra_body, block),
        (steps,),
        [blk, blk, blk],
        pl.BlockSpec((rows, PAIR * DH), lambda i, s: (0, i)),
        sds((rows, half_heads * DH), F32),
        4 * rows * (block + DH) * DH * half_heads,
        rows * DH * half_heads * 10,
    )(half, q, k, v)


def attn_body(scale, idx, q, part, state, out):
    for i in range(PAIR):
        c = slice(i * DH, (i + 1) * DH)
        out[:, c] = (scale * (part[:, c] + dot(q[:, c], state[i]))).astype(BF16)


def attend(half, scale, q, part, state, half_heads):
    rows = q.shape[0]
    steps = half_heads // PAIR
    return call(
        functools.partial(attn_body, scale),
        (steps,),
        [
            pl.BlockSpec((rows, PAIR * DH), lambda i, s: (0, s[0] * steps + i)),
            pl.BlockSpec((rows, PAIR * DH), lambda i, s: (0, i)),
            pl.BlockSpec((PAIR, DH, DH), lambda i, s: (i, 0, 0)),
        ],
        pl.BlockSpec((rows, PAIR * DH), lambda i, s: (0, i)),
        sds((rows, half_heads * DH), BF16),
        2 * rows * DH * DH * half_heads,
        rows * DH * half_heads * 8,
    )(half, q, part, state)


def project_body(idx, a0, a1, w0, w1, out):
    out[...] = (dot(a0[...], w0[...]) + dot(a1[...], w1[...])).astype(BF16)


def project(idx, a0, a1, weight, tile, tiles):
    rows, depth = a0.shape
    return call(
        project_body,
        (tiles,),
        [
            pl.BlockSpec((rows, depth), lambda i, s: (0, 0)),
            pl.BlockSpec((rows, depth), lambda i, s: (0, 0)),
            pl.BlockSpec((depth, tile), lambda i, s: (s[0], s[2] + i)),
            pl.BlockSpec((depth, tile), lambda i, s: (s[1], s[2] + i)),
        ],
        pl.BlockSpec((rows, tile), lambda i, s: (0, i)),
        sds((rows, tiles * tile), BF16),
        4 * rows * depth * tile * tiles,
        4 * depth * tile * tiles + 4 * rows * depth + 2 * rows * tile * tiles,
    )(idx, a0, a1, weight, weight)


def grad_body(groups, with_acc, spans, idx, *refs):
    refs = list(refs)
    acc = refs.pop(0)[...] if with_acc else None
    out = refs.pop()
    for _ in range(groups):
        pieces = [refs.pop(0) for _ in spans]
        w = refs.pop(0)
        for piece, (lo, hi) in zip(pieces, spans):
            t = dot(piece[...], w[:, lo:hi], NT)
            acc = t if acc is None else acc + t
    out[...] = acc


def grad_accumulate(idx, groups, acc, spans, weight, width, row_tile):
    depth = weight.shape[0]
    rows = groups[0][0].shape[0]
    in_specs, args = [], []
    if acc is not None:
        in_specs.append(pl.BlockSpec((rows, row_tile), lambda i, s: (0, i)))
        args.append(acc)
    total = 0
    for g, pieces in enumerate(groups):
        for piece in pieces:
            in_specs.append(pl.BlockSpec(piece.shape, lambda i, s: (0, 0)))
            args.append(piece)
            total += piece.shape[1]
        in_specs.append(pl.BlockSpec((row_tile, width), lambda i, s, g=g: (i, s[g])))
        args.append(weight)
    return call(
        functools.partial(grad_body, len(groups), acc is not None, spans),
        (depth // row_tile,),
        in_specs,
        pl.BlockSpec((rows, row_tile), lambda i, s: (0, i)),
        sds((rows, depth), F32),
        2 * rows * depth * total,
        2 * depth * total + 8 * rows * depth,
        {1: 0} if acc is not None else None,
    )(idx, *args)


def last_body(groups, idx, acc, q, *refs):
    *refs, g_out, r_out = refs
    t = acc[...]
    for n in range(groups):
        t = t + dot(refs[2 * n][...], refs[2 * n + 1][...], NT)
    g = t.astype(BF16)
    g_out[...] = g
    for i in range(PAIR):
        c = slice(i * DH, (i + 1) * DH)
        r_out[i] = dot(q[:, c], g[:, c], TN).astype(BF16)


def grad_last(idx, acc, q, pieces, weight, half_heads):
    rows, tile = pieces[0].shape
    steps = half_heads // PAIR
    wide = PAIR * DH
    mine = pl.BlockSpec((rows, wide), lambda i, s: (0, s[0] * steps + i))
    in_specs, args = [mine, mine], [acc, q]
    for n, piece in enumerate(pieces):
        in_specs.append(pl.BlockSpec(piece.shape, lambda i, s: (0, 0)))
        in_specs.append(pl.BlockSpec((wide, tile), lambda i, s, n=n: (s[0] * steps + i, s[1 + n])))
        args += [piece, weight]
    return call(
        functools.partial(last_body, len(pieces)),
        (steps,),
        in_specs,
        [
            pl.BlockSpec((rows, wide), lambda i, s: (0, i)),
            pl.BlockSpec((PAIR, DH, DH), lambda i, s: (i, 0, 0)),
        ],
        [sds((rows, half_heads * DH), BF16), sds((half_heads, DH, DH), BF16)],
        2 * rows * half_heads * DH * (tile * len(pieces) + DH),
        half_heads * DH * (rows * 8 + 2 * tile * len(pieces)),
    )(idx, *args)


def back_body(block, scale, extra, idx, q, k, v, g, state, *refs):
    dq, dk, dv = refs[extra:]
    mask = lower_mask(block)
    n = q.shape[0] // block
    for i in range(PAIR):
        c = slice(i * DH, (i + 1) * DH)
        before = state[i].astype(F32)
        later = None
        dks, dvs = [], []
        for b in range(n):
            r = slice(b * block, (b + 1) * block)
            qb, kb, vb, gb = q[r, c], k[r, c], v[r, c], g[r, c]
            gs = jnp.where(mask, dot(gb, vb, NT), 0.0).astype(BF16)
            s = jnp.where(mask, dot(qb, kb, NT), 0.0).astype(BF16)
            dq[r, c] = scale * (dot(gs, kb) + dot(gb, before.astype(BF16), NT))
            dks.append(dot(gs, qb, TN))
            dvs.append(dot(s, gb, TN))
            if b < n - 1:
                before = before + dot(kb, vb, TN)
        for b in reversed(range(n)):
            r = slice(b * block, (b + 1) * block)
            qb, kb, vb, gb = q[r, c], k[r, c], v[r, c], g[r, c]
            dkb, dvb = dks[b], dvs[b]
            if later is not None:
                lb = later.astype(BF16)
                dkb = dkb + dot(vb, lb, NT)
                dvb = dvb + dot(kb, lb)
            dk[r, c] = scale * dkb
            dv[r, c] = scale * dvb
            if b > 0:
                qg = dot(qb, gb, TN)
                later = qg if later is None else later + qg


def back_local(half, scale, q, k, v, g, state, filled, half_heads):
    rows, width = q.shape
    block = math.gcd(rows, 256)
    steps = half_heads // PAIR
    wide = PAIR * DH
    mine = pl.BlockSpec((rows, wide), lambda i, s: (0, s[0] * steps + i))
    extra = len(filled)
    return call(
        functools.partial(back_body, block, scale, extra),
        (steps,),
        [
            mine,
            mine,
            mine,
            pl.BlockSpec((rows, wide), lambda i, s: (0, i)),
            pl.BlockSpec((PAIR, DH, DH), lambda i, s: (i, 0, 0)),
        ]
        + [pl.BlockSpec(memory_space=pl.ANY)] * extra,
        [mine] * 3,
        [sds((rows, width), F32)] * 3,
        2 * rows * DH * (5 * block + 4 * DH) * half_heads,
        rows * DH * half_heads * 20,
        {6 + n: n for n in range(extra)},
    )(half, q, k, v, g, state, *filled)


def later_body(scale, idx, k, v, later, dk_in, dv_in, dk, dv):
    for i in range(PAIR):
        c = slice(i * DH, (i + 1) * DH)
        dk[:, c] = dk_in[:, c] + scale * dot(v[:, c], later[i], NT)
        dv[:, c] = dv_in[:, c] + scale * dot(k[:, c], later[i])


def add_later(half, scale, k, v, later, dk, dv, half_heads):
    rows, width = k.shape
    steps = half_heads // PAIR
    mine = pl.BlockSpec((rows, PAIR * DH), lambda i, s: (0, s[0] * steps + i))
    return call(
        functools.partial(later_body, scale),
        (steps,),
        [mine, mine, pl.BlockSpec((PAIR, DH, DH), lambda i, s: (i, 0, 0)), mine, mine],
        [mine, mine],
        [sds((rows, width), F32)] * 2,
        4 * rows * DH * DH * half_heads,
        rows * DH * half_heads * 20,
        {4: 0, 5: 1},
    )(half, k, v, later, dk, dv)


def swap(array, axis, bit):
    size = lax.axis_size(axis)
    return lax.ppermute(array, axis, [(i, i ^ (1 << bit)) for i in range(size)])


def scan_states(theirs, mine, ctx_bits, flipped):
    pos = lax.axis_index("ctx")
    if flipped:
        pos = lax.axis_size("ctx") - 1 - pos
    own = mine.astype(F32)
    got = swap(theirs, "ctx", 0).astype(F32)
    total = own + got
    prefix = jnp.zeros_like(total)
    for bit in range(1, ctx_bits):
        other = swap(total.astype(BF16), "ctx", bit).astype(F32)
        prefix = prefix + jnp.where((pos >> bit) & 1 == 1, other, 0.0)
        total = total + other
    upper = pos & 1 == 1
    mine_prefix = (prefix + jnp.where(upper, got, 0.0)).astype(BF16)
    sent = (prefix + jnp.where(upper, 0.0, own)).astype(BF16)
    return mine_prefix, swap(sent, "ctx", 0)


def on_device(queries, keys, values, teacher, out_weight, valid):
    rows, width = queries.shape
    heads = width // DH
    half_heads = heads // 2
    ctx_size = lax.axis_size("ctx")
    ctx_bits = ctx_size.bit_length() - 1
    chips = lax.axis_size("head") // 2
    ctx_id, head_id = lax.axis_index("ctx"), lax.axis_index("head")
    chip, core = head_id // 2, head_id % 2
    scale = 1.0 / math.sqrt(DH * rows * ctx_size)
    piece_width = teacher.shape[1]
    tile = 256 if piece_width % 256 == 0 else 128
    tiles = piece_width // tile
    cuts = [0, 1, tiles - 1, tiles] if tiles > 2 else list(range(tiles + 1))
    spans = [(lo * tile, hi * tile) for lo, hi in zip(cuts[:-1], cuts[1:])]

    my_half = ctx_id & 1
    mine_ix = my_half[None].astype(jnp.int32)
    theirs_ix = 1 - mine_ix

    count = jnp.full((8, 128), jnp.sum(valid), jnp.int32)

    kv_theirs = kv_states(theirs_ix, keys, values, half_heads)
    kv_mine = kv_states(mine_ix, keys, values, half_heads)
    before_mine, before_theirs = scan_states(kv_theirs, kv_mine, ctx_bits, False)
    part_mine = intra(mine_ix, queries, keys, values, half_heads)
    part_theirs = intra(theirs_ix, queries, keys, values, half_heads)
    attn_mine = attend(mine_ix, scale, queries, part_mine, before_mine, half_heads)
    attn_theirs = attend(theirs_ix, scale, queries, part_theirs, before_theirs, half_heads)

    for bit in range(ctx_bits):
        count = count + swap(count, "ctx", bit)
    factor = rows * ctx_size / count[0, 0].astype(F32)
    weigh = (valid.astype(F32) * factor)[:, None]

    def column_tile(to_chip, to_core, lo):
        return (to_chip * 2 + to_core) * tiles + lo // tile

    def terms(to_chip, to_core, lo, hi):
        idx = jnp.stack([my_half, 1 - my_half, column_tile(to_chip, to_core, lo)])
        return project(
            idx.astype(jnp.int32), attn_mine, attn_theirs, out_weight, tile, (hi - lo) // tile
        )

    def shift(array, by):
        size = 2 * chips
        return lax.ppermute(array, "head", [(i, (i + 2 * by) % size) for i in range(size)])

    arrived = []
    for lo, hi in spans:
        got = []
        for by in range(1, chips):
            to_chip = lax.rem(chip + by, chips)
            away = terms(to_chip, 1 - core, lo, hi)
            kept = terms(to_chip, core, lo, hi)
            summed = kept.astype(F32) + swap(away, "head", 0).astype(F32)
            got.append(shift(summed.astype(BF16), by))
        arrived.append(got)
    away = terms(chip, 1 - core, 0, piece_width)
    kept = terms(chip, core, 0, piece_width)
    other_core = swap(away, "head", 0)

    errors = []
    for (lo, hi), got in zip(spans, arrived):
        predicted = kept[:, lo:hi].astype(F32) + other_core[:, lo:hi].astype(F32)
        for piece in got:
            predicted = predicted + piece.astype(F32)
        errors.append((weigh * (predicted - teacher[:, lo:hi].astype(F32))).astype(BF16))

    gathered = [[shift(error, by) for by in range(1, chips)] for error in errors]
    near = [errors, [swap(error, "head", 0) for error in errors]]
    row_tile = PAIR * DH
    idx = jnp.stack([chip * 2 + core, chip * 2 + 1 - core]).astype(jnp.int32)
    acc = grad_accumulate(idx, near, None, spans, out_weight, piece_width, row_tile)

    far, far_ix, last, last_ix = [], [], [], [theirs_ix[0]]
    for by in range(1, chips):
        from_chip = lax.rem(chip + chips - by, chips)
        pieces = [got[by - 1] for got in gathered]
        crossed = [swap(piece, "head", 0) for piece in pieces]
        for from_core, group in ((core, pieces), (1 - core, crossed)):
            far.append(group[:-1])
            far_ix.append(from_chip * 2 + from_core)
            last.append(group[-1])
            last_ix.append(column_tile(from_chip, from_core, spans[-1][0]))
    if far:
        acc = grad_accumulate(
            jnp.stack(far_ix).astype(jnp.int32),
            far, acc, spans[:-1], out_weight, piece_width, row_tile,
        )
    last_ix = jnp.stack(last_ix).astype(jnp.int32)
    g_theirs, r_theirs = grad_last(last_ix, acc, queries, last, out_weight, half_heads)
    g_mine, r_mine = grad_last(
        last_ix.at[0].set(mine_ix[0]), acc, queries, last, out_weight, half_heads
    )
    later_mine, later_theirs = scan_states(r_theirs, r_mine, ctx_bits, True)

    grads = back_local(
        theirs_ix, scale, queries, keys, values, g_theirs, before_theirs, [], half_heads
    )
    q_grad, k_grad, v_grad = back_local(
        mine_ix, scale, queries, keys, values, g_mine, before_mine, grads, half_heads
    )
    k_grad, v_grad = add_later(
        mine_ix, scale, keys, values, later_mine, k_grad, v_grad, half_heads
    )
    k_grad, v_grad = add_later(
        theirs_ix, scale, keys, values, later_theirs, k_grad, v_grad, half_heads
    )
    return q_grad, k_grad, v_grad


def solution(mesh):
    in_specs = (
        P("ctx", "head"),
        P("ctx", "head"),
        P("ctx", "head"),
        P("ctx", "head"),
        P("head", None),
        P("ctx"),
    )
    out_specs = (P("ctx", "head"), P("ctx", "head"), P("ctx", "head"))
    return jax.shard_map(
        on_device, mesh=mesh, in_specs=in_specs, out_specs=out_specs, check_vma=False
    )
```

time: 373 us -> 229 us (0.61); the launches traced: 366 us -> 228 us
  matrix products: 153 us -> 0 us
  Pallas kernels: 0 us -> 102 us
  waiting for transfers between devices: 138 us -> 72.9 us
  starting transfers between devices: 0.16 us -> 28 us
  blocking collectives: 18.7 us -> 0 us
  local copies, waits for them, and re-layouts: 34.7 us -> 17.4 us
  between operations: 15.7 us -> 1.73 us
    dot_general x16 -> x0, matrix products: 153 us -> none  [the longest x1 17.2 us: on_device(): v_grad = jnp.einsum('nhts,nthe->nshe', scores, grad_f, precision=precise)]
    all_gather x3 -> x0, waiting for transfers between devices: 111 us -> none  [the longest x1 65.6 us: on_device(): lax.all_gather(kv_local[None].astype(jnp.bfloat16), 'ctx', axis=0, tiled=...]
    pallas_call x0 -> x22, Pallas kernels: none -> 102 us  [the longest x8 31.6 us: project(): call(project_body, (tiles,), [pl.BlockSpec((rows, depth), lambda i, s: (0...]
    ppermute x0 -> x27, waiting for transfers between devices: none -> 72.9 us  [the longest x6 40.8 us: shift(): lax.ppermute(array, 'head', [(i, (i + 2 * by) % size) for i in range(size)])]
    ppermute x0 -> x27, starting transfers between devices: none -> 28 us  [the longest x21 20.7 us: swap(): return lax.ppermute(array, axis, [(i, i ^ 1 << bit) for i in range(size)])]
    reduce_scatter x1 -> x0, waiting for transfers between devices: 26.5 us -> none  [on_device(): lax.psum_scatter(terms.astype(jnp.bfloat16), 'head', scatter_dimension=1,...]
    unnamed x1 -> x0, blocking collectives: 18.7 us -> none
    unnamed x33 -> x46, local copies, waits for them, and re-layouts: 24.8 us -> 16.3 us
  transfers between devices with their start and end apart: 4 -> 27, of which waited for: 4 -> 12; matrix products, arithmetic and copies ran while one was open for 22% -> 2% of each run, Pallas kernels for 0% -> 40%
where the time goes in v1:
time: 229 us; the launch traced here: 228 us
  Pallas kernels  102 us (45%)
  waiting for transfers between devices  72.9 us (32%)
  starting transfers between devices  28 us (12%)
  local copies, waits for them, and re-layouts  17.4 us (8%)
  other arithmetic  5.62 us (2%)
    ppermute x6, waiting for transfers between devices, shift(): lax.ppermute(array, 'head', [(i, (i + 2 * by) % size) for i in range(size)])  40.8 us
    ppermute x21, waiting for transfers between devices, swap(): return lax.ppermute(array, axis, [(i, i ^ 1 << bit) for i in range(size)])  32.1 us
    pallas_call x8, Pallas kernels, project(): call(project_body, (tiles,), [pl.BlockSpec((rows, depth), lambda i, s: (0...  31.6 us
    pallas_call x2, Pallas kernels, grad_accumulate(): call(functools.partial(grad_body, len(groups), acc is not None, spans), (...  21.7 us
    ppermute x21, starting transfers between devices, swap(): return lax.ppermute(array, axis, [(i, i ^ 1 << bit) for i in range(size)])  20.7 us
    unnamed x46, local copies, waits for them, and re-layouts  16.3 us
    pallas_call x2, Pallas kernels, back_local(): call(functools.partial(back_body, block, scale, extra), (steps,), [mine,...  16 us
    pallas_call x2, Pallas kernels, add_later(): call(functools.partial(later_body, scale), (steps,), [mine, mine, pl.Bloc...  10.4 us
  transfers between devices with their start and end apart: 27, of which 12 were waited for; matrix products, arithmetic and copies ran while one was open for 2% of the time, Pallas kernels for 40%

profile of v1, /device:TPU:0, one launch (start us, length us, event | category | flops | bytes accessed | tf_op | source)
XLA Modules:
  0.0 228.1 jit_solution(15123997765332379534)
XLA Ops:
  0.6 1.6 copy-done.1
  2.2 1.6 copy-done.7
  5.3 3.0 %collective-permute-start.3 = (bf16[8,128,128]{2,1,0:T(8,128)(2,1)S(1)}, bf16[8,128,128]{2,1,0:T(8,128)(2,1)S(1)}, u32[]{:S(2)}, u32[]{:S(2)}) collective-permute-start(bf16[8,128,128]{2,1,0:T(8,128)(2,1)S(1)} %shard_map.87), channel_id=1, source_target_pairs={{0,4},{4,0},{8,12},{12,8},{16,20},{20,16},{24,28},{28,24},{1,5},{5... | collective-permute-start | bytes 786440 | tf_op jit(solution)/shard_map/ppermute | solution.py:310
  9.9 4.8 %collective-permute-done.3 = bf16[8,128,128]{2,1,0:T(8,128)(2,1)S(1)} collective-permute-done((bf16[8,128,128]{2,1,0:T(8,128)(2,1)S(1)}, bf16[8,128,128]{2,1,0:T(8,128)(2,1)S(1)}, u32[]{:S(2)}, u32[]{:S(2)}) %collective-permute-start.3) | collective-permute-done | bytes 262176 | tf_op jit(solution)/shard_map/ppermute | solution.py:310
  14.7 1.9 collective-permute-start.4
  17.9 1.6 collective-permute-start
  19.5 2.7 %collective-permute-done.4 = bf16[8,128,128]{2,1,0:T(8,128)(2,1)S(1)} collective-permute-done((bf16[8,128,128]{2,1,0:T(8,128)(2,1)S(1)}, bf16[8,128,128]{2,1,0:T(8,128)(2,1)S(1)}, u32[]{:S(2)}, u32[]{:S(2)}) %collective-permute-start.4) | collective-permute-done | bytes 262176 | tf_op jit(solution)/shard_map/ppermute | solution.py:310
  22.4 2.6 %collective-permute-start.5 = (bf16[8,128,128]{2,1,0:T(8,128)(2,1)S(1)}, bf16[8,128,128]{2,1,0:T(8,128)(2,1)S(1)}, u32[]{:S(2)}, u32[]{:S(2)}) collective-permute-start(bf16[8,128,128]{2,1,0:T(8,128)(2,1)S(1)} %fusion.5), channel_id=1, source_target_pairs={{0,16},{4,20},{8,24},{12,28},{16,0},{20,4},{24,8},{28,12},{1,17},{... | collective-permute-start | bytes 786440 | tf_op jit(solution)/shard_map/ppermute | solution.py:310
  25.0 1.6 copy-done.3
  26.6 1.6 copy-done.8
  28.2 3.6 %shard_map.89.part = f32[512,1024]{1,0:T(8,128)S(1)} custom-call(s32[1]{0:T(128)S(6)} %sub.42.idx, bf16[512,2048]{1,0:T(8,128)(2,1)S(1)} %copy-done, bf16[512,2048]{1,0:T(8,128)(2,1)S(1)} %copy-done.3, bf16[512,2048]{1,0:T(8,128)(2,1)S(1)} %copy-done.8), custom_call_target="tpu_custom_call" | custom-call | flops 805306368 | bytes 5242880 | tf_op jit(solution)/shard_map/pallas_call | solution.py:92
  33.2 2.4 %collective-permute-done.5 = bf16[8,128,128]{2,1,0:T(8,128)(2,1)S(1)} collective-permute-done((bf16[8,128,128]{2,1,0:T(8,128)(2,1)S(1)}, bf16[8,128,128]{2,1,0:T(8,128)(2,1)S(1)}, u32[]{:S(2)}, u32[]{:S(2)}) %collective-permute-start.5) | collective-permute-done | bytes 262176 | tf_op jit(solution)/shard_map/ppermute | solution.py:310
  37.0 1.6 copy-done.4
  38.6 1.6 copy-done.9
  40.1 3.6 %shard_map.85.part = f32[512,1024]{1,0:T(8,128)S(1)} custom-call(s32[1]{0:T(128)} %bitcast.idx, bf16[512,2048]{1,0:T(8,128)(2,1)S(1)} %copy-done, bf16[512,2048]{1,0:T(8,128)(2,1)S(1)} %copy-done.4, bf16[512,2048]{1,0:T(8,128)(2,1)S(1)} %copy-done.9), custom_call_target="tpu_custom_call" | custom-call | flops 805306368 | bytes 5242880 | tf_op jit(solution)/shard_map/pallas_call | solution.py:92
  48.1 4.5 %shard_map.96 = bf16[512,768]{1,0:T(8,128)(2,1)S(1)} custom-call(s32[3]{0:T(128)S(1)} %get-tuple-element.52.idx, bf16[512,1024]{1,0:T(8,128)(2,1)S(1)} %shard_map.88.a0, bf16[512,1024]{1,0:T(8,128)(2,1)S(1)} %shard_map.90.a1, bf16[2048,5120]{1,0:T(8,128)(2,1)} %refs_3_.7, bf16[2048,5120]{1,0:T(8,128)(2,1)} %refs_3_.7), custom_call_target="tpu_custom_call" | custom-call | flops 1610612736 | bytes 6029312 | tf_op jit(solution)/shard_map/pallas_call | solution.py:133
  53.3 3.4 %collective-permute-start.2 = (s32[8,128]{1,0:T(8,128)S(1)}, s32[8,128]{1,0:T(8,128)S(1)}, u32[]{:S(2)}, u32[]{:S(2)}) collective-permute-start(s32[8,128]{1,0:T(8,128)S(1)} %fusion.14), channel_id=1, source_target_pairs={{0,16},{4,20},{8,24},{12,28},{16,0},{20,4},{24,8},{28,12},{1,17},{... | collective-permute-start | bytes 12296 | tf_op jit(solution)/shard_map/ppermute | solution.py:310
  56.8 1.6 collective-permute-done.2
  59.6 2.5 %shard_map.94 = bf16[512,256]{1,0:T(8,128)(2,1)S(1)} custom-call(s32[3]{0:T(128)S(1)} %get-tuple-element.54.idx, bf16[512,1024]{1,0:T(8,128)(2,1)S(1)} %shard_map.88.a0, bf16[512,1024]{1,0:T(8,128)(2,1)S(1)} %shard_map.90.a1, bf16[2048,5120]{1,0:T(8,128)(2,1)} %refs_3_.7, bf16[2048,5120]{1,0:T(8,128)(2,1)} %refs_3_.7), custom_call_target="tpu_custom_call" | custom-call | flops 536870912 | bytes 3407872 | tf_op jit(solution)/shard_map/pallas_call | solution.py:133
  62.1 6.4 %shard_map.92 = bf16[512,1280]{1,0:T(8,128)(2,1)S(1)} custom-call(s32[3]{0:T(128)S(1)} %get-tuple-element.56.idx, bf16[512,1024]{1,0:T(8,128)(2,1)S(1)} %shard_map.88.a0, bf16[512,1024]{1,0:T(8,128)(2,1)S(1)} %shard_map.90.a1, bf16[2048,5120]{1,0:T(8,128)(2,1)} %refs_3_.7, bf16[2048,5120]{1,0:T(8,128)(2,1)} %refs_3_.7), custom_call_target="tpu_custom_call" | custom-call | flops 2684354560 | bytes 8650752 | tf_op jit(solution)/shard_map/pallas_call | solution.py:133
  69.1 2.5 %shard_map.98 = bf16[512,256]{1,0:T(8,128)(2,1)S(1)} custom-call(s32[3]{0:T(128)S(1)} %get-tuple-element.51.idx, bf16[512,1024]{1,0:T(8,128)(2,1)S(1)} %shard_map.88.a0, bf16[512,1024]{1,0:T(8,128)(2,1)S(1)} %shard_map.90.a1, bf16[2048,5120]{1,0:T(8,128)(2,1)} %refs_3_.7, bf16[2048,5120]{1,0:T(8,128)(2,1)} %refs_3_.7), custom_call_target="tpu_custom_call" | custom-call | flops 536870912 | bytes 3407872 | tf_op jit(solution)/shard_map/pallas_call | solution.py:133
  71.7 2.5 %shard_map.97 = bf16[512,256]{1,0:T(8,128)(2,1)S(1)} custom-call(s32[3]{0:T(128)S(1)} %get-tuple-element.43.idx, bf16[512,1024]{1,0:T(8,128)(2,1)S(1)} %shard_map.88.a0, bf16[512,1024]{1,0:T(8,128)(2,1)S(1)} %shard_map.90.a1, bf16[2048,5120]{1,0:T(8,128)(2,1)} %refs_3_.7, bf16[2048,5120]{1,0:T(8,128)(2,1)} %refs_3_.7), custom_call_target="tpu_custom_call" | custom-call | flops 536870912 | bytes 3407872 | tf_op jit(solution)/shard_map/pallas_call | solution.py:133
  74.2 4.5 %shard_map.95 = bf16[512,768]{1,0:T(8,128)(2,1)S(1)} custom-call(s32[3]{0:T(128)S(1)} %get-tuple-element.53.idx, bf16[512,1024]{1,0:T(8,128)(2,1)S(1)} %shard_map.88.a0, bf16[512,1024]{1,0:T(8,128)(2,1)S(1)} %shard_map.90.a1, bf16[2048,5120]{1,0:T(8,128)(2,1)} %refs_3_.7, bf16[2048,5120]{1,0:T(8,128)(2,1)} %refs_3_.7), custom_call_target="tpu_custom_call" | custom-call | flops 1610612736 | bytes 6029312 | tf_op jit(solution)/shard_map/pallas_call | solution.py:133
  78.9 1.6 collective-permute-start.11
  80.4 6.4 %shard_map.91 = bf16[512,1280]{1,0:T(8,128)(2,1)S(1)} custom-call(s32[3]{0:T(128)S(1)} %get-tuple-element.57.idx, bf16[512,1024]{1,0:T(8,128)(2,1)S(1)} %shard_map.88.a0, bf16[512,1024]{1,0:T(8,128)(2,1)S(1)} %shard_map.90.a1, bf16[2048,5120]{1,0:T(8,128)(2,1)} %refs_3_.7, bf16[2048,5120]{1,0:T(8,128)(2,1)} %refs_3_.7), custom_call_target="tpu_custom_call" | custom-call | flops 2684354560 | bytes 8650752 | tf_op jit(solution)/shard_map/pallas_call | solution.py:133
  86.8 2.5 %shard_map.93 = bf16[512,256]{1,0:T(8,128)(2,1)S(1)} custom-call(s32[3]{0:T(128)S(1)} %get-tuple-element.55.idx, bf16[512,1024]{1,0:T(8,128)(2,1)S(1)} %shard_map.88.a0, bf16[512,1024]{1,0:T(8,128)(2,1)S(1)} %shard_map.90.a1, bf16[2048,5120]{1,0:T(8,128)(2,1)} %refs_3_.7, bf16[2048,5120]{1,0:T(8,128)(2,1)} %refs_3_.7), custom_call_target="tpu_custom_call" | custom-call | flops 536870912 | bytes 3407872 | tf_op jit(solution)/shard_map/pallas_call | solution.py:133
  90.1 1.6 collective-permute-start.13
  91.7 7.6 %collective-permute-done.11 = bf16[512,768]{1,0:T(8,128)(2,1)S(1)} collective-permute-done((bf16[512,768]{1,0:T(8,128)(2,1)S(1)}, bf16[512,768]{1,0:T(8,128)(2,1)S(1)}, u32[]{:S(2)}, u32[]{:S(2)}) %collective-permute-start.11) | collective-permute-done | bytes 786464 | tf_op jit(solution)/shard_map/ppermute | solution.py:377
  99.7 1.6 collective-permute-start.18
  101.3 3.6 %collective-permute-done.9 = bf16[512,256]{1,0:T(8,128)(2,1)S(1)} collective-permute-done((bf16[512,256]{1,0:T(8,128)(2,1)S(1)}, bf16[512,256]{1,0:T(8,128)(2,1)S(1)}, u32[]{:S(2)}, u32[]{:S(2)}) %collective-permute-start.9) | collective-permute-done | bytes 262176 | tf_op jit(solution)/shard_map/ppermute | solution.py:377
  104.9 5.6 %collective-permute-done.13 = bf16[512,256]{1,0:T(8,128)(2,1)S(1)} collective-permute-done((bf16[512,256]{1,0:T(8,128)(2,1)S(1)}, bf16[512,256]{1,0:T(8,128)(2,1)S(1)}, u32[]{:S(2)}, u32[]{:S(2)}) %collective-permute-start.13) | collective-permute-done | bytes 262176 | tf_op jit(solution)/shard_map/ppermute | solution.py:377
  111.5 1.5 collective-permute-start.21
  113.5 19.4 %collective-permute-done.21.refs_0_ = bf16[512,256]{1,0:T(8,128)(2,1)S(1)} collective-permute-done((bf16[512,256]{1,0:T(8,128)(2,1)S(1)}, bf16[512,256]{1,0:T(8,128)(2,1)S(1)}, u32[]{:S(2)}, u32[]{:S(2)}) %collective-permute-start.21) | collective-permute-done | bytes 262176 | tf_op jit(solution)/shard_map/ppermute | solution.py:377
  133.7 4.6 %collective-permute-done.17.refs_1_ = bf16[512,256]{1,0:T(8,128)(2,1)} collective-permute-done((bf16[512,256]{1,0:T(8,128)(2,1)}, bf16[512,256]{1,0:T(8,128)(2,1)}, u32[]{:S(2)}, u32[]{:S(2)}) %collective-permute-start.17) | collective-permute-done | bytes 262176 | tf_op jit(solution)/shard_map/ppermute | solution.py:377
  138.3 11.0 %shard_map.99.refs_0_ = f32[512,2048]{1,0:T(8,128)S(1)} custom-call(s32[2]{0:T(128)S(1)} %pad_add_fusion.1.idx, bf16[512,256]{1,0:T(8,128)(2,1)} %get-tuple-element.46.refs_0_, bf16[512,768]{1,0:T(8,128)(2,1)S(1)} %multiply_convert_fusion.refs_1_, bf16[512,256]{1,0:T(8,128)(2,1)S(1)} %get-tuple-element.45.refs_2_, bf16[2048,5120]{1,0:T(8,128)(2,1)} %refs_3_.7, ...), custom_call_target="tpu_custom_call" | custom-call | flops 5368709120 | bytes 18874368 | tf_op jit(solution)/shard_map/pallas_call | solution.py:177
  149.3 10.7 %shard_map.100.acc = f32[512,2048]{1,0:T(8,128)S(1)} custom-call(s32[2]{0:T(128)S(1)} %pad_add_fusion.idx, f32[512,2048]{1,0:T(8,128)S(1)} %shard_map.99.refs_0_, bf16[512,256]{1,0:T(8,128)(2,1)} %collective-permute-done.17.refs_1_, bf16[512,768]{1,0:T(8,128)(2,1)} %collective-permute-done.18.refs_2_, ...), custom_call_target="tpu_custom_call", output_to_operand_aliasing={{}: (1, {})} | custom-call | flops 4294967296 | bytes 16777216 | tf_op jit(solution)/shard_map/pallas_call | solution.py:177
  160.1 5.0 %shard_map.102 = (bf16[512,1024]{1,0:T(8,128)(2,1)S(1)}, bf16[8,128,128]{2,1,0:T(8,128)(2,1)S(1)}) custom-call(s32[3]{0:T(128)S(1)} %add_add_fusion.idx, f32[512,2048]{1,0:T(8,128)S(1)} %shard_map.100.acc, bf16[512,2048]{1,0:T(8,128)(2,1)S(1)} %copy-done, bf16[512,256]{1,0:T(8,128)(2,1)S(1)} %collective-permute-done.21.refs_0_, bf16[2048,5120]{1,0:T(8,128)(2,1)} %refs_3_.7, ...), custom_call_target="tpu_custom_call" | custom-call | flops 671088640 | bytes 5242880 | tf_op jit(solution)/shard_map/pallas_call | solution.py:211
  166.6 4.8 %shard_map.101 = (bf16[512,1024]{1,0:T(8,128)(2,1)S(1)}, bf16[8,128,128]{2,1,0:T(8,128)(2,1)S(1)}) custom-call(s32[3]{0:T(128)S(1)} %constant_dynamic-update-slice_fusion.idx, f32[512,2048]{1,0:T(8,128)S(1)} %shard_map.100.acc, bf16[512,2048]{1,0:T(8,128)(2,1)S(1)} %copy-done, bf16[512,256]{1,0:T(8,128)(2,1)S(1)} %collective-permute-done.21.refs_0_, ...), custom_call_target="tpu_custom_call" | custom-call | flops 671088640 | bytes 5242880 | tf_op jit(solution)/shard_map/pallas_call | solution.py:211
  172.4 2.4 %collective-permute-done.23 = bf16[8,128,128]{2,1,0:T(8,128)(2,1)S(1)} collective-permute-done((bf16[8,128,128]{2,1,0:T(8,128)(2,1)S(1)}, bf16[8,128,128]{2,1,0:T(8,128)(2,1)S(1)}, u32[]{:S(2)}, u32[]{:S(2)}) %collective-permute-start.23) | collective-permute-done | bytes 262176 | tf_op jit(solution)/shard_map/ppermute | solution.py:310
  175.8 7.0 %collective-permute-done.24 = bf16[8,128,128]{2,1,0:T(8,128)(2,1)S(1)} collective-permute-done((bf16[8,128,128]{2,1,0:T(8,128)(2,1)S(1)}, bf16[8,128,128]{2,1,0:T(8,128)(2,1)S(1)}, u32[]{:S(2)}, u32[]{:S(2)}) %collective-permute-start.24) | collective-permute-done | bytes 262176 | tf_op jit(solution)/shard_map/ppermute | solution.py:310
  183.6 2.9 %collective-permute-start.25 = (bf16[8,128,128]{2,1,0:T(8,128)(2,1)}, bf16[8,128,128]{2,1,0:T(8,128)(2,1)S(1)}, u32[]{:S(2)}, u32[]{:S(2)}) collective-permute-start(bf16[8,128,128]{2,1,0:T(8,128)(2,1)} %fusion.11), channel_id=1, source_target_pairs={{0,16},{4,20},{8,24},{12,28},{16,0},{20,4},{24,8},{28,12},{1,17},{... | collective-permute-start | bytes 786440 | tf_op jit(solution)/shard_map/ppermute | solution.py:310
  186.6 11.1 %collective-permute-done.25 = bf16[8,128,128]{2,1,0:T(8,128)(2,1)S(1)} collective-permute-done((bf16[8,128,128]{2,1,0:T(8,128)(2,1)}, bf16[8,128,128]{2,1,0:T(8,128)(2,1)S(1)}, u32[]{:S(2)}, u32[]{:S(2)}) %collective-permute-start.25) | collective-permute-done | bytes 262176 | tf_op jit(solution)/shard_map/ppermute | solution.py:310
  198.5 1.6 copy-done.5
  200.1 1.6 copy-done.10
  201.7 8.0 %shard_map.103 = (f32[512,2048]{1,0:T(8,128)}, f32[512,2048]{1,0:T(8,128)}, f32[512,2048]{1,0:T(8,128)}) custom-call(s32[1]{0:T(128)S(6)} %sub.42.idx, bf16[512,2048]{1,0:T(8,128)(2,1)S(1)} %copy-done, bf16[512,2048]{1,0:T(8,128)(2,1)S(1)} %copy-done.5, bf16[512,2048]{1,0:T(8,128)(2,1)S(1)} %copy-done.10, bf16[512,1024]{1,0:T(8,128)(2,1)S(1)} %copy-done.20, ...), custom_call_target="tpu_custom_call" | custom-call | flops 1879048192 | bytes 10485760 | tf_op jit(solution)/shard_map/pallas_call | solution.py:266
  209.7 8.0 %shard_map.104 = (f32[512,2048]{1,0:T(8,128)}, f32[512,2048]{1,0:T(8,128)}, f32[512,2048]{1,0:T(8,128)}) custom-call(s32[1]{0:T(128)} %bitcast.idx, bf16[512,2048]{1,0:T(8,128)(2,1)S(1)} %copy-done, bf16[512,2048]{1,0:T(8,128)(2,1)S(1)} %copy-done.6, bf16[512,2048]{1,0:T(8,128)(2,1)S(1)} %copy-done.10, ...), custom_call_target="tpu_custom_call", output_to_operand_aliasing={{0}: (6, {}), {1}: (7, {}), {2}: (8, {})} | custom-call | flops 1879048192 | bytes 10485760 | tf_op jit(solution)/shard_map/pallas_call | solution.py:266
  217.7 5.2 %shard_map.105 = (f32[512,2048]{1,0:T(8,128)}, f32[512,2048]{1,0:T(8,128)}) custom-call(s32[1]{0:T(128)} %bitcast.idx, bf16[512,2048]{1,0:T(8,128)(2,1)S(1)} %copy-done.6, bf16[512,2048]{1,0:T(8,128)(2,1)S(1)} %copy-done.10, bf16[8,128,128]{2,1,0:T(8,128)(2,1)S(1)} %get-tuple-element.47.later, ...), custom_call_target="tpu_custom_call", output_to_operand_aliasing={{0}: (4, {}), {1}: (5, {})} | custom-call | flops 268435456 | bytes 10485760 | tf_op jit(solution)/shard_map/pallas_call | solution.py:296
  222.9 5.2 %shard_map.106 = (f32[512,2048]{1,0:T(8,128)}, f32[512,2048]{1,0:T(8,128)}) custom-call(s32[1]{0:T(128)S(6)} %sub.42.idx, bf16[512,2048]{1,0:T(8,128)(2,1)S(1)} %copy-done.6, bf16[512,2048]{1,0:T(8,128)(2,1)S(1)} %copy-done.10, bf16[8,128,128]{2,1,0:T(8,128)(2,1)S(1)} %collective-permute-done.26.later, ...), custom_call_target="tpu_custom_call", output_to_operand_aliasing={{0}: (4, {}), {1}: (5, {})} | custom-call | flops 268435456 | bytes 10485760 | tf_op jit(solution)/shard_map/pallas_call | solution.py:296
  (98 shorter events, 22.5 us)
Async XLA Ops:
  0.6 1.6 copy-start.1
  2.2 1.6 copy-start.7
  3.8 4.5 %copy-start.2 = (bf16[512,2048]{1,0:T(8,128)(2,1)S(1)}, bf16[512,2048]{1,0:T(8,128)(2,1)}, u32[]{:S(2)}) copy-start(bf16[512,2048]{1,0:T(8,128)(2,1)} %k.15) | copy-start | bytes 6291460
  5.3 11.3 %copy-start.22 = (s32[512]{0:T(512)S(1)}, s32[512]{0:T(512)}, u32[]{:S(2)}) copy-start(s32[512]{0:T(512)} %param.13) | copy-start | bytes 6148
  5.3 9.3 %collective-permute-start.3 = (bf16[8,128,128]{2,1,0:T(8,128)(2,1)S(1)}, bf16[8,128,128]{2,1,0:T(8,128)(2,1)S(1)}, u32[]{:S(2)}, u32[]{:S(2)}) collective-permute-start(bf16[8,128,128]{2,1,0:T(8,128)(2,1)S(1)} %shard_map.87), channel_id=1, source_target_pairs={{0,4},{4,0},{8,12},{12,8},{16,20},{20,16},{24,28},{28,24},{1,5},{5... | collective-permute-start | bytes 786440 | tf_op jit(solution)/shard_map/ppermute | solution.py:310
  8.4 16.6 %copy-start = (bf16[512,2048]{1,0:T(8,128)(2,1)S(1)}, bf16[512,2048]{1,0:T(8,128)(2,1)}, u32[]{:S(2)}) copy-start(bf16[512,2048]{1,0:T(8,128)(2,1)} %q.15) | copy-start | bytes 6291460
  14.7 7.6 %collective-permute-start.4 = (bf16[8,128,128]{2,1,0:T(8,128)(2,1)S(1)}, bf16[8,128,128]{2,1,0:T(8,128)(2,1)S(1)}, u32[]{:S(2)}, u32[]{:S(2)}) collective-permute-start(bf16[8,128,128]{2,1,0:T(8,128)(2,1)S(1)} %fusion.12), channel_id=1, source_target_pairs={{0,8},{4,12},{8,0},{12,4},{16,24},{20,28},{24,16},{28,20},{1,9},{5... | collective-permute-start | bytes 786440 | tf_op jit(solution)/shard_map/ppermute | solution.py:310
  17.9 25.9 %collective-permute-start = (s32[8,128]{1,0:T(8,128)S(1)}, s32[8,128]{1,0:T(8,128)S(1)}, u32[]{:S(2)}, u32[]{:S(2)}) collective-permute-start(s32[8,128]{1,0:T(8,128)S(1)} %broadcast_in_dim.20), channel_id=1, source_target_pairs={{0,4},{4,0},{8,12},{12,8},{16,20},{20,16},{24,28},{28,24},{1,5},{5... | collective-permute-start | bytes 12296 | tf_op jit(solution)/shard_map/ppermute | solution.py:310
  22.4 13.1 %collective-permute-start.5 = (bf16[8,128,128]{2,1,0:T(8,128)(2,1)S(1)}, bf16[8,128,128]{2,1,0:T(8,128)(2,1)S(1)}, u32[]{:S(2)}, u32[]{:S(2)}) collective-permute-start(bf16[8,128,128]{2,1,0:T(8,128)(2,1)S(1)} %fusion.5), channel_id=1, source_target_pairs={{0,16},{4,20},{8,24},{12,28},{16,0},{20,4},{24,8},{28,12},{1,17},{... | collective-permute-start | bytes 786440 | tf_op jit(solution)/shard_map/ppermute | solution.py:310
  25.0 1.6 copy-start.3
  26.6 1.6 copy-start.8
  31.8 1.3 copy-start.11
  35.8 9.4 %copy-start.13 = (bf16[8,128,128]{2,1,0:T(8,128)(2,1)}, bf16[8,128,128]{2,1,0:T(8,128)(2,1)S(1)}, u32[]{:S(2)}) copy-start(bf16[8,128,128]{2,1,0:T(8,128)(2,1)S(1)} %get-tuple-element.50.state) | copy-start | bytes 786436
  35.8 10.8 %collective-permute-start.6 = (bf16[8,128,128]{2,1,0:T(8,128)(2,1)S(1)}, bf16[8,128,128]{2,1,0:T(8,128)(2,1)S(1)}, u32[]{:S(2)}, u32[]{:S(2)}) collective-permute-start(bf16[8,128,128]{2,1,0:T(8,128)(2,1)S(1)} %get-tuple-element.49), channel_id=1, source_target_pairs={{0,4},{4,0},{8,12},{12,8},{16,20},{20,16},{24,28},{28,24},{1,5},{5... | collective-permute-start | bytes 786440 | tf_op jit(solution)/shard_map/ppermute | solution.py:310
  37.0 1.6 copy-start.4
  38.6 1.6 copy-start.9
  44.4 8.3 %collective-permute-start.1 = (s32[8,128]{1,0:T(8,128)S(1)}, s32[8,128]{1,0:T(8,128)S(1)}, u32[]{:S(2)}, u32[]{:S(2)}) collective-permute-start(s32[8,128]{1,0:T(8,128)S(1)} %broadcast_add_fusion), channel_id=1, source_target_pairs={{0,8},{4,12},{8,0},{12,4},{16,24},{20,28},{24,16},{28,20},{1,9},{5... | collective-permute-start | bytes 12296 | tf_op jit(solution)/shard_map/ppermute | solution.py:310
  45.2 1.6 copy-start.12
  46.8 1.4 copy-start.17
  52.6 26.0 %collective-permute-start.10 = (bf16[512,768]{1,0:T(8,128)(2,1)S(1)}, bf16[512,768]{1,0:T(8,128)(2,1)S(1)}, u32[]{:S(2)}, u32[]{:S(2)}) collective-permute-start(bf16[512,768]{1,0:T(8,128)(2,1)S(1)} %shard_map.96), channel_id=1, source_target_pairs={{0,1},{1,0},{2,3},{3,2},{4,5},{5,4},{6,7},{7,6},{8,9},{9,8},{10,11... | collective-permute-start | bytes 2359304 | tf_op jit(solution)/shard_map/ppermute | solution.py:310
  53.3 5.0 %collective-permute-start.2 = (s32[8,128]{1,0:T(8,128)S(1)}, s32[8,128]{1,0:T(8,128)S(1)}, u32[]{:S(2)}, u32[]{:S(2)}) collective-permute-start(s32[8,128]{1,0:T(8,128)S(1)} %fusion.14), channel_id=1, source_target_pairs={{0,16},{4,20},{8,24},{12,28},{16,0},{20,4},{24,8},{28,12},{1,17},{... | collective-permute-start | bytes 12296 | tf_op jit(solution)/shard_map/ppermute | solution.py:310
  62.1 27.3 %collective-permute-start.8 = (bf16[512,256]{1,0:T(8,128)(2,1)S(1)}, bf16[512,256]{1,0:T(8,128)(2,1)S(1)}, u32[]{:S(2)}, u32[]{:S(2)}) collective-permute-start(bf16[512,256]{1,0:T(8,128)(2,1)S(1)} %shard_map.94), channel_id=1, source_target_pairs={{0,1},{1,0},{2,3},{3,2},{4,5},{5,4},{6,7},{7,6},{8,9},{9,8},{10,11... | collective-permute-start | bytes 786440 | tf_op jit(solution)/shard_map/ppermute | solution.py:310
  68.6 23.1 %collective-permute-start.7 = (bf16[512,1280]{1,0:T(8,128)(2,1)S(1)}, bf16[512,1280]{1,0:T(8,128)(2,1)S(1)}, u32[]{:S(2)}, u32[]{:S(2)}) collective-permute-start(bf16[512,1280]{1,0:T(8,128)(2,1)S(1)} %shard_map.92), channel_id=1, source_target_pairs={{0,1},{1,0},{2,3},{3,2},{4,5},{5,4},{6,7},{7,6},{8,9},{9,8},{10,11... | collective-permute-start | bytes 3932168 | tf_op jit(solution)/shard_map/ppermute | solution.py:310
  71.6 18.4 %collective-permute-start.12 = (bf16[512,256]{1,0:T(8,128)(2,1)S(1)}, bf16[512,256]{1,0:T(8,128)(2,1)S(1)}, u32[]{:S(2)}, u32[]{:S(2)}) collective-permute-start(bf16[512,256]{1,0:T(8,128)(2,1)S(1)} %shard_map.98), channel_id=1, source_target_pairs={{0,1},{1,0},{2,3},{3,2},{4,5},{5,4},{6,7},{7,6},{8,9},{9,8},{10,11... | collective-permute-start | bytes 786440 | tf_op jit(solution)/shard_map/ppermute | solution.py:310
  78.9 20.4 %collective-permute-start.11 = (bf16[512,768]{1,0:T(8,128)(2,1)S(1)}, bf16[512,768]{1,0:T(8,128)(2,1)S(1)}, u32[]{:S(2)}, u32[]{:S(2)}) collective-permute-start(bf16[512,768]{1,0:T(8,128)(2,1)S(1)} %add_convert_fusion), channel_id=1, source_target_pairs={{0,2},{1,3},{2,0},{3,1},{4,6},{5,7},{6,4},{7,5},{8,10},{9,11},{10,... | collective-permute-start | bytes 2359304 | tf_op jit(solution)/shard_map/ppermute | solution.py:377
  89.3 10.0 %copy-start.21 = (bf16[512,1280]{1,0:T(8,128)(2,1)S(1)}, bf16[512,1280]{1,0:T(8,128)(2,1)}, u32[]{:S(2)}) copy-start(bf16[512,1280]{1,0:T(8,128)(2,1)} %param.11) | copy-start | bytes 3932164
  89.4 15.5 %collective-permute-start.9 = (bf16[512,256]{1,0:T(8,128)(2,1)S(1)}, bf16[512,256]{1,0:T(8,128)(2,1)S(1)}, u32[]{:S(2)}, u32[]{:S(2)}) collective-permute-start(bf16[512,256]{1,0:T(8,128)(2,1)S(1)} %add_convert_fusion.2), channel_id=1, source_target_pairs={{0,2},{1,3},{2,0},{3,1},{4,6},{5,7},{6,4},{7,5},{8,10},{9,11},{10,... | collective-permute-start | bytes 786440 | tf_op jit(solution)/shard_map/ppermute | solution.py:377
  90.1 20.4 %collective-permute-start.13 = (bf16[512,256]{1,0:T(8,128)(2,1)S(1)}, bf16[512,256]{1,0:T(8,128)(2,1)S(1)}, u32[]{:S(2)}, u32[]{:S(2)}) collective-permute-start(bf16[512,256]{1,0:T(8,128)(2,1)S(1)} %add_convert_fusion.1), channel_id=1, source_target_pairs={{0,2},{1,3},{2,0},{3,1},{4,6},{5,7},{6,4},{7,5},{8,10},{9,11},{10,... | collective-permute-start | bytes 786440 | tf_op jit(solution)/shard_map/ppermute | solution.py:377
  99.7 33.2 %collective-permute-start.18 = (bf16[512,768]{1,0:T(8,128)(2,1)S(1)}, bf16[512,768]{1,0:T(8,128)(2,1)}, u32[]{:S(2)}, u32[]{:S(2)}) collective-permute-start(bf16[512,768]{1,0:T(8,128)(2,1)S(1)} %multiply_convert_fusion.refs_1_), channel_id=1, source_target_pairs={{0,2},{1,3},{2,0},{3,1},{4,6},{5,7},{6,4},{7,5},{8,10},{9,11},{10,... | collective-permute-start | bytes 2359304 | tf_op jit(solution)/shard_map/ppermute | solution.py:377
  101.3 37.0 %collective-permute-start.15 = (bf16[512,768]{1,0:T(8,128)(2,1)S(1)}, bf16[512,768]{1,0:T(8,128)(2,1)}, u32[]{:S(2)}, u32[]{:S(2)}) collective-permute-start(bf16[512,768]{1,0:T(8,128)(2,1)S(1)} %multiply_convert_fusion.refs_1_), channel_id=1, source_target_pairs={{0,1},{1,0},{2,3},{3,2},{4,5},{5,4},{6,7},{7,6},{8,9},{9,8},{10,11... | collective-permute-start | bytes 2359304 | tf_op jit(solution)/shard_map/ppermute | solution.py:310
  111.5 21.5 %collective-permute-start.21 = (bf16[512,256]{1,0:T(8,128)(2,1)S(1)}, bf16[512,256]{1,0:T(8,128)(2,1)S(1)}, u32[]{:S(2)}, u32[]{:S(2)}) collective-permute-start(bf16[512,256]{1,0:T(8,128)(2,1)S(1)} %get-tuple-element.45.refs_2_), channel_id=1, source_target_pairs={{0,2},{1,3},{2,0},{3,1},{4,6},{5,7},{6,4},{7,5},{8,10},{9,11},{10,... | collective-permute-start | bytes 786440 | tf_op jit(solution)/shard_map/ppermute | solution.py:377
  113.0 20.7 %collective-permute-start.16 = (bf16[512,256]{1,0:T(8,128)(2,1)S(1)}, bf16[512,256]{1,0:T(8,128)(2,1)}, u32[]{:S(2)}, u32[]{:S(2)}) collective-permute-start(bf16[512,256]{1,0:T(8,128)(2,1)S(1)} %get-tuple-element.45.refs_2_), channel_id=1, source_target_pairs={{0,1},{1,0},{2,3},{3,2},{4,5},{5,4},{6,7},{7,6},{8,9},{9,8},{10,11... | collective-permute-start | bytes 786440 | tf_op jit(solution)/shard_map/ppermute | solution.py:310
  113.0 25.3 %collective-permute-start.17 = (bf16[512,256]{1,0:T(8,128)(2,1)}, bf16[512,256]{1,0:T(8,128)(2,1)}, u32[]{:S(2)}, u32[]{:S(2)}) collective-permute-start(bf16[512,256]{1,0:T(8,128)(2,1)} %get-tuple-element.46.refs_0_), channel_id=1, source_target_pairs={{0,2},{1,3},{2,0},{3,1},{4,6},{5,7},{6,4},{7,5},{8,10},{9,11},{10,... | collective-permute-start | bytes 786440 | tf_op jit(solution)/shard_map/ppermute | solution.py:377
  133.0 5.3 %collective-permute-start.14 = (bf16[512,256]{1,0:T(8,128)(2,1)}, bf16[512,256]{1,0:T(8,128)(2,1)}, u32[]{:S(2)}, u32[]{:S(2)}) collective-permute-start(bf16[512,256]{1,0:T(8,128)(2,1)} %get-tuple-element.46.refs_0_), channel_id=1, source_target_pairs={{0,1},{1,0},{2,3},{3,2},{4,5},{5,4},{6,7},{7,6},{8,9},{9,8},{10,11... | collective-permute-start | bytes 786440 | tf_op jit(solution)/shard_map/ppermute | solution.py:310
  133.0 16.4 %collective-permute-start.20 = (bf16[512,768]{1,0:T(8,128)(2,1)}, bf16[512,768]{1,0:T(8,128)(2,1)}, u32[]{:S(2)}, u32[]{:S(2)}) collective-permute-start(bf16[512,768]{1,0:T(8,128)(2,1)} %collective-permute-done.18.refs_2_), channel_id=1, source_target_pairs={{0,1},{1,0},{2,3},{3,2},{4,5},{5,4},{6,7},{7,6},{8,9},{9,8},{10,11... | collective-permute-start | bytes 2359304 | tf_op jit(solution)/shard_map/ppermute | solution.py:310
  133.7 26.4 %collective-permute-start.22 = (bf16[512,256]{1,0:T(8,128)(2,1)S(1)}, bf16[512,256]{1,0:T(8,128)(2,1)S(1)}, u32[]{:S(2)}, u32[]{:S(2)}) collective-permute-start(bf16[512,256]{1,0:T(8,128)(2,1)S(1)} %collective-permute-done.21.refs_0_), channel_id=1, source_target_pairs={{0,1},{1,0},{2,3},{3,2},{4,5},{5,4},{6,7},{7,6},{8,9},{9,8},{10,11... | collective-permute-start | bytes 786440 | tf_op jit(solution)/shard_map/ppermute | solution.py:310
  138.3 11.0 %collective-permute-start.19 = (bf16[512,256]{1,0:T(8,128)(2,1)}, bf16[512,256]{1,0:T(8,128)(2,1)S(1)}, u32[]{:S(2)}, u32[]{:S(2)}) collective-permute-start(bf16[512,256]{1,0:T(8,128)(2,1)} %collective-permute-done.17.refs_1_), channel_id=1, source_target_pairs={{0,1},{1,0},{2,3},{3,2},{4,5},{5,4},{6,7},{7,6},{8,9},{9,8},{10,11... | collective-permute-start | bytes 786440 | tf_op jit(solution)/shard_map/ppermute | solution.py:310
  166.0 8.7 %collective-permute-start.23 = (bf16[8,128,128]{2,1,0:T(8,128)(2,1)S(1)}, bf16[8,128,128]{2,1,0:T(8,128)(2,1)S(1)}, u32[]{:S(2)}, u32[]{:S(2)}) collective-permute-start(bf16[8,128,128]{2,1,0:T(8,128)(2,1)S(1)} %get-tuple-element.36), channel_id=1, source_target_pairs={{0,4},{4,0},{8,12},{12,8},{16,20},{20,16},{24,28},{28,24},{1,5},{5... | collective-permute-start | bytes 786440 | tf_op jit(solution)/shard_map/ppermute | solution.py:310
  174.8 23.7 %copy-start.18 = (bf16[8,128,128]{2,1,0:T(8,128)(2,1)S(1)}, bf16[8,128,128]{2,1,0:T(8,128)(2,1)}, u32[]{:S(2)}) copy-start(bf16[8,128,128]{2,1,0:T(8,128)(2,1)} %copy-done.17) | copy-start | bytes 786436
  174.8 8.0 %collective-permute-start.24 = (bf16[8,128,128]{2,1,0:T(8,128)(2,1)S(1)}, bf16[8,128,128]{2,1,0:T(8,128)(2,1)S(1)}, u32[]{:S(2)}, u32[]{:S(2)}) collective-permute-start(bf16[8,128,128]{2,1,0:T(8,128)(2,1)S(1)} %fusion.13), channel_id=1, source_target_pairs={{0,8},{4,12},{8,0},{12,4},{16,24},{20,28},{24,16},{28,20},{1,9},{5... | collective-permute-start | bytes 786440 | tf_op jit(solution)/shard_map/ppermute | solution.py:310
  183.6 14.1 %collective-permute-start.25 = (bf16[8,128,128]{2,1,0:T(8,128)(2,1)}, bf16[8,128,128]{2,1,0:T(8,128)(2,1)S(1)}, u32[]{:S(2)}, u32[]{:S(2)}) collective-permute-start(bf16[8,128,128]{2,1,0:T(8,128)(2,1)} %fusion.11), channel_id=1, source_target_pairs={{0,16},{4,20},{8,24},{12,28},{16,0},{20,4},{24,8},{28,12},{1,17},{... | collective-permute-start | bytes 786440 | tf_op jit(solution)/shard_map/ppermute | solution.py:310
  186.6 11.9 %copy-start.20 = (bf16[512,1024]{1,0:T(8,128)(2,1)S(1)}, bf16[512,1024]{1,0:T(8,128)(2,1)}, u32[]{:S(2)}) copy-start(bf16[512,1024]{1,0:T(8,128)(2,1)} %copy-done.19) | copy-start | bytes 3145732
  197.9 25.0 %collective-permute-start.26 = (bf16[8,128,128]{2,1,0:T(8,128)(2,1)S(1)}, bf16[8,128,128]{2,1,0:T(8,128)(2,1)S(1)}, u32[]{:S(2)}, u32[]{:S(2)}) collective-permute-start(bf16[8,128,128]{2,1,0:T(8,128)(2,1)S(1)} %get-tuple-element.48), channel_id=1, source_target_pairs={{0,4},{4,0},{8,12},{12,8},{16,20},{20,16},{24,28},{28,24},{1,5},{5... | collective-permute-start | bytes 786440 | tf_op jit(solution)/shard_map/ppermute | solution.py:310
  198.5 1.6 copy-start.5
  200.1 1.6 copy-start.10
  201.7 8.0 %copy-start.6 = (bf16[512,2048]{1,0:T(8,128)(2,1)S(1)}, bf16[512,2048]{1,0:T(8,128)(2,1)}, u32[]{:S(2)}) copy-start(bf16[512,2048]{1,0:T(8,128)(2,1)} %k.15) | copy-start | bytes 6291460
  201.7 8.0 %copy-start.14 = (bf16[8,128,128]{2,1,0:T(8,128)(2,1)S(1)}, bf16[8,128,128]{2,1,0:T(8,128)(2,1)}, u32[]{:S(2)}) copy-start(bf16[8,128,128]{2,1,0:T(8,128)(2,1)} %copy-done.13) | copy-start | bytes 786436
  201.7 8.0 %copy-start.16 = (bf16[512,1024]{1,0:T(8,128)(2,1)S(1)}, bf16[512,1024]{1,0:T(8,128)(2,1)}, u32[]{:S(2)}) copy-start(bf16[512,1024]{1,0:T(8,128)(2,1)} %copy-done.15) | copy-start | bytes 3145732
  (2 other events, 2.0 us)

commit v2 on v1

v2 whole, which is shorter than its diff:
```python
import functools
import math

import jax
import jax.numpy as jnp
from jax import lax
from jax.experimental import pallas as pl
from jax.experimental.pallas import tpu as pltpu
from jax.sharding import PartitionSpec as P

DH = 128
GROUP = 4
HINT = 1000000000000
NT = (((1,), (1,)), ((), ()))
TN = (((0,), (0,)), ((), ()))
F32 = jnp.float32
BF16 = jnp.bfloat16


def dot(a, b, dims=(((1,), (0,)), ((), ()))):
    return lax.dot_general(a, b, dims, preferred_element_type=F32)


def call(body, grid, in_specs, out_specs, out_shape, flops, moved, aliases=None, after=(), vmem=40, scratch=(), token=False):
    count = len(in_specs)
    if token:
        out_specs = [*out_specs, pl.BlockSpec((8, 128), lambda *_: (0, 0))]
        out_shape = [*out_shape, sds((8, 128), F32)]

    def ordered(idx, *refs):
        refs = list(refs)
        if token:
            refs.pop(count + len(after) + len(out_shape) - 1)[...] = jnp.zeros((8, 128), F32)
        body(idx, *refs[:count], *refs[count + len(after) :])

    kernel = pl.pallas_call(
        ordered,
        grid_spec=pltpu.PrefetchScalarGridSpec(
            num_scalar_prefetch=1,
            grid=grid,
            in_specs=list(in_specs) + [pl.BlockSpec(memory_space=pl.ANY)] * len(after),
            out_specs=out_specs,
            scratch_shapes=list(scratch),
        ),
        out_shape=out_shape,
        input_output_aliases=aliases or {},
        compiler_params=pltpu.CompilerParams(vmem_limit_bytes=vmem * 1024 * 1024),
        cost_estimate=pl.CostEstimate(
            flops=max(1, flops // HINT), bytes_accessed=max(1, moved // HINT), transcendentals=0
        ),
    )
    return lambda *args: kernel(*args, *after)


def sds(shape, dtype):
    return jax.ShapeDtypeStruct(shape, dtype)


def lower_mask(n):
    rows = lax.broadcasted_iota(jnp.int32, (n, n), 0)
    cols = lax.broadcasted_iota(jnp.int32, (n, n), 1)
    return rows >= cols


def cut(i):
    return slice(i * DH, (i + 1) * DH)


def group_of(half_heads):
    return math.gcd(half_heads, GROUP)


def kv_body(group, idx, k, v, out):
    for i in range(group):
        out[i] = dot(k[:, cut(i)], v[:, cut(i)], TN).astype(BF16)


def kv_states(half, k, v, half_heads, after=()):
    rows = k.shape[0]
    group = group_of(half_heads)
    steps = half_heads // group
    blk = pl.BlockSpec((rows, group * DH), lambda i, s: (0, s[0] * steps + i))
    return call(
        functools.partial(kv_body, group),
        (steps,),
        [blk, blk],
        pl.BlockSpec((group, DH, DH), lambda i, s: (i, 0, 0)),
        sds((half_heads, DH, DH), BF16),
        2 * rows * DH * DH * half_heads,
        rows * DH * half_heads * 4,
        after=after,
        vmem=58,
    )(half, k, v)


def intra_body(group, block, idx, q, k, v, out):
    mask = lower_mask(block)
    n = q.shape[0] // block
    for i in range(group):
        c = cut(i)
        state = None
        for b in range(n):
            r = slice(b * block, (b + 1) * block)
            qb, kb, vb = q[r, c], k[r, c], v[r, c]
            s = jnp.where(mask, dot(qb, kb, NT), 0.0).astype(BF16)
            o = dot(s, vb)
            if state is not None:
                o = o + dot(qb, state.astype(BF16))
            if b < n - 1:
                kv = dot(kb, vb, TN)
                state = kv if state is None else state + kv
            out[r, c] = o


def intra(half, q, k, v, half_heads, after):
    rows = k.shape[0]
    block = math.gcd(rows, 256)
    group = group_of(half_heads)
    steps = half_heads // group
    blk = pl.BlockSpec((rows, group * DH), lambda i, s: (0, s[0] * steps + i))
    return call(
        functools.partial(intra_body, group, block),
        (steps,),
        [blk, blk, blk],
        pl.BlockSpec((rows, group * DH), lambda i, s: (0, i)),
        sds((rows, half_heads * DH), F32),
        4 * rows * (block + DH) * DH * half_heads,
        rows * DH * half_heads * 10,
        after=after,
        vmem=58,
    )(half, q, k, v)


def attn_body(group, scale, idx, q, part, state, out):
    for i in range(group):
        c = cut(i)
        out[:, c] = (scale * (part[:, c] + dot(q[:, c], state[i]))).astype(BF16)


def attend(half, scale, q, part, state, half_heads):
    rows = q.shape[0]
    group = group_of(half_heads)
    steps = half_heads // group
    blk = pl.BlockSpec((rows, group * DH), lambda i, s: (0, i))
    return call(
        functools.partial(attn_body, group, scale),
        (steps,),
        [
            pl.BlockSpec((rows, group * DH), lambda i, s: (0, s[0] * steps + i)),
            blk,
            pl.BlockSpec((group, DH, DH), lambda i, s: (i, 0, 0)),
        ],
        blk,
        sds((rows, half_heads * DH), BF16),
        2 * rows * DH * DH * half_heads,
        rows * DH * half_heads * 8,
    )(half, q, part, state)


def project_body(idx, a0, b0, a1, b1, w, wo, out, acc):
    i = pl.program_id(0)

    @pl.when(i == 0)
    def _():
        acc[...] = dot(a0[...], w[...]) + dot(b0[...], wo[...])

    @pl.when(i == 1)
    def _():
        out[...] = (acc[...] + dot(a1[...], w[...]) + dot(b1[...], wo[...])).astype(BF16)


def project(idx, mine, theirs, weight, other_weight, span, after=()):
    rows, depth = mine[0].shape
    whole = pl.BlockSpec((rows, depth), lambda i, s: (0, 0))
    return call(
        project_body,
        (2,),
        [
            whole,
            whole,
            whole,
            whole,
            pl.BlockSpec(
                (pl.Element(depth), pl.Element(span)), lambda i, s: (s[i] * depth, s[2] * 128)
            ),
            pl.BlockSpec(
                (pl.Element(depth), pl.Element(span)), lambda i, s: (s[i] * depth, s[2] * 128)
            ),
        ],
        pl.BlockSpec((rows, span), lambda i, s: (0, 0)),
        sds((rows, span), BF16),
        8 * rows * depth * span,
        8 * depth * span + 8 * rows * depth + 2 * rows * span,
        after=after,
        vmem=44,
        scratch=[pltpu.VMEM((rows, span), F32)],
    )(idx, *mine, *theirs, weight, other_weight)


def grad_body(groups, with_acc, spans, idx, *refs):
    refs = list(refs)
    acc = refs.pop(0)[...] if with_acc else None
    out = refs.pop()
    for _ in range(groups):
        pieces = [refs.pop(0) for _ in spans]
        w = refs.pop(0)
        for piece, (lo, hi) in zip(pieces, spans):
            t = dot(piece[...], w[:, lo:hi], NT)
            acc = t if acc is None else acc + t
    out[...] = acc


def grad_accumulate(idx, groups, acc, spans, weight, width, after=()):
    depth = weight.shape[0]
    rows = groups[0][0].shape[0]
    row_tile = math.gcd(depth, 512)
    in_specs, args = [], []
    if acc is not None:
        in_specs.append(pl.BlockSpec((rows, row_tile), lambda i, s: (0, i)))
        args.append(acc)
    total = 0
    for g, pieces in enumerate(groups):
        for piece in pieces:
            in_specs.append(pl.BlockSpec(piece.shape, lambda i, s: (0, 0)))
            args.append(piece)
            total += piece.shape[1]
        in_specs.append(pl.BlockSpec((row_tile, width), lambda i, s, g=g: (i, s[g])))
        args.append(weight)
    return call(
        functools.partial(grad_body, len(groups), acc is not None, spans),
        (depth // row_tile,),
        in_specs,
        [pl.BlockSpec((rows, row_tile), lambda i, s: (0, i))],
        [sds((rows, depth), F32)],
        2 * rows * depth * total,
        2 * depth * total + 8 * rows * depth,
        {1: 0} if acc is not None else None,
        after=after,
        vmem=58,
        token=True,
    )(idx, *args)


def last_body(group, counts, idx, acc, q, *refs):
    *refs, g_out, r_out = refs
    t = acc[...]
    for count in counts:
        w, lo = refs[count], 0
        for piece in refs[:count]:
            hi = lo + piece.shape[1]
            t = t + dot(piece[...], w[:, lo:hi], NT)
            lo = hi
        refs = refs[count + 1 :]
    g = t.astype(BF16)
    g_out[...] = g
    for i in range(group):
        r_out[i] = dot(q[:, cut(i)], g[:, cut(i)], TN).astype(BF16)


def grad_last(idx, acc, q, groups, weight, half_heads, after=()):
    rows = acc.shape[0]
    group = group_of(half_heads)
    steps = half_heads // group
    wide = group * DH
    mine = pl.BlockSpec((rows, wide), lambda i, s: (0, s[0] * steps + i))
    in_specs, args, total = [mine, mine], [acc, q], 0
    for n, pieces in enumerate(groups):
        span = sum(piece.shape[1] for piece in pieces)
        total += span
        in_specs += [pl.BlockSpec(piece.shape, lambda i, s: (0, 0)) for piece in pieces]
        in_specs.append(
            pl.BlockSpec(
                (pl.Element(wide), pl.Element(span)),
                lambda i, s, n=n: ((s[0] * steps + i) * wide, s[1 + n] * 128),
            )
        )
        args += pieces + [weight]
    return call(
        functools.partial(last_body, group, [len(pieces) for pieces in groups]),
        (steps,),
        in_specs,
        [
            pl.BlockSpec((rows, wide), lambda i, s: (0, i)),
            pl.BlockSpec((group, DH, DH), lambda i, s: (i, 0, 0)),
        ],
        [sds((rows, half_heads * DH), BF16), sds((half_heads, DH, DH), BF16)],
        2 * rows * half_heads * DH * (total + DH),
        half_heads * DH * (rows * 8 + 2 * total),
        after=after,
        vmem=58,
    )(idx, *args)


def back_body(group, block, scale, extra, idx, q, k, v, g, state, *refs):
    dq, dk, dv = refs[extra:]
    mask = lower_mask(block)
    n = q.shape[0] // block
    for i in range(group):
        c = cut(i)
        before = state[i].astype(F32)
        later = None
        dks, dvs = [], []
        for b in range(n):
            r = slice(b * block, (b + 1) * block)
            qb, kb, vb, gb = q[r, c], k[r, c], v[r, c], g[r, c]
            gs = jnp.where(mask, dot(gb, vb, NT), 0.0).astype(BF16)
            s = jnp.where(mask, dot(qb, kb, NT), 0.0).astype(BF16)
            dq[r, c] = scale * (dot(gs, kb) + dot(gb, before.astype(BF16), NT))
            dks.append(dot(gs, qb, TN))
            dvs.append(dot(s, gb, TN))
            if b < n - 1:
                before = before + dot(kb, vb, TN)
        for b in reversed(range(n)):
            r = slice(b * block, (b + 1) * block)
            qb, kb, vb, gb = q[r, c], k[r, c], v[r, c], g[r, c]
            dkb, dvb = dks[b], dvs[b]
            if later is not None:
                lb = later.astype(BF16)
                dkb = dkb + dot(vb, lb, NT)
                dvb = dvb + dot(kb, lb)
            dk[r, c] = dkb
            dv[r, c] = dvb
            if b > 0:
                qg = dot(qb, gb, TN)
                later = qg if later is None else later + qg


def back_local(idx, cuts, scale, q, k, v, g, state, filled, half_heads, after):
    rows, width = q.shape
    block = math.gcd(rows, 256)
    heads = half_heads // cuts
    group = math.gcd(heads, 2)
    steps = heads // group
    wide = group * DH
    mine = pl.BlockSpec((rows, wide), lambda i, s: (0, (s[0] * cuts + s[1]) * steps + i))
    own = pl.BlockSpec((rows, wide), lambda i, s: (0, s[1] * steps + i))
    extra = len(filled)
    half = sds((rows, half_heads * DH), F32)
    return call(
        functools.partial(back_body, group, block, scale, extra),
        (steps,),
        [
            mine,
            mine,
            mine,
            own,
            pl.BlockSpec((group, DH, DH), lambda i, s: (s[1] * steps + i, 0, 0)),
        ]
        + [pl.BlockSpec(memory_space=pl.ANY)] * extra,
        [mine, own, own],
        [sds((rows, width), F32), half, half],
        2 * rows * DH * (5 * block + 4 * DH) * heads,
        rows * DH * heads * 20,
        {6 + n: n for n in range(extra)},
        after=after,
        vmem=58,
        token=True,
    )(idx, q, k, v, g, state, *filled)


def later_body(heads, scale, extra, idx, k, v, later, dk_in, dv_in, *refs):
    dk, dv = refs[extra:]
    for i in range(heads):
        c = cut(i)
        dk[:, c] = scale * (dk_in[:, c] + dot(v[:, c], later[i], NT))
        dv[:, c] = scale * (dv_in[:, c] + dot(k[:, c], later[i]))


def add_later(half, scale, k, v, later, dk, dv, filled, half_heads, after):
    rows, width = k.shape
    block = math.gcd(rows, 128)
    wide = half_heads * DH
    mine = pl.BlockSpec((block, wide), lambda i, s: (i, s[0]))
    own = pl.BlockSpec((block, wide), lambda i, s: (i, 0))
    extra = len(filled)
    return call(
        functools.partial(later_body, half_heads, scale, extra),
        (rows // block,),
        [mine, mine, pl.BlockSpec((half_heads, DH, DH), lambda i, s: (0, 0, 0)), own, own]
        + [pl.BlockSpec(memory_space=pl.ANY)] * extra,
        [mine, mine],
        [sds((rows, width), F32)] * 2,
        4 * rows * DH * DH * half_heads,
        rows * DH * half_heads * 20,
        {6 + n: n for n in range(extra)},
        after=after,
        vmem=58,
    )(half, k, v, later, dk, dv, *filled)


def tie(array, *others):
    return lax.optimization_barrier((array,) + others)


def swap(array, axis, bit):
    size = lax.axis_size(axis)
    return lax.ppermute(array, axis, [(i, i ^ (1 << bit)) for i in range(size)])


def scan_states(theirs, mine, ctx_bits, flipped, fill):
    pos = lax.axis_index("ctx")
    if flipped:
        pos = lax.axis_size("ctx") - 1 - pos

    held = []

    def beside(step, sent, got):
        done = fill[step]([sent, *held]) if step in fill else held
        got, *held[:] = tie(got, *done)
        return got.astype(F32)

    got = beside(0, theirs, swap(theirs, "ctx", 0))
    own = mine.astype(F32)
    total = own + got
    prefix = jnp.zeros_like(total)
    for bit in range(1, ctx_bits):
        sent = total.astype(BF16)
        other = beside(bit, sent, swap(sent, "ctx", bit))
        prefix = prefix + jnp.where((pos >> bit) & 1 == 1, other, 0.0)
        total = total + other
    upper = pos & 1 == 1
    mine_prefix = (prefix + jnp.where(upper, got, 0.0)).astype(BF16)
    sent = (prefix + jnp.where(upper, 0.0, own)).astype(BF16)
    return mine_prefix, swap(sent, "ctx", 0), held


def cuts_of(tiles, sizes):
    ends, at = [], 0
    for size in sizes:
        at = min(at + size, tiles)
        ends.append(at)
    ends[-1] = tiles
    starts = [0] + ends[:-1]
    return [(lo, hi) for lo, hi in zip(starts, ends) if lo < hi]


def on_device(queries, keys, values, teacher, out_weight, valid):
    rows, width = queries.shape
    heads = width // DH
    half_heads = heads // 2
    ctx_size = lax.axis_size("ctx")
    ctx_bits = ctx_size.bit_length() - 1
    chips = lax.axis_size("head") // 2
    ctx_id, head_id = lax.axis_index("ctx"), lax.axis_index("head")
    chip, core = head_id // 2, head_id % 2
    scale = 1.0 / math.sqrt(DH * rows * ctx_size)
    piece_width = teacher.shape[1]
    tile = 256 if piece_width % 256 == 0 else 128
    tiles = piece_width // tile
    sum_spans = [(lo * tile, hi * tile) for lo, hi in cuts_of(tiles, (2, 2, 1))]
    error_spans = [(lo * tile, hi * tile) for lo, hi in cuts_of(tiles, (2, 2, 1))]

    my_half = ctx_id & 1
    mine_ix = my_half[None].astype(jnp.int32)
    theirs_ix = 1 - mine_ix

    kv_theirs = kv_states(theirs_ix, keys, values, half_heads)
    kv_mine = kv_states(mine_ix, keys, values, half_heads, after=[kv_theirs])
    parts = {}

    def beside_forward(step):
        def run(after):
            if step == min(1, ctx_bits - 1):
                parts["mine"] = intra(mine_ix, queries, keys, values, half_heads, after)
                after = [parts["mine"]]
            if step == ctx_bits - 1:
                parts["theirs"] = intra(theirs_ix, queries, keys, values, half_heads, after)
                count, *after = tie(jnp.full((8, 128), jnp.sum(valid), jnp.int32), *after)
                token = parts["theirs"]
                for bit in range(ctx_bits - 1):
                    got, token = tie(swap(count, "ctx", bit), token)
                    count = count + got
                after = [token, count]
            return after if step else []

        return run

    before_mine, before_theirs, (*_, count) = scan_states(
        kv_theirs, kv_mine, ctx_bits, False, {n: beside_forward(n) for n in range(ctx_bits)}
    )
    count = count + swap(count, "ctx", ctx_bits - 1)
    before_theirs, count = tie(before_theirs, count)
    other_weight = swap(out_weight, "head", 0)

    def both_cores(array):
        return array, swap(array, "head", 0)

    attn_mine = both_cores(
        attend(mine_ix, scale, queries, parts["mine"], before_mine, half_heads)
    )
    attn_theirs = both_cores(
        attend(theirs_ix, scale, queries, parts["theirs"], before_theirs, half_heads)
    )

    def column(to_chip, to_core, lo):
        return ((to_chip * 2 + to_core) * piece_width + lo) // 128

    def terms(by, lo, hi, after=()):
        start = column(lax.rem(chip + by, chips), core, lo)
        idx = jnp.stack([my_half, 1 - my_half, start]).astype(jnp.int32)
        return project(idx, attn_mine, attn_theirs, out_weight, other_weight, hi - lo, after)

    def shift(array, by):
        size = 2 * chips
        return lax.ppermute(array, "head", [(i, (i + 2 * by) % size) for i in range(size)])

    arrived, own, after = [], [], []
    first = sum_spans[0][1]
    for n, (lo, hi) in enumerate(sum_spans):
        got = []
        if n == 2:
            own.append(terms(0, 0, first, after))
            after = [own[0], *arrived[0]]
        for by in range(1, chips):
            summed = terms(by, lo, hi, after)
            after = [summed]
            got.append(shift(summed, by))
        arrived.append(got)
    if own:
        own.append(terms(0, first, piece_width, after + arrived[1]))
    else:
        own.append(terms(0, 0, piece_width, after))
    own_spans = [(0, first), (first, piece_width)] if len(own) > 1 else [(0, piece_width)]

    factor = rows * ctx_size / count[0, 0].astype(F32)
    weigh = (valid.astype(F32) * factor)[:, None]

    def columns(pieces, spans, lo, hi):
        inside = [
            piece[:, max(lo - base, 0) : hi - base].astype(F32)
            for (base, end), piece in zip(spans, pieces)
            if base < hi and lo < end
        ]
        return jnp.concatenate(inside, 1)

    def error_of(lo, hi):
        predicted = columns(own, own_spans, lo, hi)
        for by in range(1, chips):
            predicted = predicted + columns([got[by - 1] for got in arrived], sum_spans, lo, hi)
        return (weigh * (predicted - teacher[:, lo:hi].astype(F32))).astype(BF16)

    errors = [error_of(lo, hi) for lo, hi in error_spans]
    near = [errors, [swap(error, "head", 0) for error in errors]]
    idx = jnp.stack([chip * 2 + core, chip * 2 + 1 - core]).astype(jnp.int32)
    acc, summed_near = grad_accumulate(
        idx, near, None, error_spans, out_weight, piece_width
    )

    early = max(1, len(error_spans) - 2)
    gathered = [[shift(error, by) for by in range(1, chips)] for error in errors]

    def sources(select, token):
        groups, devices = [], []
        for by in range(1, chips):
            from_chip = lax.rem(chip + chips - by, chips)
            pieces = [got[by - 1] for got in gathered[select]]
            *late, token = tie(pieces[0], *pieces[1:], token)
            groups += [pieces, [swap(piece, "head", 0) for piece in late]]
            devices += [(from_chip, core), (from_chip, 1 - core)]
        return groups, devices, token

    last, last_ix, token = [], [], summed_near
    if chips > 1:
        far, devices, token = sources(slice(0, early), summed_near)
        far_ix = jnp.stack([to_chip * 2 + to_core for to_chip, to_core in devices])
        acc, summed_far = grad_accumulate(
            far_ix.astype(jnp.int32), far, acc, error_spans[:early], out_weight, piece_width,
            [token],
        )
        last, devices, token = sources(slice(early, None), summed_far)
        last_ix = [column(*device, error_spans[early][0]) for device in devices]

    def last_of(ix, after=()):
        index = jnp.stack([ix[0]] + last_ix).astype(jnp.int32)
        return grad_last(index, acc, queries, last, out_weight, half_heads, after)

    g_theirs, r_theirs = last_of(theirs_ix, [token])
    g_mine, r_mine = last_of(mine_ix, [r_theirs])
    cuts = 1
    done_q, done_kv = [], {"theirs": [], "mine": []}
    halves = {
        "theirs": (theirs_ix[0], g_theirs, before_theirs),
        "mine": (mine_ix[0], g_mine, before_mine),
    }

    def back(name, part, after):
        half, g, before = halves[name]
        *got, token = back_local(
            jnp.stack([half, jnp.int32(part)]), cuts, scale, queries, keys, values, g, before,
            done_q + done_kv[name], half_heads, after,
        )
        done_q[:], done_kv[name] = got[:1], got[1:]
        return [token]

    order = [(name, part) for name in ("mine", "theirs") for part in range(cuts)]
    plan = {}
    for n, step in enumerate((1, 2)):
        if n < len(order):
            plan.setdefault(min(step, ctx_bits - 1), []).append(order[n])

    def beside_backward(step):
        def run(after):
            if step == 0:
                return [r_mine]
            for name, part in plan.get(step, []):
                after = back(name, part, after)
            return after

        return run

    later_mine, later_theirs, token = scan_states(
        r_theirs, r_mine, ctx_bits, True, {n: beside_backward(n) for n in range(ctx_bits)}
    )
    (q_grad,) = done_q
    grads = add_later(
        mine_ix, scale, keys, values, later_mine, *done_kv["mine"], [], half_heads, token
    )
    k_grad, v_grad = add_later(
        theirs_ix, scale, keys, values, later_theirs, *done_kv["theirs"], list(grads), half_heads, []
    )
    return q_grad, k_grad, v_grad


def solution(mesh):
    in_specs = (
        P("ctx", "head"),
        P("ctx", "head"),
        P("ctx", "head"),
        P("ctx", "head"),
        P("head", None),
        P("ctx"),
    )
    out_specs = (P("ctx", "head"), P("ctx", "head"), P("ctx", "head"))
    return jax.shard_map(
        on_device, mesh=mesh, in_specs=in_specs, out_specs=out_specs, check_vma=False
    )
```

time: 229 us -> 187 us (0.82)
  waiting for transfers between devices: 72.9 us -> 32.8 us
  local copies, waits for them, and re-layouts: 17.4 us -> 6.91 us
  Pallas kernels: 102 us -> 109 us
  other arithmetic: 5.62 us -> 8.42 us
    ppermute x6, waiting for transfers between devices: 40.8 us -> 13.6 us  [shift(): lax.ppermute(array, 'head', [(i, (i + 2 * by) % size) for i in range(size)])]
    ppermute x21 -> x20, waiting for transfers between devices: 32.1 us -> 19.2 us  [swap(): return lax.ppermute(array, axis, [(i, i ^ 1 << bit) for i in range(size)])]
    unnamed x46 -> x52, local copies, waits for them, and re-layouts: 16.3 us -> 5.75 us
    pallas_call x22 -> x19, Pallas kernels: 102 us -> 109 us  [call(): return lambda *args: kernel(*args, *after)]
    another operation x4 -> x7, other arithmetic: 0.3 us -> 3.17 us  [the longest x2 1.21 us: back(): jnp.stack([half, jnp.int32(part)])]
    ppermute x21 -> x20, starting transfers between devices: 20.7 us -> 21.3 us  [swap(): return lax.ppermute(array, axis, [(i, i ^ 1 << bit) for i in range(size)])]
  transfers between devices with their start and end apart: 27 -> 26, of which waited for: 12 -> 13; matrix products, arithmetic and copies ran while one was open for 2% -> 4% of each run, Pallas kernels for 40% -> 49%
where the time goes in v2:
time: 187 us; the launch traced here: 186 us
  Pallas kernels  109 us (58%)
  waiting for transfers between devices  32.8 us (18%)
  starting transfers between devices  27.6 us (15%)
  other arithmetic  8.42 us (5%)
  local copies, waits for them, and re-layouts  6.91 us (4%)
    pallas_call x19, Pallas kernels, call(): return lambda *args: kernel(*args, *after)  109 us
    ppermute x20, starting transfers between devices, swap(): return lax.ppermute(array, axis, [(i, i ^ 1 << bit) for i in range(size)])  21.3 us
    ppermute x20, waiting for transfers between devices, swap(): return lax.ppermute(array, axis, [(i, i ^ 1 << bit) for i in range(size)])  19.2 us
    ppermute x6, waiting for transfers between devices, shift(): lax.ppermute(array, 'head', [(i, (i + 2 * by) % size) for i in range(size)])  13.6 us
    ppermute x6, starting transfers between devices, shift(): lax.ppermute(array, 'head', [(i, (i + 2 * by) % size) for i in range(size)])  6.33 us
    unnamed x52, local copies, waits for them, and re-layouts  5.75 us
  transfers between devices with their start and end apart: 26, of which 13 were waited for; matrix products, arithmetic and copies ran while one was open for 4% of the time, Pallas kernels for 49%

profile of v2, /device:TPU:0, one launch (start us, length us, event | category | flops | bytes accessed | tf_op | source)
XLA Modules:
  0.0 186.3 jit_solution(6812375447241050903)
XLA Ops:
  1.1 2.6 %shard_map.85.refs_2_ = bf16[8,128,128]{2,1,0:T(8,128)(2,1)} custom-call(s32[1]{0:T(128)S(6)} %sub.56.idx, bf16[512,2048]{1,0:T(8,128)(2,1)} %refs_0_.19, bf16[512,2048]{1,0:T(8,128)(2,1)} %refs_1_.19), custom_call_target="tpu_custom_call" | custom-call | flops 1 | bytes 1 | tf_op jit(solution)/shard_map/pallas_call | solution.py:52
  3.7 2.6 %collective-permute-start = (bf16[8,128,128]{2,1,0:T(8,128)(2,1)}, bf16[8,128,128]{2,1,0:T(8,128)(2,1)S(1)}, u32[]{:S(2)}, u32[]{:S(2)}) collective-permute-start(bf16[8,128,128]{2,1,0:T(8,128)(2,1)} %shard_map.85.refs_2_), channel_id=1, source_target_pairs={{0,4},{4,0},{8,12},{12,8},{16,20},{20,16},{24,28},{28,24},{1,5},{5... | collective-permute-start | bytes 786440 | tf_op jit(solution)/shard_map/ppermute | solution.py:397
  6.3 2.6 %shard_map.86 = bf16[8,128,128]{2,1,0:T(8,128)(2,1)} custom-call(s32[1]{0:T(128)} %bitcast.idx, bf16[512,2048]{1,0:T(8,128)(2,1)} %refs_0_.19, bf16[512,2048]{1,0:T(8,128)(2,1)} %refs_1_.19, bf16[8,128,128]{2,1,0:T(8,128)(2,1)} %shard_map.85.refs_2_), custom_call_target="tpu_custom_call" | custom-call | flops 1 | bytes 1 | tf_op jit(solution)/shard_map/pallas_call | solution.py:52
  8.9 4.6 %collective-permute-done = bf16[8,128,128]{2,1,0:T(8,128)(2,1)S(1)} collective-permute-done((bf16[8,128,128]{2,1,0:T(8,128)(2,1)}, bf16[8,128,128]{2,1,0:T(8,128)(2,1)S(1)}, u32[]{:S(2)}, u32[]{:S(2)}) %collective-permute-start) | collective-permute-done | bytes 262176 | tf_op jit(solution)/shard_map/ppermute | solution.py:397
  13.4 1.0 fusion.12.refs_3_
  14.5 1.9 collective-permute-start.1
  16.4 4.6 %shard_map.87.refs_4_.refs_1_ = f32[512,1024]{1,0:T(8,128)} custom-call(s32[1]{0:T(128)} %bitcast.idx, bf16[512,2048]{1,0:T(8,128)(2,1)} %refs_0_.17, bf16[512,2048]{1,0:T(8,128)(2,1)} %refs_0_.19, bf16[512,2048]{1,0:T(8,128)(2,1)} %refs_1_.19, bf16[8,128,128]{2,1,0:T(8,128)(2,1)} %copy-done.16), custom_call_target="tpu_custom_call" | custom-call | flops 1 | bytes 1 | tf_op jit(solution)/shard_map/pallas_call | solution.py:52
  20.9 1.7 collective-permute-done.1
  22.8 2.7 %collective-permute-start.2 = (bf16[8,128,128]{2,1,0:T(8,128)(2,1)S(1)}, bf16[8,128,128]{2,1,0:T(8,128)(2,1)S(1)}, u32[]{:S(2)}, u32[]{:S(2)}) collective-permute-start(bf16[8,128,128]{2,1,0:T(8,128)(2,1)S(1)} %fusion.5.refs_3_), channel_id=1, source_target_pairs={{0,16},{4,20},{8,24},{12,28},{16,0},{20,4},{24,8},{28,12},{1,17},{... | collective-permute-start | bytes 786440 | tf_op jit(solution)/shard_map/ppermute | solution.py:397
  26.7 1.6 collective-permute-start.3
  28.3 4.7 %shard_map.88.refs_1_ = f32[512,1024]{1,0:T(8,128)} custom-call(s32[1]{0:T(128)S(6)} %sub.56.idx, bf16[512,2048]{1,0:T(8,128)(2,1)} %refs_0_.17, bf16[512,2048]{1,0:T(8,128)(2,1)} %refs_0_.19, bf16[512,2048]{1,0:T(8,128)(2,1)} %refs_1_.19, bf16[8,128,128]{2,1,0:T(8,128)(2,1)} %copy-done.17, f32[512,1024]{1,0:T(8,128)} %shard_map.87.refs_4_.refs_1_), custom_call_target="tpu_custom_call" | custom-call | flops 1 | bytes 1 | tf_op jit(solution)/shard_map/pallas_call | solution.py:52
  33.1 1.6 collective-permute-start.4
  34.7 2.0 %collective-permute-done.4 = s32[8,128]{1,0:T(8,128)S(1)} collective-permute-done((s32[8,128]{1,0:T(8,128)S(1)}, s32[8,128]{1,0:T(8,128)S(1)}, u32[]{:S(2)}, u32[]{:S(2)}) %collective-permute-start.4) | collective-permute-done | bytes 4128 | tf_op jit(solution)/shard_map/ppermute | solution.py:397
  37.0 1.3 collective-permute-start.5
  38.3 1.6 copy-done.1
  40.9 1.9 %collective-permute-done.6 = s32[8,128]{1,0:T(8,128)S(1)} collective-permute-done((s32[8,128]{1,0:T(8,128)S(1)}, s32[8,128]{1,0:T(8,128)S(1)}, u32[]{:S(2)}, u32[]{:S(2)}) %collective-permute-start.6) | collective-permute-done | bytes 4128 | tf_op jit(solution)/shard_map/ppermute | solution.py:397
  42.8 1.5 collective-permute-done.5.refs_2_.refs_4_
  44.3 1.6 shard_map.90.refs_2_
  46.1 2.7 %collective-permute-done.8.refs_3_ = bf16[512,1024]{1,0:T(8,128)(2,1)S(1)} collective-permute-done((bf16[512,1024]{1,0:T(8,128)(2,1)}, bf16[512,1024]{1,0:T(8,128)(2,1)S(1)}, u32[]{:S(2)}, u32[]{:S(2)}) %collective-permute-start.8) | collective-permute-done | bytes 1048608 | tf_op jit(solution)/shard_map/ppermute | solution.py:397
  48.8 5.4 %shard_map.91.refs_6_ = bf16[512,512]{1,0:T(8,128)(2,1)S(1)} custom-call(s32[3]{0:T(128)S(1)} %get-tuple-element.90.idx, bf16[512,1024]{1,0:T(8,128)(2,1)S(1)} %shard_map.89.refs_0_, bf16[512,1024]{1,0:T(8,128)(2,1)} %collective-permute-done.7.refs_1_, bf16[512,1024]{1,0:T(8,128)(2,1)} %shard_map.90.refs_2_, ...), custom_call_target="tpu_custom_call" | custom-call | flops 1 | bytes 1 | tf_op jit(solution)/shard_map/pallas_call | solution.py:52
  54.2 1.1 collective-permute-start.10
  55.3 5.4 %shard_map.92.refs_6_ = bf16[512,512]{1,0:T(8,128)(2,1)S(1)} custom-call(s32[3]{0:T(128)S(1)} %get-tuple-element.91.idx, bf16[512,1024]{1,0:T(8,128)(2,1)S(1)} %shard_map.89.refs_0_, bf16[512,1024]{1,0:T(8,128)(2,1)} %collective-permute-done.7.refs_1_, bf16[512,1024]{1,0:T(8,128)(2,1)} %shard_map.90.refs_2_, ...), custom_call_target="tpu_custom_call" | custom-call | flops 1 | bytes 1 | tf_op jit(solution)/shard_map/pallas_call | solution.py:52
  60.7 1.0 collective-permute-start.11
  63.0 5.4 %shard_map.93.refs_6_ = bf16[512,512]{1,0:T(8,128)(2,1)S(1)} custom-call(s32[3]{0:T(128)S(1)} %get-tuple-element.92.idx, bf16[512,1024]{1,0:T(8,128)(2,1)S(1)} %shard_map.89.refs_0_, bf16[512,1024]{1,0:T(8,128)(2,1)} %collective-permute-done.7.refs_1_, bf16[512,1024]{1,0:T(8,128)(2,1)} %shard_map.90.refs_2_, ...), custom_call_target="tpu_custom_call" | custom-call | flops 1 | bytes 1 | tf_op jit(solution)/shard_map/pallas_call | solution.py:52
  69.0 4.0 %shard_map.94.refs_6_ = bf16[512,256]{1,0:T(8,128)(2,1)S(1)} custom-call(s32[3]{0:T(128)S(1)} %get-tuple-element.81.idx, bf16[512,1024]{1,0:T(8,128)(2,1)S(1)} %shard_map.89.refs_0_, bf16[512,1024]{1,0:T(8,128)(2,1)} %collective-permute-done.7.refs_1_, bf16[512,1024]{1,0:T(8,128)(2,1)} %shard_map.90.refs_2_, ...), custom_call_target="tpu_custom_call" | custom-call | flops 1 | bytes 1 | tf_op jit(solution)/shard_map/pallas_call | solution.py:52
  73.0 1.1 collective-permute-start.12
  74.1 6.1 %collective-permute-done.11.refs_7_ = bf16[512,512]{1,0:T(8,128)(2,1)S(1)} collective-permute-done((bf16[512,512]{1,0:T(8,128)(2,1)S(1)}, bf16[512,512]{1,0:T(8,128)(2,1)S(1)}, u32[]{:S(2)}, u32[]{:S(2)}) %collective-permute-start.11) | collective-permute-done | bytes 524320 | tf_op jit(solution)/shard_map/ppermute | solution.py:505
  80.3 7.0 %shard_map.95 = bf16[512,768]{1,0:T(8,128)(2,1)S(1)} custom-call(s32[3]{0:T(128)S(1)} %get-tuple-element.89.idx, bf16[512,1024]{1,0:T(8,128)(2,1)S(1)} %shard_map.89.refs_0_, bf16[512,1024]{1,0:T(8,128)(2,1)} %collective-permute-done.7.refs_1_, bf16[512,1024]{1,0:T(8,128)(2,1)} %shard_map.90.refs_2_, bf16[512,1024]{1,0:T(8,128)(2,1)S(1)} %collective-permute-done.8.refs_3_, ...), custom_call_target="tpu_custom_call" | custom-call | flops 1 | bytes 1 | tf_op jit(solution)/shard_map/pallas_call | solution.py:52
  88.3 1.0 collective-permute-start.16
  92.8 11.0 %shard_map.96 = (f32[512,2048]{1,0:T(8,128)}, f32[8,128]{1,0:T(8,128)}) custom-call(s32[2]{0:T(128)} %pad_add_fusion.3.idx, bf16[512,512]{1,0:T(8,128)(2,1)} %copy-done.10, bf16[512,512]{1,0:T(8,128)(2,1)} %copy-done.9, bf16[512,256]{1,0:T(8,128)(2,1)} %copy-done.14, bf16[2048,5120]{1,0:T(8,128)(2,1)} %refs_7_.5, bf16[512,512]{1,0:T(8,128)(2,1)} %copy-done.21, ...), custom_call_target="tpu_custom_call" | custom-call | flops 1 | bytes 1 | tf_op jit(solution)/shard_map/pallas_call | solution.py:52
  104.1 1.0 collective-permute-start.18
  105.1 1.0 collective-permute-start.19
  107.5 9.8 %shard_map.97 = (f32[512,2048]{1,0:T(8,128)}, f32[8,128]{1,0:T(8,128)}) custom-call(s32[2]{0:T(128)} %pad_add_fusion.2.idx, f32[512,2048]{1,0:T(8,128)} %get-tuple-element.50.refs_0_, bf16[512,512]{1,0:T(8,128)(2,1)} %copy-done.19, bf16[2048,5120]{1,0:T(8,128)(2,1)} %refs_7_.5, bf16[512,512]{1,0:T(8,128)(2,1)} %copy-done.22, ...), custom_call_target="tpu_custom_call", output_to_operand_aliasing={{0}: (1, {})} | custom-call | flops 1 | bytes 1 | tf_op jit(solution)/shard_map/pallas_call | solution.py:52
  117.4 6.7 %collective-permute-done.19.refs_3_ = bf16[512,256]{1,0:T(8,128)(2,1)S(1)} collective-permute-done((bf16[512,256]{1,0:T(8,128)(2,1)}, bf16[512,256]{1,0:T(8,128)(2,1)S(1)}, u32[]{:S(2)}, u32[]{:S(2)}) %collective-permute-start.19) | collective-permute-done | bytes 262176 | tf_op jit(solution)/shard_map/ppermute | solution.py:505
  125.3 1.2 collective-permute-done.21.refs_6_
  127.3 6.5 %shard_map.98 = (bf16[512,1024]{1,0:T(8,128)(2,1)}, bf16[8,128,128]{2,1,0:T(8,128)(2,1)}) custom-call(s32[3]{0:T(128)} %add_add_fusion.idx, f32[512,2048]{1,0:T(8,128)} %get-tuple-element.54.refs_0_, bf16[512,2048]{1,0:T(8,128)(2,1)} %refs_0_.17, bf16[512,512]{1,0:T(8,128)(2,1)} %copy-done.7, bf16[512,256]{1,0:T(8,128)(2,1)} %copy-done.12, ...), custom_call_target="tpu_custom_call" | custom-call | flops 1 | bytes 1 | tf_op jit(solution)/shard_map/pallas_call | solution.py:52
  133.8 1.5 collective-permute-start.22
  136.0 6.5 %shard_map.99 = (bf16[512,1024]{1,0:T(8,128)(2,1)}, bf16[8,128,128]{2,1,0:T(8,128)(2,1)}) custom-call(s32[3]{0:T(128)} %add_add_fusion.1.idx, f32[512,2048]{1,0:T(8,128)} %get-tuple-element.54.refs_0_, bf16[512,2048]{1,0:T(8,128)(2,1)} %refs_0_.17, bf16[512,512]{1,0:T(8,128)(2,1)} %copy-done.7, bf16[512,256]{1,0:T(8,128)(2,1)} %copy-done.12, ...), custom_call_target="tpu_custom_call" | custom-call | flops 1 | bytes 1 | tf_op jit(solution)/shard_map/pallas_call | solution.py:52
  142.4 1.0 fusion.13.refs_5_
  143.5 1.8 collective-permute-start.23
  145.9 9.7 %shard_map.100 = (f32[512,2048]{1,0:T(8,128)}, f32[512,1024]{1,0:T(8,128)}, f32[512,1024]{1,0:T(8,128)}, f32[8,128]{1,0:T(8,128)}) custom-call(s32[2]{0:T(128)} %pad_add_fusion.idx, bf16[512,2048]{1,0:T(8,128)(2,1)} %refs_0_.17, bf16[512,2048]{1,0:T(8,128)(2,1)} %refs_0_.19, bf16[512,2048]{1,0:T(8,128)(2,1)} %refs_1_.19, ...), custom_call_target="tpu_custom_call" | custom-call | flops 1 | bytes 1 | tf_op jit(solution)/shard_map/pallas_call | solution.py:52
  155.7 3.4 %collective-permute-start.24 = (bf16[8,128,128]{2,1,0:T(8,128)(2,1)S(1)}, bf16[8,128,128]{2,1,0:T(8,128)(2,1)S(1)}, u32[]{:S(2)}, u32[]{:S(2)}) collective-permute-start(bf16[8,128,128]{2,1,0:T(8,128)(2,1)S(1)} %fusion.10.refs_6_), channel_id=1, source_target_pairs={{0,16},{4,20},{8,24},{12,28},{16,0},{20,4},{24,8},{28,12},{1,17},{... | collective-permute-start | bytes 786440 | tf_op jit(solution)/shard_map/ppermute | solution.py:397
  159.8 9.6 %shard_map.101 = (f32[512,2048]{1,0:T(8,128)}, f32[512,1024]{1,0:T(8,128)}, f32[512,1024]{1,0:T(8,128)}, f32[8,128]{1,0:T(8,128)}) custom-call(s32[2]{0:T(128)} %pad_add_fusion.1.idx, bf16[512,2048]{1,0:T(8,128)(2,1)} %refs_0_.17, bf16[512,2048]{1,0:T(8,128)(2,1)} %refs_0_.19, bf16[512,2048]{1,0:T(8,128)(2,1)} %refs_1_.19, ...), custom_call_target="tpu_custom_call", output_to_operand_aliasing={{0}: (6, {})} | custom-call | flops 1 | bytes 1 | tf_op jit(solution)/shard_map/pallas_call | solution.py:52
  169.4 1.2 collective-permute-done.24
  170.6 0.9 fusion.9
  172.4 5.9 %shard_map.102 = (f32[512,2048]{1,0:T(8,128)}, f32[512,2048]{1,0:T(8,128)}) custom-call(s32[1]{0:T(128)} %bitcast.idx, bf16[512,2048]{1,0:T(8,128)(2,1)} %refs_0_.19, bf16[512,2048]{1,0:T(8,128)(2,1)} %refs_1_.19, bf16[8,128,128]{2,1,0:T(8,128)(2,1)} %get-tuple-element.85.refs_2_, f32[512,1024]{1,0:T(8,128)} %get-tuple-element.74.refs_3_, ...), custom_call_target="tpu_custom_call" | custom-call | flops 1 | bytes 1 | tf_op jit(solution)/shard_map/pallas_call | solution.py:52
  178.3 1.5 collective-permute-done.25.refs_2_
  180.5 5.9 %shard_map.103 = (f32[512,2048]{1,0:T(8,128)}, f32[512,2048]{1,0:T(8,128)}) custom-call(s32[1]{0:T(128)S(6)} %sub.56.idx, bf16[512,2048]{1,0:T(8,128)(2,1)} %refs_0_.19, bf16[512,2048]{1,0:T(8,128)(2,1)} %refs_1_.19, bf16[8,128,128]{2,1,0:T(8,128)(2,1)} %copy-done.24, ...), custom_call_target="tpu_custom_call", output_to_operand_aliasing={{0}: (6, {}), {1}: (7, {})} | custom-call | flops 1 | bytes 1 | tf_op jit(solution)/shard_map/pallas_call | solution.py:52
  (98 shorter events, 16.2 us)
Async XLA Ops:
  0.6 48.2 %collective-permute-start.9 = (bf16[2048,5120]{1,0:T(8,128)(2,1)}, bf16[2048,5120]{1,0:T(8,128)(2,1)}, u32[]{:S(2)}, u32[]{:S(2)}) collective-permute-start(bf16[2048,5120]{1,0:T(8,128)(2,1)} %refs_7_.5), channel_id=1, source_target_pairs={{0,1},{1,0},{2,3},{3,2},{4,5},{5,4},{6,7},{7,6},{8,9},{9,8},{10,11... | collective-permute-start | bytes 62914568 | tf_op jit(solution)/shard_map/ppermute | solution.py:397
  3.7 9.7 %collective-permute-start = (bf16[8,128,128]{2,1,0:T(8,128)(2,1)}, bf16[8,128,128]{2,1,0:T(8,128)(2,1)S(1)}, u32[]{:S(2)}, u32[]{:S(2)}) collective-permute-start(bf16[8,128,128]{2,1,0:T(8,128)(2,1)} %shard_map.85.refs_2_), channel_id=1, source_target_pairs={{0,4},{4,0},{8,12},{12,8},{16,20},{20,16},{24,28},{28,24},{1,5},{5... | collective-permute-start | bytes 786440 | tf_op jit(solution)/shard_map/ppermute | solution.py:397
  14.5 1.9 %copy-start.16 = (bf16[8,128,128]{2,1,0:T(8,128)(2,1)}, bf16[8,128,128]{2,1,0:T(8,128)(2,1)S(1)}, u32[]{:S(2)}) copy-start(bf16[8,128,128]{2,1,0:T(8,128)(2,1)S(1)} %fusion.12.refs_3_) | copy-start | bytes 786436
  14.5 8.2 %copy-start.6 = (bf16[8,128,128]{2,1,0:T(8,128)(2,1)S(1)}, bf16[8,128,128]{2,1,0:T(8,128)(2,1)}, u32[]{:S(2)}) copy-start(bf16[8,128,128]{2,1,0:T(8,128)(2,1)} %shard_map.86) | copy-start | bytes 786436
  14.5 11.0 %copy-start.25 = (s32[512]{0:T(512)S(1)}, s32[512]{0:T(512)}, u32[]{:S(2)}) copy-start(s32[512]{0:T(512)} %param.11) | copy-start | bytes 6148
  14.5 8.2 %collective-permute-start.1 = (bf16[8,128,128]{2,1,0:T(8,128)(2,1)S(1)}, bf16[8,128,128]{2,1,0:T(8,128)(2,1)S(1)}, u32[]{:S(2)}, u32[]{:S(2)}) collective-permute-start(bf16[8,128,128]{2,1,0:T(8,128)(2,1)S(1)} %fusion.12.refs_3_), channel_id=1, source_target_pairs={{0,8},{4,12},{8,0},{12,4},{16,24},{20,28},{24,16},{28,20},{1,9},{5... | collective-permute-start | bytes 786440 | tf_op jit(solution)/shard_map/ppermute | solution.py:397
  22.8 5.5 %copy-start.17 = (bf16[8,128,128]{2,1,0:T(8,128)(2,1)}, bf16[8,128,128]{2,1,0:T(8,128)(2,1)S(1)}, u32[]{:S(2)}) copy-start(bf16[8,128,128]{2,1,0:T(8,128)(2,1)S(1)} %fusion.5.refs_3_) | copy-start | bytes 786436
  22.8 13.9 %collective-permute-start.2 = (bf16[8,128,128]{2,1,0:T(8,128)(2,1)S(1)}, bf16[8,128,128]{2,1,0:T(8,128)(2,1)S(1)}, u32[]{:S(2)}, u32[]{:S(2)}) collective-permute-start(bf16[8,128,128]{2,1,0:T(8,128)(2,1)S(1)} %fusion.5.refs_3_), channel_id=1, source_target_pairs={{0,16},{4,20},{8,24},{12,28},{16,0},{20,4},{24,8},{28,12},{1,17},{... | collective-permute-start | bytes 786440 | tf_op jit(solution)/shard_map/ppermute | solution.py:397
  26.7 6.3 %collective-permute-start.3 = (s32[8,128]{1,0:T(8,128)S(1)}, s32[8,128]{1,0:T(8,128)S(1)}, u32[]{:S(2)}, u32[]{:S(2)}) collective-permute-start(s32[8,128]{1,0:T(8,128)S(1)} %broadcast_in_dim.21), channel_id=1, source_target_pairs={{0,4},{4,0},{8,12},{12,8},{16,20},{20,16},{24,28},{28,24},{1,5},{5... | collective-permute-start | bytes 12296 | tf_op jit(solution)/shard_map/ppermute | solution.py:397
  28.3 10.0 %copy-start = (bf16[512,2048]{1,0:T(8,128)(2,1)S(1)}, bf16[512,2048]{1,0:T(8,128)(2,1)}, u32[]{:S(2)}) copy-start(bf16[512,2048]{1,0:T(8,128)(2,1)} %refs_0_.17) | copy-start | bytes 6291460
  33.1 3.7 %collective-permute-start.4 = (s32[8,128]{1,0:T(8,128)S(1)}, s32[8,128]{1,0:T(8,128)S(1)}, u32[]{:S(2)}, u32[]{:S(2)}) collective-permute-start(s32[8,128]{1,0:T(8,128)S(1)} %add.111), channel_id=1, source_target_pairs={{0,8},{4,12},{8,0},{12,4},{16,24},{20,28},{24,16},{28,20},{1,9},{5... | collective-permute-start | bytes 12296 | tf_op jit(solution)/shard_map/ppermute | solution.py:397
  37.0 3.9 %copy-start.3 = (bf16[8,128,128]{2,1,0:T(8,128)(2,1)}, bf16[8,128,128]{2,1,0:T(8,128)(2,1)S(1)}, u32[]{:S(2)}) copy-start(bf16[8,128,128]{2,1,0:T(8,128)(2,1)S(1)} %get-tuple-element.88.refs_2_.refs_4_) | copy-start | bytes 786436
  37.0 7.3 %collective-permute-start.5 = (bf16[8,128,128]{2,1,0:T(8,128)(2,1)S(1)}, bf16[8,128,128]{2,1,0:T(8,128)(2,1)S(1)}, u32[]{:S(2)}, u32[]{:S(2)}) collective-permute-start(bf16[8,128,128]{2,1,0:T(8,128)(2,1)S(1)} %get-tuple-element.87), channel_id=1, source_target_pairs={{0,4},{4,0},{8,12},{12,8},{16,20},{20,16},{24,28},{28,24},{1,5},{5... | collective-permute-start | bytes 786440 | tf_op jit(solution)/shard_map/ppermute | solution.py:397
  38.3 4.5 %collective-permute-start.6 = (s32[8,128]{1,0:T(8,128)S(1)}, s32[8,128]{1,0:T(8,128)S(1)}, u32[]{:S(2)}, u32[]{:S(2)}) collective-permute-start(s32[8,128]{1,0:T(8,128)S(1)} %add.112), channel_id=1, source_target_pairs={{0,16},{4,20},{8,24},{12,28},{16,0},{20,4},{24,8},{28,12},{1,17},{... | collective-permute-start | bytes 12296 | tf_op jit(solution)/shard_map/ppermute | solution.py:397
  38.3 1.6 copy-start.1
  39.9 4.4 %copy-start.2 = (f32[512,1024]{1,0:T(8,128)S(1)}, f32[512,1024]{1,0:T(8,128)}, u32[]{:S(2)}) copy-start(f32[512,1024]{1,0:T(8,128)} %shard_map.88.refs_1_) | copy-start | bytes 6291460
  40.8 5.2 %collective-permute-start.7 = (bf16[512,1024]{1,0:T(8,128)(2,1)S(1)}, bf16[512,1024]{1,0:T(8,128)(2,1)}, u32[]{:S(2)}, u32[]{:S(2)}) collective-permute-start(bf16[512,1024]{1,0:T(8,128)(2,1)S(1)} %shard_map.89.refs_0_), channel_id=1, source_target_pairs={{0,1},{1,0},{2,3},{3,2},{4,5},{5,4},{6,7},{7,6},{8,9},{9,8},{10,11... | collective-permute-start | bytes 3145736 | tf_op jit(solution)/shard_map/ppermute | solution.py:397
  44.3 1.6 copy-start.4
  45.9 2.9 %collective-permute-start.8 = (bf16[512,1024]{1,0:T(8,128)(2,1)}, bf16[512,1024]{1,0:T(8,128)(2,1)S(1)}, u32[]{:S(2)}, u32[]{:S(2)}) collective-permute-start(bf16[512,1024]{1,0:T(8,128)(2,1)} %shard_map.90.refs_2_), channel_id=1, source_target_pairs={{0,1},{1,0},{2,3},{3,2},{4,5},{5,4},{6,7},{7,6},{8,9},{9,8},{10,11... | collective-permute-start | bytes 3145736 | tf_op jit(solution)/shard_map/ppermute | solution.py:397
  54.2 14.8 %collective-permute-start.10 = (bf16[512,512]{1,0:T(8,128)(2,1)S(1)}, bf16[512,512]{1,0:T(8,128)(2,1)S(1)}, u32[]{:S(2)}, u32[]{:S(2)}) collective-permute-start(bf16[512,512]{1,0:T(8,128)(2,1)S(1)} %shard_map.91.refs_6_), channel_id=1, source_target_pairs={{0,2},{1,3},{2,0},{3,1},{4,6},{5,7},{6,4},{7,5},{8,10},{9,11},{10,... | collective-permute-start | bytes 1572872 | tf_op jit(solution)/shard_map/ppermute | solution.py:505
  60.7 19.6 %collective-permute-start.11 = (bf16[512,512]{1,0:T(8,128)(2,1)S(1)}, bf16[512,512]{1,0:T(8,128)(2,1)S(1)}, u32[]{:S(2)}, u32[]{:S(2)}) collective-permute-start(bf16[512,512]{1,0:T(8,128)(2,1)S(1)} %shard_map.92.refs_6_), channel_id=1, source_target_pairs={{0,2},{1,3},{2,0},{3,1},{4,6},{5,7},{6,4},{7,5},{8,10},{9,11},{10,... | collective-permute-start | bytes 1572872 | tf_op jit(solution)/shard_map/ppermute | solution.py:505
  73.0 16.3 %collective-permute-start.12 = (bf16[512,256]{1,0:T(8,128)(2,1)S(1)}, bf16[512,256]{1,0:T(8,128)(2,1)S(1)}, u32[]{:S(2)}, u32[]{:S(2)}) collective-permute-start(bf16[512,256]{1,0:T(8,128)(2,1)S(1)} %shard_map.94.refs_6_), channel_id=1, source_target_pairs={{0,2},{1,3},{2,0},{3,1},{4,6},{5,7},{6,4},{7,5},{8,10},{9,11},{10,... | collective-permute-start | bytes 786440 | tf_op jit(solution)/shard_map/ppermute | solution.py:505
  80.3 7.0 %copy-start.11 = (bf16[512,1280]{1,0:T(8,128)(2,1)S(1)}, bf16[512,1280]{1,0:T(8,128)(2,1)}, u32[]{:S(2)}) copy-start(bf16[512,1280]{1,0:T(8,128)(2,1)} %param.9) | copy-start | bytes 3932164
  87.7 3.4 %copy-start.9 = (bf16[512,512]{1,0:T(8,128)(2,1)}, bf16[512,512]{1,0:T(8,128)(2,1)S(1)}, u32[]{:S(2)}) copy-start(bf16[512,512]{1,0:T(8,128)(2,1)S(1)} %get-tuple-element.83.refs_1_) | copy-start | bytes 1572868
  87.7 3.4 %copy-start.10 = (bf16[512,512]{1,0:T(8,128)(2,1)}, bf16[512,512]{1,0:T(8,128)(2,1)S(1)}, u32[]{:S(2)}) copy-start(bf16[512,512]{1,0:T(8,128)(2,1)S(1)} %get-tuple-element.84.refs_0_) | copy-start | bytes 1572868
  87.7 3.4 %collective-permute-start.14 = (bf16[512,512]{1,0:T(8,128)(2,1)S(1)}, bf16[512,512]{1,0:T(8,128)(2,1)S(1)}, u32[]{:S(2)}, u32[]{:S(2)}) collective-permute-start(bf16[512,512]{1,0:T(8,128)(2,1)S(1)} %get-tuple-element.83.refs_1_), channel_id=1, source_target_pairs={{0,1},{1,0},{2,3},{3,2},{4,5},{5,4},{6,7},{7,6},{8,9},{9,8},{10,11... | collective-permute-start | bytes 1572872 | tf_op jit(solution)/shard_map/ppermute | solution.py:397
  87.8 3.3 %collective-permute-start.13 = (bf16[512,512]{1,0:T(8,128)(2,1)S(1)}, bf16[512,512]{1,0:T(8,128)(2,1)S(1)}, u32[]{:S(2)}, u32[]{:S(2)}) collective-permute-start(bf16[512,512]{1,0:T(8,128)(2,1)S(1)} %get-tuple-element.84.refs_0_), channel_id=1, source_target_pairs={{0,1},{1,0},{2,3},{3,2},{4,5},{5,4},{6,7},{7,6},{8,9},{9,8},{10,11... | collective-permute-start | bytes 1572872 | tf_op jit(solution)/shard_map/ppermute | solution.py:397
  88.3 15.5 %collective-permute-start.16 = (bf16[512,512]{1,0:T(8,128)(2,1)S(1)}, bf16[512,512]{1,0:T(8,128)(2,1)S(1)}, u32[]{:S(2)}, u32[]{:S(2)}) collective-permute-start(bf16[512,512]{1,0:T(8,128)(2,1)S(1)} %get-tuple-element.84.refs_0_), channel_id=1, source_target_pairs={{0,2},{1,3},{2,0},{3,1},{4,6},{5,7},{6,4},{7,5},{8,10},{9,11},{10,... | collective-permute-start | bytes 1572872 | tf_op jit(solution)/shard_map/ppermute | solution.py:505
  89.5 1.6 copy-start.14
  89.5 1.6 collective-permute-start.15
  91.1 0.9 copy-start.20
  103.9 2.9 %copy-start.19 = (bf16[512,512]{1,0:T(8,128)(2,1)}, bf16[512,512]{1,0:T(8,128)(2,1)S(1)}, u32[]{:S(2)}) copy-start(bf16[512,512]{1,0:T(8,128)(2,1)S(1)} %collective-permute-done.16.refs_1_) | copy-start | bytes 1572868
  103.9 2.8 %collective-permute-start.17 = (bf16[512,512]{1,0:T(8,128)(2,1)S(1)}, bf16[512,512]{1,0:T(8,128)(2,1)S(1)}, u32[]{:S(2)}, u32[]{:S(2)}) collective-permute-start(bf16[512,512]{1,0:T(8,128)(2,1)S(1)} %collective-permute-done.16.refs_1_), channel_id=1, source_target_pairs={{0,1},{1,0},{2,3},{3,2},{4,5},{5,4},{6,7},{7,6},{8,9},{9,8},{10,11... | collective-permute-start | bytes 1572872 | tf_op jit(solution)/shard_map/ppermute | solution.py:397
  104.1 20.0 %collective-permute-start.18 = (bf16[512,512]{1,0:T(8,128)(2,1)}, bf16[512,512]{1,0:T(8,128)(2,1)S(1)}, u32[]{:S(2)}, u32[]{:S(2)}) collective-permute-start(bf16[512,512]{1,0:T(8,128)(2,1)} %copy-done.9), channel_id=1, source_target_pairs={{0,2},{1,3},{2,0},{3,1},{4,6},{5,7},{6,4},{7,5},{8,10},{9,11},{10,... | collective-permute-start | bytes 1572872 | tf_op jit(solution)/shard_map/ppermute | solution.py:505
  105.1 19.0 %collective-permute-start.19 = (bf16[512,256]{1,0:T(8,128)(2,1)}, bf16[512,256]{1,0:T(8,128)(2,1)S(1)}, u32[]{:S(2)}, u32[]{:S(2)}) collective-permute-start(bf16[512,256]{1,0:T(8,128)(2,1)} %copy-done.14), channel_id=1, source_target_pairs={{0,2},{1,3},{2,0},{3,1},{4,6},{5,7},{6,4},{7,5},{8,10},{9,11},{10,... | collective-permute-start | bytes 786440 | tf_op jit(solution)/shard_map/ppermute | solution.py:505
  106.7 0.8 copy-start.22
  124.1 2.4 %copy-start.12 = (bf16[512,256]{1,0:T(8,128)(2,1)}, bf16[512,256]{1,0:T(8,128)(2,1)S(1)}, u32[]{:S(2)}) copy-start(bf16[512,256]{1,0:T(8,128)(2,1)S(1)} %collective-permute-done.19.refs_3_) | copy-start | bytes 786436
  124.1 2.4 %copy-start.7 = (bf16[512,512]{1,0:T(8,128)(2,1)}, bf16[512,512]{1,0:T(8,128)(2,1)S(1)}, u32[]{:S(2)}) copy-start(bf16[512,512]{1,0:T(8,128)(2,1)S(1)} %collective-permute-done.18.refs_2_) | copy-start | bytes 1572868
  124.1 2.4 %collective-permute-start.20 = (bf16[512,512]{1,0:T(8,128)(2,1)S(1)}, bf16[512,512]{1,0:T(8,128)(2,1)S(1)}, u32[]{:S(2)}, u32[]{:S(2)}) collective-permute-start(bf16[512,512]{1,0:T(8,128)(2,1)S(1)} %collective-permute-done.18.refs_2_), channel_id=1, source_target_pairs={{0,1},{1,0},{2,3},{3,2},{4,5},{5,4},{6,7},{7,6},{8,9},{9,8},{10,11... | collective-permute-start | bytes 1572872 | tf_op jit(solution)/shard_map/ppermute | solution.py:397
  124.2 2.3 %collective-permute-start.21 = (bf16[512,256]{1,0:T(8,128)(2,1)S(1)}, bf16[512,256]{1,0:T(8,128)(2,1)S(1)}, u32[]{:S(2)}, u32[]{:S(2)}) collective-permute-start(bf16[512,256]{1,0:T(8,128)(2,1)S(1)} %collective-permute-done.19.refs_3_), channel_id=1, source_target_pairs={{0,1},{1,0},{2,3},{3,2},{4,5},{5,4},{6,7},{7,6},{8,9},{9,8},{10,11... | collective-permute-start | bytes 786440 | tf_op jit(solution)/shard_map/ppermute | solution.py:397
  126.5 0.9 copy-start.8
  133.8 8.6 %collective-permute-start.22 = (bf16[8,128,128]{2,1,0:T(8,128)(2,1)}, bf16[8,128,128]{2,1,0:T(8,128)(2,1)S(1)}, u32[]{:S(2)}, u32[]{:S(2)}) collective-permute-start(bf16[8,128,128]{2,1,0:T(8,128)(2,1)} %get-tuple-element.60.refs_8_), channel_id=1, source_target_pairs={{0,4},{4,0},{8,12},{12,8},{16,20},{20,16},{24,28},{28,24},{1,5},{5... | collective-permute-start | bytes 786440 | tf_op jit(solution)/shard_map/ppermute | solution.py:397
  143.5 2.4 %copy-start.15 = (bf16[8,128,128]{2,1,0:T(8,128)(2,1)}, bf16[8,128,128]{2,1,0:T(8,128)(2,1)S(1)}, u32[]{:S(2)}) copy-start(bf16[8,128,128]{2,1,0:T(8,128)(2,1)S(1)} %fusion.13.refs_5_) | copy-start | bytes 786436
  143.5 12.1 %collective-permute-start.23 = (bf16[8,128,128]{2,1,0:T(8,128)(2,1)S(1)}, bf16[8,128,128]{2,1,0:T(8,128)(2,1)S(1)}, u32[]{:S(2)}, u32[]{:S(2)}) collective-permute-start(bf16[8,128,128]{2,1,0:T(8,128)(2,1)S(1)} %fusion.13.refs_5_), channel_id=1, source_target_pairs={{0,8},{4,12},{8,0},{12,4},{16,24},{20,28},{24,16},{28,20},{1,9},{5... | collective-permute-start | bytes 786440 | tf_op jit(solution)/shard_map/ppermute | solution.py:397
  145.9 9.7 %copy-start.5 = (bf16[8,128,128]{2,1,0:T(8,128)(2,1)S(1)}, bf16[8,128,128]{2,1,0:T(8,128)(2,1)}, u32[]{:S(2)}) copy-start(bf16[8,128,128]{2,1,0:T(8,128)(2,1)} %get-tuple-element.64.refs_6_) | copy-start | bytes 786436
  155.7 4.1 %copy-start.18 = (bf16[8,128,128]{2,1,0:T(8,128)(2,1)}, bf16[8,128,128]{2,1,0:T(8,128)(2,1)S(1)}, u32[]{:S(2)}) copy-start(bf16[8,128,128]{2,1,0:T(8,128)(2,1)S(1)} %fusion.10.refs_6_) | copy-start | bytes 786436
  155.7 14.9 %collective-permute-start.24 = (bf16[8,128,128]{2,1,0:T(8,128)(2,1)S(1)}, bf16[8,128,128]{2,1,0:T(8,128)(2,1)S(1)}, u32[]{:S(2)}, u32[]{:S(2)}) collective-permute-start(bf16[8,128,128]{2,1,0:T(8,128)(2,1)S(1)} %fusion.10.refs_6_), channel_id=1, source_target_pairs={{0,16},{4,20},{8,24},{12,28},{16,0},{20,4},{24,8},{28,12},{1,17},{... | collective-permute-start | bytes 786440 | tf_op jit(solution)/shard_map/ppermute | solution.py:397
  171.5 8.2 %collective-permute-start.25 = (bf16[8,128,128]{2,1,0:T(8,128)(2,1)S(1)}, bf16[8,128,128]{2,1,0:T(8,128)(2,1)S(1)}, u32[]{:S(2)}, u32[]{:S(2)}) collective-permute-start(bf16[8,128,128]{2,1,0:T(8,128)(2,1)S(1)} %get-tuple-element.86), channel_id=1, source_target_pairs={{0,4},{4,0},{8,12},{12,8},{16,20},{20,16},{24,28},{28,24},{1,5},{5... | collective-permute-start | bytes 786440 | tf_op jit(solution)/shard_map/ppermute | solution.py:397
  (4 other events, 3.0 us)

commit v3 on v2

--- a/solution.py
+++ b/solution.py
@@ -197,46 +197,56 @@
     )(idx, *mine, *theirs, weight, other_weight)
 
 
-def grad_body(groups, with_acc, spans, idx, *refs):
+def grad_body(counts, row_tile, with_acc, idx, *refs):
     refs = list(refs)
-    acc = refs.pop(0)[...] if with_acc else None
+    cols = pl.ds(pl.multiple_of(pl.program_id(0) * row_tile, row_tile), row_tile)
+    acc = refs.pop(0)[:, cols] if with_acc else None
     out = refs.pop()
-    for _ in range(groups):
-        pieces = [refs.pop(0) for _ in spans]
-        w = refs.pop(0)
-        for piece, (lo, hi) in zip(pieces, spans):
+    for count in counts:
+        w, lo = refs[count], 0
+        for piece in refs[:count]:
+            hi = lo + piece.shape[1]
             t = dot(piece[...], w[:, lo:hi], NT)
             acc = t if acc is None else acc + t
-    out[...] = acc
-
-
-def grad_accumulate(idx, groups, acc, spans, weight, width, after=()):
+            lo = hi
+        refs = refs[count + 1 :]
+    out[:, cols] = acc
+
+
+def grad_accumulate(idx, groups, acc, weight, after=()):
     depth = weight.shape[0]
     rows = groups[0][0].shape[0]
     row_tile = math.gcd(depth, 512)
+    vmem = pl.BlockSpec(memory_space=pltpu.VMEM)
     in_specs, args = [], []
     if acc is not None:
-        in_specs.append(pl.BlockSpec((rows, row_tile), lambda i, s: (0, i)))
+        in_specs.append(vmem)
         args.append(acc)
     total = 0
     for g, pieces in enumerate(groups):
-        for piece in pieces:
-            in_specs.append(pl.BlockSpec(piece.shape, lambda i, s: (0, 0)))
-            args.append(piece)
-            total += piece.shape[1]
-        in_specs.append(pl.BlockSpec((row_tile, width), lambda i, s, g=g: (i, s[g])))
-        args.append(weight)
-    return call(
-        functools.partial(grad_body, len(groups), acc is not None, spans),
+        span = sum(piece.shape[1] for piece in pieces)
+        total += span
+        in_specs += [pl.BlockSpec(piece.shape, lambda i, s: (0, 0)) for piece in pieces]
+        in_specs.append(
+            pl.BlockSpec(
+                (pl.Element(row_tile), pl.Element(span)),
+                lambda i, s, g=g: (i * row_tile, s[g] * 128),
+            )
+        )
+        args += [*pieces, weight]
+    return call(
+        functools.partial(
+            grad_body, [len(pieces) for pieces in groups], row_tile, acc is not None
+        ),
         (depth // row_tile,),
         in_specs,
-        [pl.BlockSpec((rows, row_tile), lambda i, s: (0, i))],
-        [sds((rows, depth), F32)],
+        [vmem],
+        [pltpu.VMEM((rows, depth), F32)],
         2 * rows * depth * total,
         2 * depth * total + 8 * rows * depth,
-        {1: 0} if acc is not None else None,
+        None,
         after=after,
-        vmem=58,
+        vmem=44,
         token=True,
     )(idx, *args)
 
@@ -283,11 +293,11 @@
             pl.BlockSpec((rows, wide), lambda i, s: (0, i)),
             pl.BlockSpec((group, DH, DH), lambda i, s: (i, 0, 0)),
         ],
-        [sds((rows, half_heads * DH), BF16), sds((half_heads, DH, DH), BF16)],
+        [pltpu.HBM((rows, half_heads * DH), BF16), sds((half_heads, DH, DH), BF16)],
         2 * rows * half_heads * DH * (total + DH),
         half_heads * DH * (rows * 8 + 2 * total),
         after=after,
-        vmem=58,
+        vmem=44,
     )(idx, *args)
 
 
@@ -384,7 +394,7 @@
         rows * DH * half_heads * 20,
         {6 + n: n for n in range(extra)},
         after=after,
-        vmem=58,
+        vmem=24,
     )(half, k, v, later, dk, dv, *filled)
 
 
@@ -448,7 +458,7 @@
     tile = 256 if piece_width % 256 == 0 else 128
     tiles = piece_width // tile
     sum_spans = [(lo * tile, hi * tile) for lo, hi in cuts_of(tiles, (2, 2, 1))]
-    error_spans = [(lo * tile, hi * tile) for lo, hi in cuts_of(tiles, (2, 2, 1))]
+    error_spans = [(lo * tile, hi * tile) for lo, hi in cuts_of(tiles, (3, 2))]
 
     my_half = ctx_id & 1
     mine_ix = my_half[None].astype(jnp.int32)
@@ -508,16 +518,18 @@
     first = sum_spans[0][1]
     for n, (lo, hi) in enumerate(sum_spans):
         got = []
+        if n == 1:
+            own.append(terms(0, 0, first, after))
+            after = [own[0]]
         if n == 2:
-            own.append(terms(0, 0, first, after))
-            after = [own[0], *arrived[0]]
+            after = after + arrived[0]
         for by in range(1, chips):
             summed = terms(by, lo, hi, after)
             after = [summed]
             got.append(shift(summed, by))
         arrived.append(got)
-    if own:
-        own.append(terms(0, first, piece_width, after + arrived[1]))
+    if first < piece_width:
+        own.append(terms(0, first, piece_width, after))
     else:
         own.append(terms(0, 0, piece_width, after))
     own_spans = [(0, first), (first, piece_width)] if len(own) > 1 else [(0, piece_width)]
@@ -541,12 +553,10 @@
 
     errors = [error_of(lo, hi) for lo, hi in error_spans]
     near = [errors, [swap(error, "head", 0) for error in errors]]
-    idx = jnp.stack([chip * 2 + core, chip * 2 + 1 - core]).astype(jnp.int32)
-    acc, summed_near = grad_accumulate(
-        idx, near, None, error_spans, out_weight, piece_width
-    )
-
-    early = max(1, len(error_spans) - 2)
+    idx = jnp.stack([column(chip, core, 0), column(chip, 1 - core, 0)]).astype(jnp.int32)
+    acc, summed_near = grad_accumulate(idx, near, None, out_weight)
+
+    early = max(1, len(error_spans) - 1)
     gathered = [[shift(error, by) for by in range(1, chips)] for error in errors]
 
     def sources(select, token):
@@ -562,11 +572,8 @@
     last, last_ix, token = [], [], summed_near
     if chips > 1:
         far, devices, token = sources(slice(0, early), summed_near)
-        far_ix = jnp.stack([to_chip * 2 + to_core for to_chip, to_core in devices])
-        acc, summed_far = grad_accumulate(
-            far_ix.astype(jnp.int32), far, acc, error_spans[:early], out_weight, piece_width,
-            [token],
-        )
+        far_ix = jnp.stack([column(*device, 0) for device in devices]).astype(jnp.int32)
+        acc, summed_far = grad_accumulate(far_ix, far, acc, out_weight, [token])
         last, devices, token = sources(slice(early, None), summed_far)
         last_ix = [column(*device, error_spans[early][0]) for device in devices]
 

time: 187 us -> 176 us (0.941)
  Pallas kernels: 109 us -> 96.9 us
  local copies, waits for them, and re-layouts: 6.91 us -> 16.5 us
  waiting for transfers between devices: 32.8 us -> 28.3 us
  other arithmetic: 8.42 us -> 5.6 us
    pallas_call x19, Pallas kernels: 109 us -> 96.9 us  [call(): return lambda *args: kernel(*args, *after)]
    unnamed x52 -> x54, local copies, waits for them, and re-layouts: 5.75 us -> 15.3 us
    ppermute x6 -> x5, waiting for transfers between devices: 13.6 us -> 6.03 us  [shift(): lax.ppermute(array, 'head', [(i, (i + 2 * by) % size) for i in range(size)])]
    ppermute x20 -> x18, waiting for transfers between devices: 19.2 us -> 22.3 us  [swap(): return lax.ppermute(array, axis, [(i, i ^ 1 << bit) for i in range(size)])]
    ppermute x6 -> x5, starting transfers between devices: 6.33 us -> 5.3 us  [shift(): lax.ppermute(array, 'head', [(i, (i + 2 * by) % size) for i in range(size)])]
    ppermute x20 -> x18, starting transfers between devices: 21.3 us -> 20.7 us  [swap(): return lax.ppermute(array, axis, [(i, i ^ 1 << bit) for i in range(size)])]
  transfers between devices with their start and end apart: 26 -> 23, of which waited for: 13 -> 14; matrix products, arithmetic and copies ran while one was open for 4% -> 3% of each run, Pallas kernels for 49% -> 48%
where the time goes in v3:
time: 176 us; the launch traced here: 175 us
  Pallas kernels  96.9 us (55%)
  waiting for transfers between devices  28.3 us (16%)
  starting transfers between devices  26 us (15%)
  local copies, waits for them, and re-layouts  16.5 us (9%)
  other arithmetic  5.6 us (3%)
    pallas_call x19, Pallas kernels, call(): return lambda *args: kernel(*args, *after)  96.9 us
    ppermute x18, waiting for transfers between devices, swap(): return lax.ppermute(array, axis, [(i, i ^ 1 << bit) for i in range(size)])  22.3 us
    ppermute x18, starting transfers between devices, swap(): return lax.ppermute(array, axis, [(i, i ^ 1 << bit) for i in range(size)])  20.7 us
    unnamed x54, local copies, waits for them, and re-layouts  15.3 us
    ppermute x5, waiting for transfers between devices, shift(): lax.ppermute(array, 'head', [(i, (i + 2 * by) % size) for i in range(size)])  6.03 us
    ppermute x5, starting transfers between devices, shift(): lax.ppermute(array, 'head', [(i, (i + 2 * by) % size) for i in range(size)])  5.3 us
  transfers between devices with their start and end apart: 23, of which 14 were waited for; matrix products, arithmetic and copies ran while one was open for 3% of the time, Pallas kernels for 48%

profile of v3, /device:TPU:0, one launch (start us, length us, event | category | flops | bytes accessed | tf_op | source)
XLA Modules:
  0.0 175.0 jit_solution(16165227713213997351)
XLA Ops:
  1.1 2.6 %shard_map.85.refs_2_ = bf16[8,128,128]{2,1,0:T(8,128)(2,1)} custom-call(s32[1]{0:T(128)S(6)} %sub.63.idx, bf16[512,2048]{1,0:T(8,128)(2,1)} %refs_0_.19, bf16[512,2048]{1,0:T(8,128)(2,1)} %refs_1_.19), custom_call_target="tpu_custom_call" | custom-call | flops 1 | bytes 1 | tf_op jit(solution)/shard_map/pallas_call | solution.py:52
  3.7 2.6 %collective-permute-start = (bf16[8,128,128]{2,1,0:T(8,128)(2,1)}, bf16[8,128,128]{2,1,0:T(8,128)(2,1)S(1)}, u32[]{:S(2)}, u32[]{:S(2)}) collective-permute-start(bf16[8,128,128]{2,1,0:T(8,128)(2,1)} %shard_map.85.refs_2_), channel_id=1, source_target_pairs={{0,4},{4,0},{8,12},{12,8},{16,20},{20,16},{24,28},{28,24},{1,5},{5... | collective-permute-start | bytes 786440 | tf_op jit(solution)/shard_map/ppermute | solution.py:407
  6.3 2.6 %shard_map.86 = bf16[8,128,128]{2,1,0:T(8,128)(2,1)} custom-call(s32[1]{0:T(128)} %bitcast.idx, bf16[512,2048]{1,0:T(8,128)(2,1)} %refs_0_.19, bf16[512,2048]{1,0:T(8,128)(2,1)} %refs_1_.19, bf16[8,128,128]{2,1,0:T(8,128)(2,1)} %shard_map.85.refs_2_), custom_call_target="tpu_custom_call" | custom-call | flops 1 | bytes 1 | tf_op jit(solution)/shard_map/pallas_call | solution.py:52
  8.9 4.6 %collective-permute-done = bf16[8,128,128]{2,1,0:T(8,128)(2,1)S(1)} collective-permute-done((bf16[8,128,128]{2,1,0:T(8,128)(2,1)}, bf16[8,128,128]{2,1,0:T(8,128)(2,1)S(1)}, u32[]{:S(2)}, u32[]{:S(2)}) %collective-permute-start) | collective-permute-done | bytes 262176 | tf_op jit(solution)/shard_map/ppermute | solution.py:407
  14.5 1.9 %collective-permute-start.1 = (bf16[8,128,128]{2,1,0:T(8,128)(2,1)S(1)}, bf16[8,128,128]{2,1,0:T(8,128)(2,1)S(1)}, u32[]{:S(2)}, u32[]{:S(2)}) collective-permute-start(bf16[8,128,128]{2,1,0:T(8,128)(2,1)S(1)} %fusion.12.refs_3_), channel_id=1, source_target_pairs={{0,8},{4,12},{8,0},{12,4},{16,24},{20,28},{24,16},{28,20},{1,9},{5... | collective-permute-start | bytes 786440 | tf_op jit(solution)/shard_map/ppermute | solution.py:407
  16.4 4.6 %shard_map.87.refs_4_.refs_1_ = f32[512,1024]{1,0:T(8,128)} custom-call(s32[1]{0:T(128)} %bitcast.idx, bf16[512,2048]{1,0:T(8,128)(2,1)} %refs_0_.17, bf16[512,2048]{1,0:T(8,128)(2,1)} %refs_0_.19, bf16[512,2048]{1,0:T(8,128)(2,1)} %refs_1_.19, bf16[8,128,128]{2,1,0:T(8,128)(2,1)} %copy-done.23), custom_call_target="tpu_custom_call" | custom-call | flops 1 | bytes 1 | tf_op jit(solution)/shard_map/pallas_call | solution.py:52
  20.9 1.7 collective-permute-done.1
  22.8 2.7 %collective-permute-start.2 = (bf16[8,128,128]{2,1,0:T(8,128)(2,1)S(1)}, bf16[8,128,128]{2,1,0:T(8,128)(2,1)S(1)}, u32[]{:S(2)}, u32[]{:S(2)}) collective-permute-start(bf16[8,128,128]{2,1,0:T(8,128)(2,1)S(1)} %fusion.5.refs_3_), channel_id=1, source_target_pairs={{0,16},{4,20},{8,24},{12,28},{16,0},{20,4},{24,8},{28,12},{1,17},{... | collective-permute-start | bytes 786440 | tf_op jit(solution)/shard_map/ppermute | solution.py:407
  26.7 1.6 collective-permute-start.3
  28.3 4.7 %shard_map.88.refs_1_ = f32[512,1024]{1,0:T(8,128)} custom-call(s32[1]{0:T(128)S(6)} %sub.63.idx, bf16[512,2048]{1,0:T(8,128)(2,1)} %refs_0_.17, bf16[512,2048]{1,0:T(8,128)(2,1)} %refs_0_.19, bf16[512,2048]{1,0:T(8,128)(2,1)} %refs_1_.19, bf16[8,128,128]{2,1,0:T(8,128)(2,1)} %copy-done.24, f32[512,1024]{1,0:T(8,128)} %shard_map.87.refs_4_.refs_1_), custom_call_target="tpu_custom_call" | custom-call | flops 1 | bytes 1 | tf_op jit(solution)/shard_map/pallas_call | solution.py:52
  33.1 1.6 collective-permute-start.4
  34.7 2.0 %collective-permute-done.4 = s32[8,128]{1,0:T(8,128)S(1)} collective-permute-done((s32[8,128]{1,0:T(8,128)S(1)}, s32[8,128]{1,0:T(8,128)S(1)}, u32[]{:S(2)}, u32[]{:S(2)}) %collective-permute-start.4) | collective-permute-done | bytes 4128 | tf_op jit(solution)/shard_map/ppermute | solution.py:407
  37.0 1.3 collective-permute-start.5
  38.3 1.6 copy-done.3
  40.9 1.9 %collective-permute-done.6 = s32[8,128]{1,0:T(8,128)S(1)} collective-permute-done((s32[8,128]{1,0:T(8,128)S(1)}, s32[8,128]{1,0:T(8,128)S(1)}, u32[]{:S(2)}, u32[]{:S(2)}) %collective-permute-start.6) | collective-permute-done | bytes 4128 | tf_op jit(solution)/shard_map/ppermute | solution.py:407
  42.8 1.5 collective-permute-done.5.refs_2_.refs_4_
  44.3 1.6 shard_map.90.refs_2_
  46.0 2.9 %collective-permute-done.8.refs_3_ = bf16[512,1024]{1,0:T(8,128)(2,1)} collective-permute-done((bf16[512,1024]{1,0:T(8,128)(2,1)}, bf16[512,1024]{1,0:T(8,128)(2,1)}, u32[]{:S(2)}, u32[]{:S(2)}) %collective-permute-start.8) | collective-permute-done | bytes 1048608 | tf_op jit(solution)/shard_map/ppermute | solution.py:407
  48.9 5.7 %shard_map.91.refs_6_ = bf16[512,512]{1,0:T(8,128)(2,1)S(1)} custom-call(s32[3]{0:T(128)S(1)} %get-tuple-element.79.idx, bf16[512,1024]{1,0:T(8,128)(2,1)S(1)} %shard_map.89.refs_0_, bf16[512,1024]{1,0:T(8,128)(2,1)} %collective-permute-done.7.refs_1_, bf16[512,1024]{1,0:T(8,128)(2,1)} %shard_map.90.refs_2_, ...), custom_call_target="tpu_custom_call" | custom-call | flops 1 | bytes 1 | tf_op jit(solution)/shard_map/pallas_call | solution.py:52
  55.8 5.7 %shard_map.92.refs_6_ = bf16[512,512]{1,0:T(8,128)(2,1)S(1)} custom-call(s32[3]{0:T(128)S(1)} %get-tuple-element.87.idx, bf16[512,1024]{1,0:T(8,128)(2,1)S(1)} %shard_map.89.refs_0_, bf16[512,1024]{1,0:T(8,128)(2,1)} %collective-permute-done.7.refs_1_, bf16[512,1024]{1,0:T(8,128)(2,1)} %shard_map.90.refs_2_, ...), custom_call_target="tpu_custom_call" | custom-call | flops 1 | bytes 1 | tf_op jit(solution)/shard_map/pallas_call | solution.py:52
  61.5 5.7 %shard_map.93.refs_6_ = bf16[512,512]{1,0:T(8,128)(2,1)S(1)} custom-call(s32[3]{0:T(128)S(1)} %get-tuple-element.90.idx, bf16[512,1024]{1,0:T(8,128)(2,1)S(1)} %shard_map.89.refs_0_, bf16[512,1024]{1,0:T(8,128)(2,1)} %collective-permute-done.7.refs_1_, bf16[512,1024]{1,0:T(8,128)(2,1)} %shard_map.90.refs_2_, ...), custom_call_target="tpu_custom_call" | custom-call | flops 1 | bytes 1 | tf_op jit(solution)/shard_map/pallas_call | solution.py:52
  69.5 4.3 %shard_map.94.refs_6_ = bf16[512,256]{1,0:T(8,128)(2,1)S(1)} custom-call(s32[3]{0:T(128)S(1)} %get-tuple-element.88.idx, bf16[512,1024]{1,0:T(8,128)(2,1)S(1)} %shard_map.89.refs_0_, bf16[512,1024]{1,0:T(8,128)(2,1)} %collective-permute-done.7.refs_1_, bf16[512,1024]{1,0:T(8,128)(2,1)} %shard_map.90.refs_2_, ...), custom_call_target="tpu_custom_call" | custom-call | flops 1 | bytes 1 | tf_op jit(solution)/shard_map/pallas_call | solution.py:52
  75.0 7.3 %shard_map.95 = bf16[512,768]{1,0:T(8,128)(2,1)S(1)} custom-call(s32[3]{0:T(128)S(1)} %get-tuple-element.89.idx, bf16[512,1024]{1,0:T(8,128)(2,1)S(1)} %shard_map.89.refs_0_, bf16[512,1024]{1,0:T(8,128)(2,1)} %collective-permute-done.7.refs_1_, bf16[512,1024]{1,0:T(8,128)(2,1)} %shard_map.90.refs_2_, bf16[512,1024]{1,0:T(8,128)(2,1)} %collective-permute-done.8.refs_3_, ...), custom_call_target="tpu_custom_call" | custom-call | flops 1 | bytes 1 | tf_op jit(solution)/shard_map/pallas_call | solution.py:52
  82.3 1.2 copy-done.21
  85.0 1.6 collective-permute-done.12
  87.1 1.9 %collective-permute-done.14.refs_4_ = bf16[512,512]{1,0:T(8,128)(2,1)} collective-permute-done((bf16[512,512]{1,0:T(8,128)(2,1)S(1)}, bf16[512,512]{1,0:T(8,128)(2,1)}, u32[]{:S(2)}, u32[]{:S(2)}) %collective-permute-start.14) | collective-permute-done | bytes 524320 | tf_op jit(solution)/shard_map/ppermute | solution.py:407
  89.0 9.1 %shard_map.96 = (f32[512,2048]{1,0:T(8,128)S(1)}, f32[8,128]{1,0:T(8,128)S(1)}) custom-call(s32[2]{0:T(128)S(1)} %pad_add_fusion.3.idx, bf16[512,768]{1,0:T(8,128)(2,1)S(1)} %multiply_convert_fusion.refs_0_, bf16[512,512]{1,0:T(8,128)(2,1)S(1)} %multiply_convert_fusion.1.refs_1_, bf16[2048,5120]{1,0:T(8,128)(2,1)} %refs_5_.5, ...), custom_call_target="tpu_custom_call" | custom-call | flops 1 | bytes 1 | tf_op jit(solution)/shard_map/pallas_call | solution.py:52
  98.1 2.0 %copy-done.7 = f32[512,2048]{1,0:T(8,128)} copy-done((f32[512,2048]{1,0:T(8,128)}, f32[512,2048]{1,0:T(8,128)S(1)}, u32[]{:S(2)}) %copy-start.7) | copy-done | bytes 4194328
  100.1 4.0 %collective-permute-done.15.refs_1_ = bf16[512,768]{1,0:T(8,128)(2,1)} collective-permute-done((bf16[512,768]{1,0:T(8,128)(2,1)S(1)}, bf16[512,768]{1,0:T(8,128)(2,1)}, u32[]{:S(2)}, u32[]{:S(2)}) %collective-permute-start.15) | collective-permute-done | bytes 786464 | tf_op jit(solution)/shard_map/ppermute | solution.py:515
  105.1 1.6 collective-permute-done.16.refs_3_
  106.7 2.2 %copy-done.8 = f32[512,2048]{1,0:T(8,128)S(1)} copy-done((f32[512,2048]{1,0:T(8,128)S(1)}, f32[512,2048]{1,0:T(8,128)}, u32[]{:S(2)}) %copy-start.8) | copy-done | bytes 4194328
  108.9 7.0 %shard_map.97 = (f32[512,2048]{1,0:T(8,128)S(1)}, f32[8,128]{1,0:T(8,128)S(1)}) custom-call(s32[2]{0:T(128)S(1)} %pad_add_fusion.2.idx, f32[512,2048]{1,0:T(8,128)S(1)} %copy-done.8, bf16[512,768]{1,0:T(8,128)(2,1)} %collective-permute-done.15.refs_1_, bf16[2048,5120]{1,0:T(8,128)(2,1)} %refs_5_.5, bf16[512,768]{1,0:T(8,128)(2,1)} %collective-permute-done.16.refs_3_, ...), custom_call_target="tpu_custom_call" | custom-call | flops 1 | bytes 1 | tf_op jit(solution)/shard_map/pallas_call | solution.py:52
  115.9 2.0 %copy-done.4 = f32[512,2048]{1,0:T(8,128)} copy-done((f32[512,2048]{1,0:T(8,128)}, f32[512,2048]{1,0:T(8,128)S(1)}, u32[]{:S(2)}) %copy-start.4) | copy-done | bytes 4194328
  118.5 1.8 %collective-permute-done.18.refs_4_ = bf16[512,512]{1,0:T(8,128)(2,1)S(1)} collective-permute-done((bf16[512,512]{1,0:T(8,128)(2,1)S(1)}, bf16[512,512]{1,0:T(8,128)(2,1)S(1)}, u32[]{:S(2)}, u32[]{:S(2)}) %collective-permute-start.18) | collective-permute-done | bytes 524320 | tf_op jit(solution)/shard_map/ppermute | solution.py:407
  120.3 2.2 %copy-done.5 = f32[512,2048]{1,0:T(8,128)S(1)} copy-done((f32[512,2048]{1,0:T(8,128)S(1)}, f32[512,2048]{1,0:T(8,128)}, u32[]{:S(2)}) %copy-start.5) | copy-done | bytes 4194328
  122.5 4.5 %shard_map.98 = (bf16[512,1024]{1,0:T(8,128)(2,1)}, bf16[8,128,128]{2,1,0:T(8,128)(2,1)S(1)}) custom-call(s32[3]{0:T(128)S(1)} %add_add_fusion.idx, f32[512,2048]{1,0:T(8,128)S(1)} %copy-done.5, bf16[512,2048]{1,0:T(8,128)(2,1)S(1)} %copy-done.2, bf16[512,512]{1,0:T(8,128)(2,1)S(1)} %collective-permute-done.17.refs_2_, bf16[2048,5120]{1,0:T(8,128)(2,1)} %refs_5_.5, ...), custom_call_target="tpu_custom_call" | custom-call | flops 1 | bytes 1 | tf_op jit(solution)/shard_map/pallas_call | solution.py:52
  127.0 1.5 collective-permute-start.19
  128.6 4.5 %shard_map.99 = (bf16[512,1024]{1,0:T(8,128)(2,1)}, bf16[8,128,128]{2,1,0:T(8,128)(2,1)S(1)}) custom-call(s32[3]{0:T(128)S(1)} %add_add_fusion.1.idx, f32[512,2048]{1,0:T(8,128)S(1)} %copy-done.5, bf16[512,2048]{1,0:T(8,128)(2,1)S(1)} %copy-done.2, bf16[512,512]{1,0:T(8,128)(2,1)S(1)} %collective-permute-done.17.refs_2_, bf16[2048,5120]{1,0:T(8,128)(2,1)} %refs_5_.5, ...), custom_call_target="tpu_custom_call" | custom-call | flops 1 | bytes 1 | tf_op jit(solution)/shard_map/pallas_call | solution.py:52
  133.1 2.2 %collective-permute-done.19 = bf16[8,128,128]{2,1,0:T(8,128)(2,1)S(1)} collective-permute-done((bf16[8,128,128]{2,1,0:T(8,128)(2,1)S(1)}, bf16[8,128,128]{2,1,0:T(8,128)(2,1)S(1)}, u32[]{:S(2)}, u32[]{:S(2)}) %collective-permute-start.19) | collective-permute-done | bytes 262176 | tf_op jit(solution)/shard_map/ppermute | solution.py:407
  135.4 1.8 %collective-permute-start.20 = (bf16[8,128,128]{2,1,0:T(8,128)(2,1)S(1)}, bf16[8,128,128]{2,1,0:T(8,128)(2,1)S(1)}, u32[]{:S(2)}, u32[]{:S(2)}) collective-permute-start(bf16[8,128,128]{2,1,0:T(8,128)(2,1)S(1)} %fusion.13.refs_5_), channel_id=1, source_target_pairs={{0,8},{4,12},{8,0},{12,4},{16,24},{20,28},{24,16},{28,20},{1,9},{5... | collective-permute-start | bytes 786440 | tf_op jit(solution)/shard_map/ppermute | solution.py:407
  137.9 9.5 %shard_map.100 = (f32[512,2048]{1,0:T(8,128)}, f32[512,1024]{1,0:T(8,128)}, f32[512,1024]{1,0:T(8,128)}, f32[8,128]{1,0:T(8,128)}) custom-call(s32[2]{0:T(128)} %pad_add_fusion.idx, bf16[512,2048]{1,0:T(8,128)(2,1)} %refs_0_.17, bf16[512,2048]{1,0:T(8,128)(2,1)} %refs_0_.19, bf16[512,2048]{1,0:T(8,128)(2,1)} %refs_1_.19, ...), custom_call_target="tpu_custom_call" | custom-call | flops 1 | bytes 1 | tf_op jit(solution)/shard_map/pallas_call | solution.py:52
  148.5 3.5 %collective-permute-start.21 = (bf16[8,128,128]{2,1,0:T(8,128)(2,1)S(1)}, bf16[8,128,128]{2,1,0:T(8,128)(2,1)S(1)}, u32[]{:S(2)}, u32[]{:S(2)}) collective-permute-start(bf16[8,128,128]{2,1,0:T(8,128)(2,1)S(1)} %fusion.10.refs_6_), channel_id=1, source_target_pairs={{0,16},{4,20},{8,24},{12,28},{16,0},{20,4},{24,8},{28,12},{1,17},{... | collective-permute-start | bytes 786440 | tf_op jit(solution)/shard_map/ppermute | solution.py:407
  152.5 10.1 %shard_map.101 = (f32[512,2048]{1,0:T(8,128)}, f32[512,1024]{1,0:T(8,128)}, f32[512,1024]{1,0:T(8,128)}, f32[8,128]{1,0:T(8,128)}) custom-call(s32[2]{0:T(128)} %pad_add_fusion.1.idx, bf16[512,2048]{1,0:T(8,128)(2,1)} %refs_0_.17, bf16[512,2048]{1,0:T(8,128)(2,1)} %refs_0_.19, bf16[512,2048]{1,0:T(8,128)(2,1)} %refs_1_.19, ...), custom_call_target="tpu_custom_call", output_to_operand_aliasing={{0}: (6, {})} | custom-call | flops 1 | bytes 1 | tf_op jit(solution)/shard_map/pallas_call | solution.py:52
  163.0 1.6 collective-permute-start.22
  164.6 1.6 copy-done.14
  166.2 1.6 copy-done.15
  168.5 3.2 %shard_map.102 = (f32[512,2048]{1,0:T(8,128)}, f32[512,2048]{1,0:T(8,128)}) custom-call(s32[1]{0:T(128)} %bitcast.idx, bf16[512,2048]{1,0:T(8,128)(2,1)S(1)} %copy-done, bf16[512,2048]{1,0:T(8,128)(2,1)S(1)} %copy-done.1, bf16[8,128,128]{2,1,0:T(8,128)(2,1)S(1)} %get-tuple-element.81.refs_2_, f32[512,1024]{1,0:T(8,128)S(1)} %copy-done.14, ...), custom_call_target="tpu_custom_call" | custom-call | flops 1 | bytes 1 | tf_op jit(solution)/shard_map/pallas_call | solution.py:52
  171.8 3.2 %shard_map.103 = (f32[512,2048]{1,0:T(8,128)}, f32[512,2048]{1,0:T(8,128)}) custom-call(s32[1]{0:T(128)S(6)} %sub.63.idx, bf16[512,2048]{1,0:T(8,128)(2,1)S(1)} %copy-done, bf16[512,2048]{1,0:T(8,128)(2,1)S(1)} %copy-done.1, bf16[8,128,128]{2,1,0:T(8,128)(2,1)S(1)} %collective-permute-done.22.refs_2_, ...), custom_call_target="tpu_custom_call", output_to_operand_aliasing={{0}: (6, {}), {1}: (7, {})} | custom-call | flops 1 | bytes 1 | tf_op jit(solution)/shard_map/pallas_call | solution.py:52
  (96 shorter events, 15.3 us)
Async XLA Ops:
  0.6 48.3 %collective-permute-start.9 = (bf16[2048,5120]{1,0:T(8,128)(2,1)}, bf16[2048,5120]{1,0:T(8,128)(2,1)}, u32[]{:S(2)}, u32[]{:S(2)}) collective-permute-start(bf16[2048,5120]{1,0:T(8,128)(2,1)} %refs_5_.5), channel_id=1, source_target_pairs={{0,1},{1,0},{2,3},{3,2},{4,5},{5,4},{6,7},{7,6},{8,9},{9,8},{10,11... | collective-permute-start | bytes 62914568 | tf_op jit(solution)/shard_map/ppermute | solution.py:407
  3.7 9.7 %collective-permute-start = (bf16[8,128,128]{2,1,0:T(8,128)(2,1)}, bf16[8,128,128]{2,1,0:T(8,128)(2,1)S(1)}, u32[]{:S(2)}, u32[]{:S(2)}) collective-permute-start(bf16[8,128,128]{2,1,0:T(8,128)(2,1)} %shard_map.85.refs_2_), channel_id=1, source_target_pairs={{0,4},{4,0},{8,12},{12,8},{16,20},{20,16},{24,28},{28,24},{1,5},{5... | collective-permute-start | bytes 786440 | tf_op jit(solution)/shard_map/ppermute | solution.py:407
  14.5 1.9 %copy-start.23 = (bf16[8,128,128]{2,1,0:T(8,128)(2,1)}, bf16[8,128,128]{2,1,0:T(8,128)(2,1)S(1)}, u32[]{:S(2)}) copy-start(bf16[8,128,128]{2,1,0:T(8,128)(2,1)S(1)} %fusion.12.refs_3_) | copy-start | bytes 786436
  14.5 8.2 %copy-start.18 = (bf16[8,128,128]{2,1,0:T(8,128)(2,1)S(1)}, bf16[8,128,128]{2,1,0:T(8,128)(2,1)}, u32[]{:S(2)}) copy-start(bf16[8,128,128]{2,1,0:T(8,128)(2,1)} %shard_map.86) | copy-start | bytes 786436
  14.5 11.0 %copy-start.26 = (s32[512]{0:T(512)S(1)}, s32[512]{0:T(512)}, u32[]{:S(2)}) copy-start(s32[512]{0:T(512)} %param.11) | copy-start | bytes 6148
  14.5 8.2 %collective-permute-start.1 = (bf16[8,128,128]{2,1,0:T(8,128)(2,1)S(1)}, bf16[8,128,128]{2,1,0:T(8,128)(2,1)S(1)}, u32[]{:S(2)}, u32[]{:S(2)}) collective-permute-start(bf16[8,128,128]{2,1,0:T(8,128)(2,1)S(1)} %fusion.12.refs_3_), channel_id=1, source_target_pairs={{0,8},{4,12},{8,0},{12,4},{16,24},{20,28},{24,16},{28,20},{1,9},{5... | collective-permute-start | bytes 786440 | tf_op jit(solution)/shard_map/ppermute | solution.py:407
  22.8 5.5 %copy-start.24 = (bf16[8,128,128]{2,1,0:T(8,128)(2,1)}, bf16[8,128,128]{2,1,0:T(8,128)(2,1)S(1)}, u32[]{:S(2)}) copy-start(bf16[8,128,128]{2,1,0:T(8,128)(2,1)S(1)} %fusion.5.refs_3_) | copy-start | bytes 786436
  22.8 13.9 %collective-permute-start.2 = (bf16[8,128,128]{2,1,0:T(8,128)(2,1)S(1)}, bf16[8,128,128]{2,1,0:T(8,128)(2,1)S(1)}, u32[]{:S(2)}, u32[]{:S(2)}) collective-permute-start(bf16[8,128,128]{2,1,0:T(8,128)(2,1)S(1)} %fusion.5.refs_3_), channel_id=1, source_target_pairs={{0,16},{4,20},{8,24},{12,28},{16,0},{20,4},{24,8},{28,12},{1,17},{... | collective-permute-start | bytes 786440 | tf_op jit(solution)/shard_map/ppermute | solution.py:407
  26.7 6.3 %collective-permute-start.3 = (s32[8,128]{1,0:T(8,128)S(1)}, s32[8,128]{1,0:T(8,128)S(1)}, u32[]{:S(2)}, u32[]{:S(2)}) collective-permute-start(s32[8,128]{1,0:T(8,128)S(1)} %broadcast_in_dim.21), channel_id=1, source_target_pairs={{0,4},{4,0},{8,12},{12,8},{16,20},{20,16},{24,28},{28,24},{1,5},{5... | collective-permute-start | bytes 12296 | tf_op jit(solution)/shard_map/ppermute | solution.py:407
  28.3 10.0 %copy-start.2 = (bf16[512,2048]{1,0:T(8,128)(2,1)S(1)}, bf16[512,2048]{1,0:T(8,128)(2,1)}, u32[]{:S(2)}) copy-start(bf16[512,2048]{1,0:T(8,128)(2,1)} %refs_0_.17) | copy-start | bytes 6291460
  33.1 3.7 %collective-permute-start.4 = (s32[8,128]{1,0:T(8,128)S(1)}, s32[8,128]{1,0:T(8,128)S(1)}, u32[]{:S(2)}, u32[]{:S(2)}) collective-permute-start(s32[8,128]{1,0:T(8,128)S(1)} %add.114), channel_id=1, source_target_pairs={{0,8},{4,12},{8,0},{12,4},{16,24},{20,28},{24,16},{28,20},{1,9},{5... | collective-permute-start | bytes 12296 | tf_op jit(solution)/shard_map/ppermute | solution.py:407
  37.0 3.9 %copy-start.11 = (bf16[8,128,128]{2,1,0:T(8,128)(2,1)}, bf16[8,128,128]{2,1,0:T(8,128)(2,1)S(1)}, u32[]{:S(2)}) copy-start(bf16[8,128,128]{2,1,0:T(8,128)(2,1)S(1)} %get-tuple-element.86.refs_2_.refs_4_) | copy-start | bytes 786436
  37.0 7.3 %collective-permute-start.5 = (bf16[8,128,128]{2,1,0:T(8,128)(2,1)S(1)}, bf16[8,128,128]{2,1,0:T(8,128)(2,1)S(1)}, u32[]{:S(2)}, u32[]{:S(2)}) collective-permute-start(bf16[8,128,128]{2,1,0:T(8,128)(2,1)S(1)} %get-tuple-element.85), channel_id=1, source_target_pairs={{0,4},{4,0},{8,12},{12,8},{16,20},{20,16},{24,28},{28,24},{1,5},{5... | collective-permute-start | bytes 786440 | tf_op jit(solution)/shard_map/ppermute | solution.py:407
  38.3 4.5 %collective-permute-start.6 = (s32[8,128]{1,0:T(8,128)S(1)}, s32[8,128]{1,0:T(8,128)S(1)}, u32[]{:S(2)}, u32[]{:S(2)}) collective-permute-start(s32[8,128]{1,0:T(8,128)S(1)} %add.115), channel_id=1, source_target_pairs={{0,16},{4,20},{8,24},{12,28},{16,0},{20,4},{24,8},{28,12},{1,17},{... | collective-permute-start | bytes 12296 | tf_op jit(solution)/shard_map/ppermute | solution.py:407
  38.3 1.6 copy-start.3
  39.9 4.4 %copy-start.6 = (f32[512,1024]{1,0:T(8,128)S(1)}, f32[512,1024]{1,0:T(8,128)}, u32[]{:S(2)}) copy-start(f32[512,1024]{1,0:T(8,128)} %shard_map.88.refs_1_) | copy-start | bytes 6291460
  40.8 5.2 %collective-permute-start.7 = (bf16[512,1024]{1,0:T(8,128)(2,1)S(1)}, bf16[512,1024]{1,0:T(8,128)(2,1)}, u32[]{:S(2)}, u32[]{:S(2)}) collective-permute-start(bf16[512,1024]{1,0:T(8,128)(2,1)S(1)} %shard_map.89.refs_0_), channel_id=1, source_target_pairs={{0,1},{1,0},{2,3},{3,2},{4,5},{5,4},{6,7},{7,6},{8,9},{9,8},{10,11... | collective-permute-start | bytes 3145736 | tf_op jit(solution)/shard_map/ppermute | solution.py:407
  44.3 1.6 copy-start.16
  45.9 3.0 %collective-permute-start.8 = (bf16[512,1024]{1,0:T(8,128)(2,1)}, bf16[512,1024]{1,0:T(8,128)(2,1)}, u32[]{:S(2)}, u32[]{:S(2)}) collective-permute-start(bf16[512,1024]{1,0:T(8,128)(2,1)} %shard_map.90.refs_2_), channel_id=1, source_target_pairs={{0,1},{1,0},{2,3},{3,2},{4,5},{5,4},{6,7},{7,6},{8,9},{9,8},{10,11... | collective-permute-start | bytes 3145736 | tf_op jit(solution)/shard_map/ppermute | solution.py:407
  54.6 14.9 %collective-permute-start.10 = (bf16[512,512]{1,0:T(8,128)(2,1)S(1)}, bf16[512,512]{1,0:T(8,128)(2,1)S(1)}, u32[]{:S(2)}, u32[]{:S(2)}) collective-permute-start(bf16[512,512]{1,0:T(8,128)(2,1)S(1)} %shard_map.91.refs_6_), channel_id=1, source_target_pairs={{0,2},{1,3},{2,0},{3,1},{4,6},{5,7},{6,4},{7,5},{8,10},{9,11},{10,... | collective-permute-start | bytes 1572872 | tf_op jit(solution)/shard_map/ppermute | solution.py:515
  67.2 15.0 %collective-permute-start.11 = (bf16[512,512]{1,0:T(8,128)(2,1)S(1)}, bf16[512,512]{1,0:T(8,128)(2,1)S(1)}, u32[]{:S(2)}, u32[]{:S(2)}) collective-permute-start(bf16[512,512]{1,0:T(8,128)(2,1)S(1)} %shard_map.93.refs_6_), channel_id=1, source_target_pairs={{0,2},{1,3},{2,0},{3,1},{4,6},{5,7},{6,4},{7,5},{8,10},{9,11},{10,... | collective-permute-start | bytes 1572872 | tf_op jit(solution)/shard_map/ppermute | solution.py:515
  73.8 12.8 %collective-permute-start.12 = (bf16[512,256]{1,0:T(8,128)(2,1)S(1)}, bf16[512,256]{1,0:T(8,128)(2,1)S(1)}, u32[]{:S(2)}, u32[]{:S(2)}) collective-permute-start(bf16[512,256]{1,0:T(8,128)(2,1)S(1)} %shard_map.94.refs_6_), channel_id=1, source_target_pairs={{0,2},{1,3},{2,0},{3,1},{4,6},{5,7},{6,4},{7,5},{8,10},{9,11},{10,... | collective-permute-start | bytes 786440 | tf_op jit(solution)/shard_map/ppermute | solution.py:515
  83.9 5.1 %collective-permute-start.13 = (bf16[512,768]{1,0:T(8,128)(2,1)S(1)}, bf16[512,768]{1,0:T(8,128)(2,1)}, u32[]{:S(2)}, u32[]{:S(2)}) collective-permute-start(bf16[512,768]{1,0:T(8,128)(2,1)S(1)} %multiply_convert_fusion.refs_0_), channel_id=1, source_target_pairs={{0,1},{1,0},{2,3},{3,2},{4,5},{5,4},{6,7},{7,6},{8,9},{9,8},{10,11... | collective-permute-start | bytes 2359304 | tf_op jit(solution)/shard_map/ppermute | solution.py:407
  84.0 20.1 %collective-permute-start.15 = (bf16[512,768]{1,0:T(8,128)(2,1)S(1)}, bf16[512,768]{1,0:T(8,128)(2,1)}, u32[]{:S(2)}, u32[]{:S(2)}) collective-permute-start(bf16[512,768]{1,0:T(8,128)(2,1)S(1)} %multiply_convert_fusion.refs_0_), channel_id=1, source_target_pairs={{0,2},{1,3},{2,0},{3,1},{4,6},{5,7},{6,4},{7,5},{8,10},{9,11},{10,... | collective-permute-start | bytes 2359304 | tf_op jit(solution)/shard_map/ppermute | solution.py:515
  86.8 2.1 %collective-permute-start.14 = (bf16[512,512]{1,0:T(8,128)(2,1)S(1)}, bf16[512,512]{1,0:T(8,128)(2,1)}, u32[]{:S(2)}, u32[]{:S(2)}) collective-permute-start(bf16[512,512]{1,0:T(8,128)(2,1)S(1)} %multiply_convert_fusion.1.refs_1_), channel_id=1, source_target_pairs={{0,1},{1,0},{2,3},{3,2},{4,5},{5,4},{6,7},{7,6},{8,9},{9,8},{10,11... | collective-permute-start | bytes 1572872 | tf_op jit(solution)/shard_map/ppermute | solution.py:407
  98.1 2.0 %copy-start.7 = (f32[512,2048]{1,0:T(8,128)}, f32[512,2048]{1,0:T(8,128)S(1)}, u32[]{:S(2)}) copy-start(f32[512,2048]{1,0:T(8,128)S(1)} %get-tuple-element.49.refs_0_) | copy-start | bytes 12582916
  104.0 2.6 %collective-permute-start.16 = (bf16[512,768]{1,0:T(8,128)(2,1)}, bf16[512,768]{1,0:T(8,128)(2,1)}, u32[]{:S(2)}, u32[]{:S(2)}) collective-permute-start(bf16[512,768]{1,0:T(8,128)(2,1)} %collective-permute-done.15.refs_1_), channel_id=1, source_target_pairs={{0,1},{1,0},{2,3},{3,2},{4,5},{5,4},{6,7},{7,6},{8,9},{9,8},{10,11... | collective-permute-start | bytes 2359304 | tf_op jit(solution)/shard_map/ppermute | solution.py:407
  104.1 14.3 %collective-permute-start.17 = (bf16[512,512]{1,0:T(8,128)(2,1)S(1)}, bf16[512,512]{1,0:T(8,128)(2,1)S(1)}, u32[]{:S(2)}, u32[]{:S(2)}) collective-permute-start(bf16[512,512]{1,0:T(8,128)(2,1)S(1)} %multiply_convert_fusion.1.refs_1_), channel_id=1, source_target_pairs={{0,2},{1,3},{2,0},{3,1},{4,6},{5,7},{6,4},{7,5},{8,10},{9,11},{10,... | collective-permute-start | bytes 1572872 | tf_op jit(solution)/shard_map/ppermute | solution.py:515
  106.7 2.2 %copy-start.8 = (f32[512,2048]{1,0:T(8,128)S(1)}, f32[512,2048]{1,0:T(8,128)}, u32[]{:S(2)}) copy-start(f32[512,2048]{1,0:T(8,128)} %copy-done.7) | copy-start | bytes 12582916
  115.9 2.0 %copy-start.4 = (f32[512,2048]{1,0:T(8,128)}, f32[512,2048]{1,0:T(8,128)S(1)}, u32[]{:S(2)}) copy-start(f32[512,2048]{1,0:T(8,128)S(1)} %get-tuple-element.53.refs_0_) | copy-start | bytes 12582916
  118.4 1.9 %collective-permute-start.18 = (bf16[512,512]{1,0:T(8,128)(2,1)S(1)}, bf16[512,512]{1,0:T(8,128)(2,1)S(1)}, u32[]{:S(2)}, u32[]{:S(2)}) collective-permute-start(bf16[512,512]{1,0:T(8,128)(2,1)S(1)} %collective-permute-done.17.refs_2_), channel_id=1, source_target_pairs={{0,1},{1,0},{2,3},{3,2},{4,5},{5,4},{6,7},{7,6},{8,9},{9,8},{10,11... | collective-permute-start | bytes 1572872 | tf_op jit(solution)/shard_map/ppermute | solution.py:407
  120.3 2.2 %copy-start.5 = (f32[512,2048]{1,0:T(8,128)S(1)}, f32[512,2048]{1,0:T(8,128)}, u32[]{:S(2)}) copy-start(f32[512,2048]{1,0:T(8,128)} %copy-done.4) | copy-start | bytes 12582916
  127.0 8.3 %collective-permute-start.19 = (bf16[8,128,128]{2,1,0:T(8,128)(2,1)S(1)}, bf16[8,128,128]{2,1,0:T(8,128)(2,1)S(1)}, u32[]{:S(2)}, u32[]{:S(2)}) collective-permute-start(bf16[8,128,128]{2,1,0:T(8,128)(2,1)S(1)} %get-tuple-element.58.refs_6_), channel_id=1, source_target_pairs={{0,4},{4,0},{8,12},{12,8},{16,20},{20,16},{24,28},{28,24},{1,5},{5... | collective-permute-start | bytes 786440 | tf_op jit(solution)/shard_map/ppermute | solution.py:407
  133.1 4.8 %copy-start.9 = (bf16[8,128,128]{2,1,0:T(8,128)(2,1)}, bf16[8,128,128]{2,1,0:T(8,128)(2,1)S(1)}, u32[]{:S(2)}) copy-start(bf16[8,128,128]{2,1,0:T(8,128)(2,1)S(1)} %get-tuple-element.62.refs_6_) | copy-start | bytes 786436
  135.4 12.1 %copy-start.19 = (bf16[8,128,128]{2,1,0:T(8,128)(2,1)}, bf16[8,128,128]{2,1,0:T(8,128)(2,1)S(1)}, u32[]{:S(2)}) copy-start(bf16[8,128,128]{2,1,0:T(8,128)(2,1)S(1)} %collective-permute-done.19) | copy-start | bytes 786436
  135.4 2.5 %copy-start.22 = (bf16[8,128,128]{2,1,0:T(8,128)(2,1)}, bf16[8,128,128]{2,1,0:T(8,128)(2,1)S(1)}, u32[]{:S(2)}) copy-start(bf16[8,128,128]{2,1,0:T(8,128)(2,1)S(1)} %fusion.13.refs_5_) | copy-start | bytes 786436
  135.4 12.0 %collective-permute-start.20 = (bf16[8,128,128]{2,1,0:T(8,128)(2,1)S(1)}, bf16[8,128,128]{2,1,0:T(8,128)(2,1)S(1)}, u32[]{:S(2)}, u32[]{:S(2)}) collective-permute-start(bf16[8,128,128]{2,1,0:T(8,128)(2,1)S(1)} %fusion.13.refs_5_), channel_id=1, source_target_pairs={{0,8},{4,12},{8,0},{12,4},{16,24},{20,28},{24,16},{28,20},{1,9},{5... | collective-permute-start | bytes 786440 | tf_op jit(solution)/shard_map/ppermute | solution.py:407
  148.5 4.0 %copy-start.25 = (bf16[8,128,128]{2,1,0:T(8,128)(2,1)}, bf16[8,128,128]{2,1,0:T(8,128)(2,1)S(1)}, u32[]{:S(2)}) copy-start(bf16[8,128,128]{2,1,0:T(8,128)(2,1)S(1)} %fusion.10.refs_6_) | copy-start | bytes 786436
  148.5 14.3 %collective-permute-start.21 = (bf16[8,128,128]{2,1,0:T(8,128)(2,1)S(1)}, bf16[8,128,128]{2,1,0:T(8,128)(2,1)S(1)}, u32[]{:S(2)}, u32[]{:S(2)}) collective-permute-start(bf16[8,128,128]{2,1,0:T(8,128)(2,1)S(1)} %fusion.10.refs_6_), channel_id=1, source_target_pairs={{0,16},{4,20},{8,24},{12,28},{16,0},{20,4},{24,8},{28,12},{1,17},{... | collective-permute-start | bytes 786440 | tf_op jit(solution)/shard_map/ppermute | solution.py:407
  152.5 10.3 %copy-start.10 = (bf16[8,128,128]{2,1,0:T(8,128)(2,1)S(1)}, bf16[8,128,128]{2,1,0:T(8,128)(2,1)}, u32[]{:S(2)}) copy-start(bf16[8,128,128]{2,1,0:T(8,128)(2,1)} %copy-done.9) | copy-start | bytes 786436
  152.5 10.3 %copy-start.20 = (bf16[8,128,128]{2,1,0:T(8,128)(2,1)S(1)}, bf16[8,128,128]{2,1,0:T(8,128)(2,1)}, u32[]{:S(2)}) copy-start(bf16[8,128,128]{2,1,0:T(8,128)(2,1)} %copy-done.19) | copy-start | bytes 786436
  152.5 12.1 %copy-start = (bf16[512,2048]{1,0:T(8,128)(2,1)S(1)}, bf16[512,2048]{1,0:T(8,128)(2,1)}, u32[]{:S(2)}) copy-start(bf16[512,2048]{1,0:T(8,128)(2,1)} %refs_0_.19) | copy-start | bytes 6291460
  152.5 12.1 %copy-start.1 = (bf16[512,2048]{1,0:T(8,128)(2,1)S(1)}, bf16[512,2048]{1,0:T(8,128)(2,1)}, u32[]{:S(2)}) copy-start(bf16[512,2048]{1,0:T(8,128)(2,1)} %refs_1_.19) | copy-start | bytes 6291460
  163.0 8.7 %collective-permute-start.22 = (bf16[8,128,128]{2,1,0:T(8,128)(2,1)S(1)}, bf16[8,128,128]{2,1,0:T(8,128)(2,1)S(1)}, u32[]{:S(2)}, u32[]{:S(2)}) collective-permute-start(bf16[8,128,128]{2,1,0:T(8,128)(2,1)S(1)} %get-tuple-element.82), channel_id=1, source_target_pairs={{0,4},{4,0},{8,12},{12,8},{16,20},{20,16},{24,28},{28,24},{1,5},{5... | collective-permute-start | bytes 786440 | tf_op jit(solution)/shard_map/ppermute | solution.py:407
  164.6 1.6 copy-start.14
  166.2 1.6 copy-start.15
  168.5 3.2 %copy-start.12 = (f32[512,1024]{1,0:T(8,128)S(1)}, f32[512,1024]{1,0:T(8,128)}, u32[]{:S(2)}) copy-start(f32[512,1024]{1,0:T(8,128)} %get-tuple-element.70.refs_3_) | copy-start | bytes 6291460
  168.5 3.3 %copy-start.13 = (f32[512,1024]{1,0:T(8,128)S(1)}, f32[512,1024]{1,0:T(8,128)}, u32[]{:S(2)}) copy-start(f32[512,1024]{1,0:T(8,128)} %get-tuple-element.71.refs_4_) | copy-start | bytes 6291460
  (2 other events, 2.0 us)

commit v4 on v3

v4 whole, which is shorter than its diff:
```python
import functools
import math

import jax
import jax.numpy as jnp
from jax import lax
from jax.experimental import pallas as pl
from jax.experimental.pallas import tpu as pltpu
from jax.sharding import PartitionSpec as P

DH = 128
GROUP = 4
HINT = 1000000000000
NT = (((1,), (1,)), ((), ()))
TN = (((0,), (0,)), ((), ()))
F32 = jnp.float32
BF16 = jnp.bfloat16


def dot(a, b, dims=(((1,), (0,)), ((), ()))):
    return lax.dot_general(a, b, dims, preferred_element_type=F32)


class Entries:
    def __init__(self, refs, at):
        self.refs, self.at = refs, at

    def __getitem__(self, n):
        if not isinstance(n, int):
            return jnp.where(n == 0, self[0], self[1])
        more = self.at[n][1]
        return self.refs[n][0] + more if more else self.refs[n][0]


def call(body, at, grid, in_specs, out_specs, out_shape, flops, moved, aliases=None, after=(), vmem=40, scratch=(), token=False):
    count = len(in_specs)
    many = isinstance(out_specs, (list, tuple))
    if token:
        out_specs = [*out_specs, pl.BlockSpec((8, 128), lambda i, s: (0, 0))]
        out_shape = [*out_shape, sds((8, 128), F32)]

    def seen(spec):
        if spec.index_map is None:
            return spec
        index_map = spec.index_map
        return pl.BlockSpec(spec.block_shape, lambda i, *s: index_map(i, Entries(s, at)))

    in_specs = [seen(spec) for spec in in_specs]
    out_specs = [seen(spec) for spec in out_specs] if many else seen(out_specs)

    def ordered(*refs):
        scalars, refs = refs[: len(at)], list(refs[len(at) :])
        if token:
            refs.pop(count + len(after) + len(out_shape) - 1)[...] = jnp.zeros((8, 128), F32)
        body(Entries(scalars, at), *refs[:count], *refs[count + len(after) :])

    kernel = pl.pallas_call(
        ordered,
        grid_spec=pltpu.PrefetchScalarGridSpec(
            num_scalar_prefetch=len(at),
            grid=grid,
            in_specs=list(in_specs) + [pl.BlockSpec(memory_space=pl.ANY)] * len(after),
            out_specs=out_specs,
            scratch_shapes=list(scratch),
        ),
        out_shape=out_shape,
        input_output_aliases={n + len(at) - 1: m for n, m in (aliases or {}).items()},
        compiler_params=pltpu.CompilerParams(vmem_limit_bytes=vmem * 1024 * 1024),
        cost_estimate=pl.CostEstimate(
            flops=max(1, flops // HINT), bytes_accessed=max(1, moved // HINT), transcendentals=0
        ),
    )
    return lambda table, *args: kernel(*(table[n] for n, _ in at), *args, *after)


def sds(shape, dtype):
    return jax.ShapeDtypeStruct(shape, dtype)


def lower_mask(n):
    rows = lax.broadcasted_iota(jnp.int32, (n, n), 0)
    cols = lax.broadcasted_iota(jnp.int32, (n, n), 1)
    return rows >= cols


def cut(i):
    return slice(i * DH, (i + 1) * DH)


def group_of(half_heads):
    return math.gcd(half_heads, GROUP)


def kv_body(group, chunks, idx, k, v, *outs):
    for n, out in enumerate(outs):

        @pl.when(pl.program_id(0) == n)
        def _(out=out):
            for i in range(group):
                out[i] = dot(k[:, cut(i)], v[:, cut(i)], TN).astype(BF16)


def kv_states(table, at, k, v, heads, chunks, after=()):
    rows = k.shape[0]
    blk = pl.BlockSpec((rows, heads * DH), lambda i, s: (0, s[0] * chunks + i))
    return call(
        functools.partial(kv_body, heads, chunks),
        at,
        (chunks,),
        [blk, blk],
        [pl.BlockSpec((heads, DH, DH), lambda i, s: (0, 0, 0))] * chunks,
        [sds((heads, DH, DH), BF16)] * chunks,
        2 * rows * DH * DH * heads * chunks,
        rows * DH * heads * chunks * 4,
        after=after,
        vmem=58,
    )(table, k, v)


def intra_body(group, block, idx, q, k, v, out):
    mask = lower_mask(block)
    n = q.shape[0] // block
    for i in range(group):
        c = cut(i)
        state = None
        for b in range(n):
            r = slice(b * block, (b + 1) * block)
            qb, kb, vb = q[r, c], k[r, c], v[r, c]
            s = jnp.where(mask, dot(qb, kb, NT), 0.0).astype(BF16)
            o = dot(s, vb)
            if state is not None:
                o = o + dot(qb, state.astype(BF16))
            if b < n - 1:
                kv = dot(kb, vb, TN)
                state = kv if state is None else state + kv
            out[r, c] = o


def intra(table, at, q, k, v, half_heads, after):
    rows = k.shape[0]
    block = math.gcd(rows, 256)
    group = group_of(half_heads)
    steps = half_heads // group
    blk = pl.BlockSpec((rows, group * DH), lambda i, s: (0, s[0] * steps + i))
    return call(
        functools.partial(intra_body, group, block),
        at,
        (steps,),
        [blk, blk, blk],
        pl.BlockSpec((rows, group * DH), lambda i, s: (0, i)),
        sds((rows, half_heads * DH), F32),
        4 * rows * (block + DH) * DH * half_heads,
        rows * DH * half_heads * 10,
        after=after,
        vmem=58,
    )(table, q, k, v)


def attn_body(heads, scale, idx, q, part, *refs):
    *states, out = refs
    for n, state in enumerate(states):

        @pl.when(pl.program_id(0) == n)
        def _(state=state):
            for i in range(heads):
                c = cut(i)
                out[:, c] = (scale * (part[:, c] + dot(q[:, c], state[i]))).astype(BF16)


def attend(table, at, scale, q, part, states):
    rows = q.shape[0]
    chunks, heads = len(states), states[0].shape[0]
    blk = pl.BlockSpec((rows, heads * DH), lambda i, s: (0, i))
    return call(
        functools.partial(attn_body, heads, scale),
        at,
        (chunks,),
        [
            pl.BlockSpec((rows, heads * DH), lambda i, s: (0, s[0] * chunks + i)),
            blk,
        ]
        + [pl.BlockSpec((heads, DH, DH), lambda i, s: (0, 0, 0))] * chunks,
        blk,
        sds((rows, chunks * heads * DH), BF16),
        2 * rows * DH * DH * heads * chunks,
        rows * DH * heads * chunks * 8,
    )(table, q, part, *states)


def project_body(idx, a0, b0, a1, b1, w, wo, out, acc):
    i = pl.program_id(0)

    @pl.when(i == 0)
    def _():
        acc[...] = dot(a0[...], w[...]) + dot(b0[...], wo[...])

    @pl.when(i == 1)
    def _():
        out[...] = (acc[...] + dot(a1[...], w[...]) + dot(b1[...], wo[...])).astype(BF16)


def project(table, at, mine, theirs, weight, other_weight, span, after=()):
    rows, depth = mine[0].shape
    whole = pl.BlockSpec((rows, depth), lambda i, s: (0, 0))
    return call(
        project_body,
        at,
        (2,),
        [
            whole,
            whole,
            whole,
            whole,
            pl.BlockSpec(
                (pl.Element(depth), pl.Element(span)), lambda i, s: (s[i] * depth, s[2] * 128)
            ),
            pl.BlockSpec(
                (pl.Element(depth), pl.Element(span)), lambda i, s: (s[i] * depth, s[2] * 128)
            ),
        ],
        pl.BlockSpec((rows, span), lambda i, s: (0, 0)),
        sds((rows, span), BF16),
        8 * rows * depth * span,
        8 * depth * span + 8 * rows * depth + 2 * rows * span,
        after=after,
        vmem=44,
        scratch=[pltpu.VMEM((rows, span), F32)],
    )(table, *mine, *theirs, weight, other_weight)


def grad_body(counts, with_acc, idx, *refs):
    refs = list(refs)
    acc = refs.pop(0)[...] if with_acc else None
    out = refs.pop()
    for count in counts:
        w, lo = refs[count], 0
        for piece in refs[:count]:
            hi = lo + piece.shape[1]
            t = dot(piece[...], w[:, lo:hi], NT)
            acc = t if acc is None else acc + t
            lo = hi
        refs = refs[count + 1 :]
    out[...] = acc


def grad_accumulate(table, at, groups, acc, weight, after=()):
    depth = weight.shape[0]
    rows = groups[0][0].shape[0]
    row_tile = math.gcd(depth, 512)
    in_specs, args = [], []
    if acc is not None:
        in_specs.append(pl.BlockSpec((rows, row_tile), lambda i, s: (0, i)))
        args.append(pltpu.with_memory_space_constraint(acc, pltpu.HBM))
    total = 0
    for g, pieces in enumerate(groups):
        span = sum(piece.shape[1] for piece in pieces)
        total += span
        in_specs += [pl.BlockSpec(piece.shape, lambda i, s: (0, 0)) for piece in pieces]
        in_specs.append(
            pl.BlockSpec(
                (pl.Element(row_tile), pl.Element(span)),
                lambda i, s, g=g: (i * row_tile, s[g] * 128),
            )
        )
        args += [*pieces, weight]
    return call(
        functools.partial(grad_body, [len(pieces) for pieces in groups], acc is not None),
        at,
        (depth // row_tile,),
        in_specs,
        [pl.BlockSpec((rows, row_tile), lambda i, s: (0, i))],
        [pltpu.HBM((rows, depth), F32)],
        2 * rows * depth * total,
        2 * depth * total + 8 * rows * depth,
        None,
        after=after,
        vmem=44,
        token=True,
    )(table, *args)


def last_body(group, counts, idx, acc, q, *refs):
    *refs, g_out, r_out, held, sems = refs
    i = pl.program_id(0)
    wide = held.shape[2]
    steps = held.shape[0]

    def fetch(n):
        start = pl.multiple_of((idx[0] * steps + n) * wide, wide)
        return pltpu.make_async_copy(acc.at[:, pl.ds(start, wide)], held.at[n], sems.at[n])

    @pl.when(i == 0)
    def _():
        for n in range(steps):
            fetch(n).start()

    t = None
    for count in counts:
        w, lo = refs[count], 0
        for piece in refs[:count]:
            hi = lo + piece.shape[1]
            u = dot(piece[...], w[:, lo:hi], NT)
            t = u if t is None else t + u
            lo = hi
        refs = refs[count + 1 :]
    fetch(i).wait()
    t = held[i] if t is None else t + held[i]
    g = t.astype(BF16)
    g_out[...] = g
    for i in range(group):
        r_out[i] = dot(q[:, cut(i)], g[:, cut(i)], TN).astype(BF16)


def grad_last(table, at, acc, q, groups, weight, half_heads, after=()):
    rows = acc.shape[0]
    group = group_of(half_heads)
    steps = half_heads // group
    wide = group * DH
    mine = pl.BlockSpec((rows, wide), lambda i, s: (0, s[0] * steps + i))
    in_specs, total = [pl.BlockSpec(memory_space=pltpu.HBM), mine], 0
    args = [pltpu.with_memory_space_constraint(acc, pltpu.HBM), q]
    for n, pieces in enumerate(groups):
        span = sum(piece.shape[1] for piece in pieces)
        total += span
        in_specs += [pl.BlockSpec(piece.shape, lambda i, s: (0, 0)) for piece in pieces]
        in_specs.append(
            pl.BlockSpec(
                (pl.Element(wide), pl.Element(span)),
                lambda i, s, n=n: ((s[0] * steps + i) * wide, s[1 + n] * 128),
            )
        )
        args += [*pieces, weight]
    return call(
        functools.partial(last_body, group, [len(pieces) for pieces in groups]),
        at,
        (steps,),
        in_specs,
        [
            pl.BlockSpec((rows, wide), lambda i, s: (0, i)),
            pl.BlockSpec((group, DH, DH), lambda i, s: (i, 0, 0)),
        ],
        [pltpu.HBM((rows, half_heads * DH), BF16), sds((half_heads, DH, DH), BF16)],
        2 * rows * half_heads * DH * (total + DH),
        half_heads * DH * (rows * 8 + 2 * total),
        after=after,
        vmem=44,
        scratch=[
            pltpu.VMEM((steps, rows, wide), F32),
            pltpu.SemaphoreType.DMA((steps,)),
        ],
    )(table, *args)


def back_body(group, block, scale, extra, idx, q, k, v, g, state, *refs):
    dq, dk, dv = refs[extra:]
    mask = lower_mask(block)
    n = q.shape[0] // block
    for i in range(group):
        c = cut(i)
        before = state[i].astype(F32)
        later = None
        dks, dvs = [], []
        for b in range(n):
            r = slice(b * block, (b + 1) * block)
            qb, kb, vb, gb = q[r, c], k[r, c], v[r, c], g[r, c]
            gs = jnp.where(mask, dot(gb, vb, NT), 0.0).astype(BF16)
            s = jnp.where(mask, dot(qb, kb, NT), 0.0).astype(BF16)
            dq[r, c] = scale * (dot(gs, kb) + dot(gb, before.astype(BF16), NT))
            dks.append(dot(gs, qb, TN))
            dvs.append(dot(s, gb, TN))
            if b < n - 1:
                before = before + dot(kb, vb, TN)
        for b in reversed(range(n)):
            r = slice(b * block, (b + 1) * block)
            qb, kb, vb, gb = q[r, c], k[r, c], v[r, c], g[r, c]
            dkb, dvb = dks[b], dvs[b]
            if later is not None:
                lb = later.astype(BF16)
                dkb = dkb + dot(vb, lb, NT)
                dvb = dvb + dot(kb, lb)
            dk[r, c] = dkb.astype(dk.dtype)
            dv[r, c] = dvb.astype(dv.dtype)
            if b > 0:
                qg = dot(qb, gb, TN)
                later = qg if later is None else later + qg


def back_local(table, at, pairs, scale, q, k, v, g, state, filled, half_heads, after):
    rows, width = q.shape
    block = math.gcd(rows, 256)
    group = math.gcd(half_heads, 2)
    first, steps = pairs[0], pairs[1] - pairs[0]
    heads = group * steps
    wide = group * DH
    mine = pl.BlockSpec((rows, wide), lambda i, s: (0, s[0] * (half_heads // group) + first + i))
    own = pl.BlockSpec((rows, wide), lambda i, s: (0, first + i))
    extra = len(filled)
    half = sds((rows, half_heads * DH), BF16)
    return call(
        functools.partial(back_body, group, block, scale, extra),
        at,
        (steps,),
        [
            mine,
            mine,
            mine,
            own,
            pl.BlockSpec((group, DH, DH), lambda i, s: (first + i, 0, 0)),
        ]
        + [pl.BlockSpec(memory_space=pl.ANY)] * extra,
        [mine, own, own],
        [sds((rows, width), F32), half, half],
        2 * rows * DH * (5 * block + 4 * DH) * heads,
        rows * DH * heads * 20,
        {6 + n: n for n in range(extra)},
        after=after,
        vmem=58,
        token=True,
    )(table, q, k, v, g, state, *filled)


def later_body(heads, scale, extra, idx, k, v, later, dk_in, dv_in, *refs):
    dk, dv = refs[extra:]
    for i in range(heads):
        c = cut(i)
        dk[:, c] = scale * (dk_in[:, c] + dot(v[:, c], later[i], NT))
        dv[:, c] = scale * (dv_in[:, c] + dot(k[:, c], later[i]))


def add_later(table, at, scale, k, v, later, dk, dv, filled, half_heads, after):
    rows, width = k.shape
    block = math.gcd(rows, 128)
    wide = half_heads * DH
    mine = pl.BlockSpec((block, wide), lambda i, s: (i, s[0]))
    own = pl.BlockSpec((block, wide), lambda i, s: (i, 0))
    extra = len(filled)
    return call(
        functools.partial(later_body, half_heads, scale, extra),
        at,
        (rows // block,),
        [mine, mine, pl.BlockSpec((half_heads, DH, DH), lambda i, s: (0, 0, 0)), own, own]
        + [pl.BlockSpec(memory_space=pl.ANY)] * extra,
        [mine, mine],
        [sds((rows, width), F32)] * 2,
        4 * rows * DH * DH * half_heads,
        rows * DH * half_heads * 20,
        {6 + n: n for n in range(extra)},
        after=after,
        vmem=24,
    )(table, k, v, later, dk, dv, *filled)


def tie(array, *others):
    return lax.optimization_barrier((array,) + others)


def swap(array, axis, bit):
    size = lax.axis_size(axis)
    return lax.ppermute(array, axis, [(i, i ^ (1 << bit)) for i in range(size)])


def scan_states(theirs, mine, ctx_bits, flipped, fill):
    chunks = range(len(mine))
    pos = lax.axis_index("ctx")
    if flipped:
        pos = lax.axis_size("ctx") - 1 - pos
    held = []

    def beside(step, sent):
        got = [swap(array, "ctx", step) for array in sent]
        for n in chunks:
            done = fill[step, n]([sent[n], *held]) if (step, n) in fill else held
            got[n], *held[:] = tie(got[n], *done)
        return [array.astype(F32) for array in got]

    got = beside(0, theirs)
    own = [array.astype(F32) for array in mine]
    total = [own[n] + got[n] for n in chunks]
    prefix = [jnp.zeros_like(array) for array in total]
    for bit in range(1, ctx_bits):
        other = beside(bit, [array.astype(BF16) for array in total])
        before = (pos >> bit) & 1 == 1
        prefix = [prefix[n] + jnp.where(before, other[n], 0.0) for n in chunks]
        total = [total[n] + other[n] for n in chunks]
    upper = pos & 1 == 1
    mine_prefix = [(prefix[n] + jnp.where(upper, got[n], 0.0)).astype(BF16) for n in chunks]
    crossed = []
    for n in chunks:
        sent = (prefix[n] + jnp.where(upper, 0.0, own[n])).astype(BF16)
        if crossed:
            sent, crossed[-1], *held[:] = tie(sent, crossed[-1], *held)
        crossed.append(swap(sent, "ctx", 0))
        if (ctx_bits, n) in fill:
            held[:] = fill[ctx_bits, n]([sent, *held])
    return mine_prefix, crossed, held


def cuts_of(tiles, sizes):
    ends, at = [], 0
    for size in sizes:
        at = min(at + size, tiles)
        ends.append(at)
    ends[-1] = tiles
    starts = [0] + ends[:-1]
    return [(lo, hi) for lo, hi in zip(starts, ends) if lo < hi]


def on_device(queries, keys, values, teacher, out_weight, valid):
    rows, width = queries.shape
    heads = width // DH
    half_heads = heads // 2
    ctx_size = lax.axis_size("ctx")
    ctx_bits = ctx_size.bit_length() - 1
    chips = lax.axis_size("head") // 2
    ctx_id, head_id = lax.axis_index("ctx"), lax.axis_index("head")
    chip, core = head_id // 2, head_id % 2
    scale = 1.0 / math.sqrt(DH * rows * ctx_size)
    piece_width = teacher.shape[1]
    tile = 256 if piece_width % 256 == 0 else 128
    tiles = piece_width // tile
    sum_spans = [(lo * tile, hi * tile) for lo, hi in cuts_of(tiles, (2, 2, 1))]
    error_spans = [(lo * tile, hi * tile) for lo, hi in cuts_of(tiles, (3, 2))]

    my_half = ctx_id & 1
    entries = [my_half, 1 - my_half]
    for by in range(chips):
        for of_core in (core, 1 - core):
            device = lax.rem(chip + by, chips) * 2 + of_core
            entries.append(device * (piece_width // 128))
    table = [entry.astype(jnp.int32)[None] for entry in entries]
    mine_ix, theirs_ix = (0, 0), (1, 0)

    def column(by, crossed, lo):
        return 2 + 2 * (by % chips) + crossed, lo // 128


    chunks = 2 if half_heads % 2 == 0 else 1
    chunk_heads = half_heads // chunks
    last_step = ctx_bits - 1

    kv_theirs = kv_states(table, [theirs_ix], keys, values, chunk_heads, chunks)
    kv_mine = kv_states(table, [mine_ix], keys, values, chunk_heads, chunks, [kv_theirs[0]])
    parts, counts = {}, {}

    def intra_of(name, half):
        def run(after):
            parts[name] = intra(table, [half], queries, keys, values, half_heads, after)
            return [parts[name]]

        return run

    def first_fill(after):
        counts["own"], *after = tie(jnp.full((8, 128), jnp.sum(valid), jnp.int32), *after)
        got = swap(counts["own"], "ctx", 0)
        after = intra_of("mine", mine_ix)(after)
        got, *after = tie(got, *after)
        counts["pair"] = counts["own"] + got
        if last_step > 1:
            counts["got"] = swap(counts["pair"], "ctx", 1)
        return after

    def last_fill(after):
        if "own" not in counts:
            after = first_fill(after)
        after = intra_of("theirs", theirs_ix)(after)
        count = counts["pair"]
        for bit in range(1, last_step):
            got = counts["got"] if bit == 1 else swap(count, "ctx", bit)
            got, *after = tie(got, *after)
            count = count + got
        return [*after, count]

    if chunks > 1:
        fill = {(last_step, 0): first_fill, (ctx_bits, 0): last_fill}
    else:
        fill = {(last_step, 0): last_fill}
    before_mine, before_theirs, (*_, count) = scan_states(
        kv_theirs, kv_mine, ctx_bits, False, fill
    )
    count = count + swap(count, "ctx", last_step)
    before_theirs[-1], count = tie(before_theirs[-1], count)
    other_weight = swap(out_weight, "head", 0)

    def both_cores(array):
        return array, swap(array, "head", 0)

    attn_mine = both_cores(
        attend(table, [mine_ix], scale, queries, parts["mine"], before_mine)
    )
    attn_theirs = both_cores(
        attend(table, [theirs_ix], scale, queries, parts["theirs"], before_theirs)
    )

    def terms(by, lo, hi, after=()):
        at = [mine_ix, theirs_ix, column(by, 0, lo)]
        return project(
            table, at, attn_mine, attn_theirs, out_weight, other_weight, hi - lo, after
        )

    def shift(array, by):
        size = 2 * chips
        return lax.ppermute(array, "head", [(i, (i + 2 * by) % size) for i in range(size)])

    arrived, own, after = [], [], []
    first = sum_spans[0][1]
    for n, (lo, hi) in enumerate(sum_spans):
        got = []
        if n == 1:
            own.append(terms(0, 0, first, after))
            after = [own[0]]
        if n == 2:
            after = after + arrived[0]
        for by in range(1, chips):
            summed = terms(by, lo, hi, after)
            after = [summed]
            got.append(shift(summed, by))
        arrived.append(got)
    if first < piece_width:
        own.append(terms(0, first, piece_width, after))
    else:
        own.append(terms(0, 0, piece_width, after))
    own_spans = [(0, first), (first, piece_width)] if len(own) > 1 else [(0, piece_width)]

    factor = rows * ctx_size / count[0, 0].astype(F32)
    weigh = (valid.astype(F32) * factor)[:, None]

    def columns(pieces, spans, lo, hi):
        inside = [
            piece[:, max(lo - base, 0) : hi - base].astype(F32)
            for (base, end), piece in zip(spans, pieces)
            if base < hi and lo < end
        ]
        return jnp.concatenate(inside, 1)

    def error_of(lo, hi):
        predicted = columns(own, own_spans, lo, hi)
        for by in range(1, chips):
            predicted = predicted + columns([got[by - 1] for got in arrived], sum_spans, lo, hi)
        return (weigh * (predicted - teacher[:, lo:hi].astype(F32))).astype(BF16)

    errors = [error_of(lo, hi) for lo, hi in error_spans]
    near = [errors, [swap(error, "head", 0) for error in errors]]
    states = {
        "theirs": jnp.concatenate(before_theirs),
        "mine": jnp.concatenate(before_mine),
    }
    acc, summed_near = grad_accumulate(
        table, [column(0, 0, 0), column(0, 1, 0)], near, None, out_weight, list(states.values())
    )

    early = max(1, len(error_spans) - 1)
    gathered = [[shift(error, by) for by in range(1, chips)] for error in errors]

    def sources(select, token, lo):
        groups, at = [], []
        for by in range(1, chips):
            pieces = [got[by - 1] for got in gathered[select]]
            *late, token = tie(pieces[0], *pieces[1:], token)
            groups += [pieces, [swap(piece, "head", 0) for piece in late]]
            at += [column(chips - by, 0, lo), column(chips - by, 1, lo)]
        return groups, at, token

    last, last_at, token = [], [], summed_near
    if chips > 1:
        far, at, token = sources(slice(0, early), summed_near, 0)
        acc, summed_far = grad_accumulate(table, at, far, acc, out_weight, [token])
        last, last_at, token = sources(slice(early, None), summed_far, error_spans[early][0])

    def last_of(half, after=()):
        return grad_last(table, [half, *last_at], acc, queries, last, out_weight, half_heads, after)

    g_theirs, r_theirs = last_of(theirs_ix, [token])
    g_mine, r_mine = last_of(mine_ix, [r_theirs])
    done_q, done_kv = [], {"theirs": [], "mine": []}
    halves = {"theirs": (theirs_ix, g_theirs), "mine": (mine_ix, g_mine)}

    def back(name, lo, hi, after):
        half, g = halves[name]
        *got, token = back_local(
            table, [half], (lo, hi), scale, queries, keys, values, g, states[name],
            done_q + done_kv[name], half_heads, after,
        )
        done_q[:], done_kv[name] = got[:1], got[1:]
        return [token]

    groups = half_heads // math.gcd(half_heads, 2)
    split = max(1, groups * 3 // 4)
    order = [("mine", 0, split), ("theirs", 0, groups), ("mine", split, groups)]

    def beside_backward(step):
        def run(after):
            if step == 0:
                return [r_mine]
            todo = order[: step if step < 3 else 0]
            del order[: len(todo)]
            for name, lo, hi in todo:
                if lo < hi:
                    after = back(name, lo, hi, after)
            return after

        return run

    (later_mine,), (later_theirs,), token = scan_states(
        [r_theirs], [r_mine], ctx_bits, True,
        {(n, 0): beside_backward(n) for n in range(ctx_bits)},
    )
    token = [*token, later_mine]
    for name, lo, hi in order:
        if lo < hi:
            token = back(name, lo, hi, token)
    (q_grad,) = done_q
    grads = add_later(
        table, [mine_ix], scale, keys, values, later_mine, *done_kv["mine"], [], half_heads, token
    )
    k_grad, v_grad = add_later(
        table, [theirs_ix], scale, keys, values, later_theirs, *done_kv["theirs"], list(grads),
        half_heads, [],
    )
    return q_grad, k_grad, v_grad


def solution(mesh):
    in_specs = (
        P("ctx", "head"),
        P("ctx", "head"),
        P("ctx", "head"),
        P("ctx", "head"),
        P("head", None),
        P("ctx"),
    )
    out_specs = (P("ctx", "head"), P("ctx", "head"), P("ctx", "head"))
    return jax.shard_map(
        on_device, mesh=mesh, in_specs=in_specs, out_specs=out_specs, check_vma=False
    )
```

time: 176 us -> 169 us (0.960)
  local copies, waits for them, and re-layouts: 16.5 us -> 4.51 us
  starting transfers between devices: 26 us -> 29.8 us
  other arithmetic: 5.6 us -> 8.54 us
  waiting for transfers between devices: 28.3 us -> 25.8 us
    unnamed x54 -> x49, local copies, waits for them, and re-layouts: 15.3 us -> 3.24 us
    ppermute x18 -> x22, waiting for transfers between devices: 22.3 us -> 15.6 us  [swap(): return lax.ppermute(array, axis, [(i, i ^ 1 << bit) for i in range(size)])]
    ppermute x5, waiting for transfers between devices: 6.03 us -> 10.2 us  [shift(): lax.ppermute(array, 'head', [(i, (i + 2 * by) % size) for i in range(size)])]
    ppermute x18 -> x22, starting transfers between devices: 20.7 us -> 24.8 us  [swap(): return lax.ppermute(array, axis, [(i, i ^ 1 << bit) for i in range(size)])]
    convert_element_type x6 -> x9, other arithmetic: 2.71 us -> 5.39 us  [the longest x6 4.93 us: scan_states(): other = beside(bit, [array.astype(BF16) for array in total])]
    convert_element_type x2, other arithmetic: 0.59 us -> 2.4 us  [error_of(): return (weigh * (predicted - teacher[:, lo:hi].astype(F32))).astype(BF16)]
    pallas_call x19 -> x20, Pallas kernels: 96.9 us -> 97.6 us  [call(): kernel(*(table[n] for n, _ in at), *args, *after)]
  transfers between devices with their start and end apart: 23 -> 27, of which waited for: 14 -> 14; matrix products, arithmetic and copies ran while one was open for 3% -> 5% of each run, Pallas kernels for 48% -> 50%
where the time goes in v4:
time: 169 us; the launch traced here: 168 us
  Pallas kernels  97.6 us (58%)
  starting transfers between devices  29.8 us (18%)
  waiting for transfers between devices  25.8 us (15%)
  other arithmetic  8.54 us (5%)
  local copies, waits for them, and re-layouts  4.51 us (3%)
  between operations  1.7 us (1%)
    pallas_call x20, Pallas kernels, call(): kernel(*(table[n] for n, _ in at), *args, *after)  97.6 us
    ppermute x22, starting transfers between devices, swap(): return lax.ppermute(array, axis, [(i, i ^ 1 << bit) for i in range(size)])  24.8 us
    ppermute x22, waiting for transfers between devices, swap(): return lax.ppermute(array, axis, [(i, i ^ 1 << bit) for i in range(size)])  15.6 us
    ppermute x5, waiting for transfers between devices, shift(): lax.ppermute(array, 'head', [(i, (i + 2 * by) % size) for i in range(size)])  10.2 us
    ppermute x5, starting transfers between devices, shift(): lax.ppermute(array, 'head', [(i, (i + 2 * by) % size) for i in range(size)])  5.03 us
    convert_element_type x6, other arithmetic, scan_states(): other = beside(bit, [array.astype(BF16) for array in total])  4.93 us
  transfers between devices with their start and end apart: 27, of which 14 were waited for; matrix products, arithmetic and copies ran while one was open for 5% of the time, Pallas kernels for 50%

profile of v4, /device:TPU:0, one launch (start us, length us, event | category | flops | bytes accessed | tf_op | source)
XLA Modules:
  0.0 168.0 jit_solution(10324127303583315734)
XLA Ops:
  1.1 2.6 %shard_map.85 = (bf16[4,128,128]{2,1,0:T(8,128)(2,1)}, bf16[4,128,128]{2,1,0:T(8,128)(2,1)}) custom-call(s32[1]{0:T(128)} %bitcast.5.refs_0_.refs_1_, bf16[512,2048]{1,0:T(8,128)(2,1)} %refs_1_.21, bf16[512,2048]{1,0:T(8,128)(2,1)} %refs_2_.17), custom_call_target="tpu_custom_call" | custom-call | flops 1 | bytes 1 | tf_op jit(solution)/shard_map/pallas_call | solution.py:73
  3.8 2.6 %collective-permute-start.3 = (bf16[4,128,128]{2,1,0:T(8,128)(2,1)}, bf16[4,128,128]{2,1,0:T(8,128)(2,1)S(1)}, u32[]{:S(2)}, u32[]{:S(2)}) collective-permute-start(bf16[4,128,128]{2,1,0:T(8,128)(2,1)} %get-tuple-element.55.refs_3_), channel_id=1, source_target_pairs={{0,4},{4,0},{8,12},{12,8},{16,20},{20,16},{24,28},{28,24},{1,5},{5... | collective-permute-start | bytes 393224 | tf_op jit(solution)/shard_map/ppermute | solution.py:459
  6.4 2.6 %shard_map.86 = (bf16[4,128,128]{2,1,0:T(8,128)(2,1)}, bf16[4,128,128]{2,1,0:T(8,128)(2,1)}) custom-call(s32[1]{0:T(128)} %bitcast.refs_0_, bf16[512,2048]{1,0:T(8,128)(2,1)} %refs_1_.21, bf16[512,2048]{1,0:T(8,128)(2,1)} %refs_2_.17, bf16[4,128,128]{2,1,0:T(8,128)(2,1)} %get-tuple-element.55.refs_3_), custom_call_target="tpu_custom_call" | custom-call | flops 1 | bytes 1 | tf_op jit(solution)/shard_map/pallas_call | solution.py:73
  9.7 1.2 collective-permute-done.3
  11.8 2.1 %collective-permute-start.4 = (bf16[4,128,128]{2,1,0:T(8,128)(2,1)S(1)}, bf16[4,128,128]{2,1,0:T(8,128)(2,1)S(1)}, u32[]{:S(2)}, u32[]{:S(2)}) collective-permute-start(bf16[4,128,128]{2,1,0:T(8,128)(2,1)S(1)} %fusion.20), channel_id=1, source_target_pairs={{0,8},{4,12},{8,0},{12,4},{16,24},{20,28},{24,16},{28,20},{1,9},{5... | collective-permute-start | bytes 393224 | tf_op jit(solution)/shard_map/ppermute | solution.py:459
  14.9 1.4 collective-permute-start.1
  18.0 3.3 %collective-permute-start.5 = (bf16[4,128,128]{2,1,0:T(8,128)(2,1)S(1)}, bf16[4,128,128]{2,1,0:T(8,128)(2,1)S(1)}, u32[]{:S(2)}, u32[]{:S(2)}) collective-permute-start(bf16[4,128,128]{2,1,0:T(8,128)(2,1)S(1)} %fusion.17.refs_4_), channel_id=1, source_target_pairs={{0,16},{4,20},{8,24},{12,28},{16,0},{20,4},{24,8},{28,12},{1,17},{... | collective-permute-start | bytes 393224 | tf_op jit(solution)/shard_map/ppermute | solution.py:459
  21.9 1.6 collective-permute-start.6
  23.5 1.0 fusion.12
  24.9 4.6 %shard_map.87.refs_5_.refs_2_ = f32[512,1024]{1,0:T(8,128)} custom-call(s32[1]{0:T(128)} %bitcast.refs_0_, bf16[512,2048]{1,0:T(8,128)(2,1)} %refs_1_.19, bf16[512,2048]{1,0:T(8,128)(2,1)} %refs_1_.21, bf16[512,2048]{1,0:T(8,128)(2,1)} %refs_2_.17, bf16[4,128,128]{2,1,0:T(8,128)(2,1)} %copy-done.22), custom_call_target="tpu_custom_call" | custom-call | flops 1 | bytes 1 | tf_op jit(solution)/shard_map/pallas_call | solution.py:73
  29.5 1.6 collective-permute-start.8
  31.8 1.6 collective-permute-start.7
  33.4 4.7 %shard_map.88.refs_2_ = f32[512,1024]{1,0:T(8,128)} custom-call(s32[1]{0:T(128)} %bitcast.5.refs_0_.refs_1_, bf16[512,2048]{1,0:T(8,128)(2,1)} %refs_1_.19, bf16[512,2048]{1,0:T(8,128)(2,1)} %refs_1_.21, bf16[512,2048]{1,0:T(8,128)(2,1)} %refs_2_.17, bf16[4,128,128]{2,1,0:T(8,128)(2,1)} %copy-done.21, f32[512,1024]{1,0:T(8,128)} %shard_map.87.refs_5_.refs_2_), custom_call_target="tpu_custom_call" | custom-call | flops 1 | bytes 1 | tf_op jit(solution)/shard_map/pallas_call | solution.py:73
  38.8 2.1 %collective-permute-start.10 = (s32[8,128]{1,0:T(8,128)S(1)}, s32[8,128]{1,0:T(8,128)S(1)}, u32[]{:S(2)}, u32[]{:S(2)}) collective-permute-start(s32[8,128]{1,0:T(8,128)S(1)} %add.96), channel_id=1, source_target_pairs={{0,16},{4,20},{8,24},{12,28},{16,0},{20,4},{24,8},{28,12},{1,17},{... | collective-permute-start | bytes 12296 | tf_op jit(solution)/shard_map/ppermute | solution.py:459
  41.9 1.4 collective-permute-done.10
  43.3 1.7 shard_map.90.refs_5_
  45.0 3.0 %collective-permute-done.12.refs_6_ = bf16[512,1024]{1,0:T(8,128)(2,1)} collective-permute-done((bf16[512,1024]{1,0:T(8,128)(2,1)}, bf16[512,1024]{1,0:T(8,128)(2,1)}, u32[]{:S(2)}, u32[]{:S(2)}) %collective-permute-start.12) | collective-permute-done | bytes 1048608 | tf_op jit(solution)/shard_map/ppermute | solution.py:459
  48.0 5.8 %shard_map.91.refs_9_ = bf16[512,512]{1,0:T(8,128)(2,1)} custom-call(s32[1]{0:T(128)} %bitcast.refs_0_, s32[1]{0:T(128)} %bitcast.5.refs_0_.refs_1_, s32[1]{0:T(128)} %bitcast.1.refs_2_.refs_0_.refs_1_, bf16[512,1024]{1,0:T(8,128)(2,1)S(1)} %shard_map.89.refs_3_, bf16[512,1024]{1,0:T(8,128)(2,1)} %collective-permute-done.11.refs_4_, ...), custom_call_target="tpu_custom_call" | custom-call | flops 1 | bytes 1 | tf_op jit(solution)/shard_map/pallas_call | solution.py:73
  53.9 1.5 collective-permute-start.14
  55.4 5.1 %shard_map.92.refs_9_ = bf16[512,512]{1,0:T(8,128)(2,1)S(1)} custom-call(s32[1]{0:T(128)} %bitcast.refs_0_, s32[1]{0:T(128)} %bitcast.5.refs_0_.refs_1_, s32[1]{0:T(128)} %bitcast.3.refs_2_.refs_0_, bf16[512,1024]{1,0:T(8,128)(2,1)S(1)} %shard_map.89.refs_3_, bf16[512,1024]{1,0:T(8,128)(2,1)} %collective-permute-done.11.refs_4_, ...), custom_call_target="tpu_custom_call" | custom-call | flops 1 | bytes 1 | tf_op jit(solution)/shard_map/pallas_call | solution.py:73
  60.5 5.1 %shard_map.93.refs_9_ = bf16[512,512]{1,0:T(8,128)(2,1)S(1)} custom-call(s32[1]{0:T(128)} %bitcast.refs_0_, s32[1]{0:T(128)} %bitcast.5.refs_0_.refs_1_, s32[1]{0:T(128)} %bitcast.1.refs_2_.refs_0_.refs_1_, bf16[512,1024]{1,0:T(8,128)(2,1)S(1)} %shard_map.89.refs_3_, bf16[512,1024]{1,0:T(8,128)(2,1)} %collective-permute-done.11.refs_4_, ...), custom_call_target="tpu_custom_call" | custom-call | flops 1 | bytes 1 | tf_op jit(solution)/shard_map/pallas_call | solution.py:73
  68.1 3.7 %shard_map.94.refs_9_ = bf16[512,256]{1,0:T(8,128)(2,1)S(1)} custom-call(s32[1]{0:T(128)} %bitcast.refs_0_, s32[1]{0:T(128)} %bitcast.5.refs_0_.refs_1_, s32[1]{0:T(128)} %bitcast.1.refs_2_.refs_0_.refs_1_, bf16[512,1024]{1,0:T(8,128)(2,1)S(1)} %shard_map.89.refs_3_, bf16[512,1024]{1,0:T(8,128)(2,1)} %collective-permute-done.11.refs_4_, ...), custom_call_target="tpu_custom_call" | custom-call | flops 1 | bytes 1 | tf_op jit(solution)/shard_map/pallas_call | solution.py:73
  71.9 2.4 %collective-permute-start.16 = (bf16[512,256]{1,0:T(8,128)(2,1)S(1)}, bf16[512,256]{1,0:T(8,128)(2,1)S(1)}, u32[]{:S(2)}, u32[]{:S(2)}) collective-permute-start(bf16[512,256]{1,0:T(8,128)(2,1)S(1)} %shard_map.94.refs_9_), channel_id=1, source_target_pairs={{0,2},{1,3},{2,0},{3,1},{4,6},{5,7},{6,4},{7,5},{8,10},{9,11},{10,... | collective-permute-start | bytes 786440 | tf_op jit(solution)/shard_map/ppermute | solution.py:602
  74.2 6.5 %shard_map.95 = bf16[512,768]{1,0:T(8,128)(2,1)S(1)} custom-call(s32[1]{0:T(128)} %bitcast.refs_0_, s32[1]{0:T(128)} %bitcast.5.refs_0_.refs_1_, s32[1]{0:T(128)} %bitcast.3.refs_2_.refs_0_, bf16[512,1024]{1,0:T(8,128)(2,1)S(1)} %shard_map.89.refs_3_, bf16[512,1024]{1,0:T(8,128)(2,1)} %collective-permute-done.11.refs_4_, ...), custom_call_target="tpu_custom_call" | custom-call | flops 1 | bytes 1 | tf_op jit(solution)/shard_map/pallas_call | solution.py:73
  80.8 1.2 copy-done.16
  82.1 1.4 multiply_convert_fusion.refs_2_
  83.8 1.1 collective-permute-done.16
  85.0 1.0 multiply_convert_fusion.1.refs_3_
  86.1 2.1 %collective-permute-done.18.refs_6_ = bf16[512,512]{1,0:T(8,128)(2,1)} collective-permute-done((bf16[512,512]{1,0:T(8,128)(2,1)}, bf16[512,512]{1,0:T(8,128)(2,1)}, u32[]{:S(2)}, u32[]{:S(2)}) %collective-permute-start.18) | collective-permute-done | bytes 524320 | tf_op jit(solution)/shard_map/ppermute | solution.py:459
  88.2 10.1 %shard_map.96 = (f32[512,2048]{1,0:T(8,128)}, f32[8,128]{1,0:T(8,128)S(1)}) custom-call(s32[1]{0:T(128)} %bitcast.3.refs_2_.refs_0_, s32[1]{0:T(128)} %bitcast.4.refs_1_, bf16[512,768]{1,0:T(8,128)(2,1)S(1)} %multiply_convert_fusion.refs_2_, bf16[512,512]{1,0:T(8,128)(2,1)} %multiply_convert_fusion.1.refs_3_, bf16[2048,5120]{1,0:T(8,128)(2,1)} %refs_8_.3, ...), custom_call_target="tpu_custom_call" | custom-call | flops 1 | bytes 1 | tf_op jit(solution)/shard_map/pallas_call | solution.py:73
  98.4 5.2 %collective-permute-done.19.refs_3_ = bf16[512,768]{1,0:T(8,128)(2,1)} collective-permute-done((bf16[512,768]{1,0:T(8,128)(2,1)S(1)}, bf16[512,768]{1,0:T(8,128)(2,1)}, u32[]{:S(2)}, u32[]{:S(2)}) %collective-permute-start.19) | collective-permute-done | bytes 786464 | tf_op jit(solution)/shard_map/ppermute | solution.py:602
  103.9 2.4 %collective-permute-done.20.refs_5_ = bf16[512,768]{1,0:T(8,128)(2,1)} collective-permute-done((bf16[512,768]{1,0:T(8,128)(2,1)}, bf16[512,768]{1,0:T(8,128)(2,1)}, u32[]{:S(2)}, u32[]{:S(2)}) %collective-permute-start.20) | collective-permute-done | bytes 786464 | tf_op jit(solution)/shard_map/ppermute | solution.py:459
  106.2 8.9 %shard_map.97 = (f32[512,2048]{1,0:T(8,128)}, f32[8,128]{1,0:T(8,128)S(1)}) custom-call(s32[1]{0:T(128)} %bitcast.1.refs_2_.refs_0_.refs_1_, s32[1]{0:T(128)} %bitcast.2.refs_1_.refs_2_, f32[512,2048]{1,0:T(8,128)} %get-tuple-element.73.refs_2_, bf16[512,768]{1,0:T(8,128)(2,1)} %collective-permute-done.19.refs_3_, bf16[2048,5120]{1,0:T(8,128)(2,1)} %refs_8_.3, ...), custom_call_target="tpu_custom_call" | custom-call | flops 1 | bytes 1 | tf_op jit(solution)/shard_map/pallas_call | solution.py:73
  115.1 3.1 %collective-permute-done.21.refs_5_ = bf16[512,512]{1,0:T(8,128)(2,1)S(1)} collective-permute-done((bf16[512,512]{1,0:T(8,128)(2,1)}, bf16[512,512]{1,0:T(8,128)(2,1)S(1)}, u32[]{:S(2)}, u32[]{:S(2)}) %collective-permute-start.21) | collective-permute-done | bytes 524320 | tf_op jit(solution)/shard_map/ppermute | solution.py:602
  118.1 1.9 %collective-permute-done.22.refs_7_ = bf16[512,512]{1,0:T(8,128)(2,1)S(1)} collective-permute-done((bf16[512,512]{1,0:T(8,128)(2,1)S(1)}, bf16[512,512]{1,0:T(8,128)(2,1)S(1)}, u32[]{:S(2)}, u32[]{:S(2)}) %collective-permute-start.22) | collective-permute-done | bytes 524320 | tf_op jit(solution)/shard_map/ppermute | solution.py:459
  120.0 4.8 %shard_map.98 = (bf16[512,1024]{1,0:T(8,128)(2,1)}, bf16[8,128,128]{2,1,0:T(8,128)(2,1)S(1)}) custom-call(s32[1]{0:T(128)} %bitcast.5.refs_0_.refs_1_, s32[1]{0:T(128)} %bitcast.1.refs_2_.refs_0_.refs_1_, s32[1]{0:T(128)} %bitcast.2.refs_1_.refs_2_, f32[512,2048]{1,0:T(8,128)} %get-tuple-element.77.refs_3_, bf16[512,2048]{1,0:T(8,128)(2,1)S(1)} %copy-done, ...), custom_call_target="tpu_custom_call" | custom-call | flops 1 | bytes 1 | tf_op jit(solution)/shard_map/pallas_call | solution.py:73
  124.8 1.6 collective-permute-start.23
  126.4 4.8 %shard_map.99 = (bf16[512,1024]{1,0:T(8,128)(2,1)}, bf16[8,128,128]{2,1,0:T(8,128)(2,1)S(1)}) custom-call(s32[1]{0:T(128)} %bitcast.refs_0_, s32[1]{0:T(128)} %bitcast.1.refs_2_.refs_0_.refs_1_, s32[1]{0:T(128)} %bitcast.2.refs_1_.refs_2_, f32[512,2048]{1,0:T(8,128)} %get-tuple-element.77.refs_3_, bf16[512,2048]{1,0:T(8,128)(2,1)S(1)} %copy-done, ...), custom_call_target="tpu_custom_call" | custom-call | flops 1 | bytes 1 | tf_op jit(solution)/shard_map/pallas_call | solution.py:73
  131.3 2.0 %collective-permute-done.23 = bf16[8,128,128]{2,1,0:T(8,128)(2,1)S(1)} collective-permute-done((bf16[8,128,128]{2,1,0:T(8,128)(2,1)S(1)}, bf16[8,128,128]{2,1,0:T(8,128)(2,1)S(1)}, u32[]{:S(2)}, u32[]{:S(2)}) %collective-permute-start.23) | collective-permute-done | bytes 262176 | tf_op jit(solution)/shard_map/ppermute | solution.py:459
  134.2 7.0 %shard_map.100 = (f32[512,2048]{1,0:T(8,128)}, bf16[512,1024]{1,0:T(8,128)(2,1)}, bf16[512,1024]{1,0:T(8,128)(2,1)}, f32[8,128]{1,0:T(8,128)}) custom-call(s32[1]{0:T(128)} %bitcast.refs_0_, bf16[512,2048]{1,0:T(8,128)(2,1)} %refs_1_.19, bf16[512,2048]{1,0:T(8,128)(2,1)} %refs_1_.21, bf16[512,2048]{1,0:T(8,128)(2,1)} %refs_2_.17, ...), custom_call_target="tpu_custom_call" | custom-call | flops 1 | bytes 1 | tf_op jit(solution)/shard_map/pallas_call | solution.py:73
  141.2 1.1 fusion.4.refs_7_
  142.2 3.0 %collective-permute-start.25 = (bf16[8,128,128]{2,1,0:T(8,128)(2,1)S(1)}, bf16[8,128,128]{2,1,0:T(8,128)(2,1)S(1)}, u32[]{:S(2)}, u32[]{:S(2)}) collective-permute-start(bf16[8,128,128]{2,1,0:T(8,128)(2,1)S(1)} %fusion.4.refs_7_), channel_id=1, source_target_pairs={{0,16},{4,20},{8,24},{12,28},{16,0},{20,4},{24,8},{28,12},{1,17},{... | collective-permute-start | bytes 786440 | tf_op jit(solution)/shard_map/ppermute | solution.py:459
  145.2 8.5 %shard_map.101 = (f32[512,2048]{1,0:T(8,128)}, bf16[512,1024]{1,0:T(8,128)(2,1)}, bf16[512,1024]{1,0:T(8,128)(2,1)}, f32[8,128]{1,0:T(8,128)}) custom-call(s32[1]{0:T(128)} %bitcast.5.refs_0_.refs_1_, bf16[512,2048]{1,0:T(8,128)(2,1)} %refs_1_.19, bf16[512,2048]{1,0:T(8,128)(2,1)} %refs_1_.21, ...), custom_call_target="tpu_custom_call", output_to_operand_aliasing={{0}: (6, {})} | custom-call | flops 1 | bytes 1 | tf_op jit(solution)/shard_map/pallas_call | solution.py:73
  153.8 3.7 %shard_map.102 = (f32[512,2048]{1,0:T(8,128)}, bf16[512,1024]{1,0:T(8,128)(2,1)}, bf16[512,1024]{1,0:T(8,128)(2,1)}, f32[8,128]{1,0:T(8,128)}) custom-call(s32[1]{0:T(128)} %bitcast.refs_0_, bf16[512,2048]{1,0:T(8,128)(2,1)} %refs_1_.19, bf16[512,2048]{1,0:T(8,128)(2,1)} %refs_1_.21, ...), custom_call_target="tpu_custom_call", output_to_operand_aliasing={{0}: (6, {}), {1}: (7, {}), {2}: (8, {})} | custom-call | flops 1 | bytes 1 | tf_op jit(solution)/shard_map/pallas_call | solution.py:73
  157.7 1.5 collective-permute-start.26
  159.3 1.2 copy-done.7
  161.2 3.2 %shard_map.103 = (f32[512,2048]{1,0:T(8,128)}, f32[512,2048]{1,0:T(8,128)}) custom-call(s32[1]{0:T(128)} %bitcast.refs_0_, bf16[512,2048]{1,0:T(8,128)(2,1)S(1)} %copy-done.1, bf16[512,2048]{1,0:T(8,128)(2,1)S(1)} %copy-done.2, bf16[8,128,128]{2,1,0:T(8,128)(2,1)S(1)} %get-tuple-element.107.refs_3_.refs_7_, bf16[512,1024]{1,0:T(8,128)(2,1)S(1)} %copy-done.6, ...), custom_call_target="tpu_custom_call" | custom-call | flops 1 | bytes 1 | tf_op jit(solution)/shard_map/pallas_call | solution.py:73
  164.8 3.2 %shard_map.104 = (f32[512,2048]{1,0:T(8,128)}, f32[512,2048]{1,0:T(8,128)}) custom-call(s32[1]{0:T(128)} %bitcast.5.refs_0_.refs_1_, bf16[512,2048]{1,0:T(8,128)(2,1)S(1)} %copy-done.1, bf16[512,2048]{1,0:T(8,128)(2,1)S(1)} %copy-done.2, bf16[8,128,128]{2,1,0:T(8,128)(2,1)S(1)} %collective-permute-done.26.refs_3_, ...), custom_call_target="tpu_custom_call", output_to_operand_aliasing={{0}: (6, {}), {1}: (7, {})} | custom-call | flops 1 | bytes 1 | tf_op jit(solution)/shard_map/pallas_call | solution.py:73
  (97 shorter events, 13.3 us)
Async XLA Ops:
  0.6 47.4 %collective-permute-start.13 = (bf16[2048,5120]{1,0:T(8,128)(2,1)}, bf16[2048,5120]{1,0:T(8,128)(2,1)}, u32[]{:S(2)}, u32[]{:S(2)}) collective-permute-start(bf16[2048,5120]{1,0:T(8,128)(2,1)} %refs_8_.3), channel_id=1, source_target_pairs={{0,1},{1,0},{2,3},{3,2},{4,5},{5,4},{6,7},{7,6},{8,9},{9,8},{10,11... | collective-permute-start | bytes 62914568 | tf_op jit(solution)/shard_map/ppermute | solution.py:459
  3.8 7.1 %collective-permute-start.3 = (bf16[4,128,128]{2,1,0:T(8,128)(2,1)}, bf16[4,128,128]{2,1,0:T(8,128)(2,1)S(1)}, u32[]{:S(2)}, u32[]{:S(2)}) collective-permute-start(bf16[4,128,128]{2,1,0:T(8,128)(2,1)} %get-tuple-element.55.refs_3_), channel_id=1, source_target_pairs={{0,4},{4,0},{8,12},{12,8},{16,20},{20,16},{24,28},{28,24},{1,5},{5... | collective-permute-start | bytes 393224 | tf_op jit(solution)/shard_map/ppermute | solution.py:459
  6.3 7.6 %collective-permute-start = (bf16[4,128,128]{2,1,0:T(8,128)(2,1)}, bf16[4,128,128]{2,1,0:T(8,128)(2,1)S(1)}, u32[]{:S(2)}, u32[]{:S(2)}) collective-permute-start(bf16[4,128,128]{2,1,0:T(8,128)(2,1)} %get-tuple-element.57), channel_id=1, source_target_pairs={{0,4},{4,0},{8,12},{12,8},{16,20},{20,16},{24,28},{28,24},{1,5},{5... | collective-permute-start | bytes 393224 | tf_op jit(solution)/shard_map/ppermute | solution.py:459
  6.4 2.6 %copy-start.23 = (s32[512]{0:T(512)S(1)}, s32[512]{0:T(512)}, u32[]{:S(2)}) copy-start(s32[512]{0:T(512)} %param.11) | copy-start | bytes 6148
  11.8 5.1 %collective-permute-start.4 = (bf16[4,128,128]{2,1,0:T(8,128)(2,1)S(1)}, bf16[4,128,128]{2,1,0:T(8,128)(2,1)S(1)}, u32[]{:S(2)}, u32[]{:S(2)}) collective-permute-start(bf16[4,128,128]{2,1,0:T(8,128)(2,1)S(1)} %fusion.20), channel_id=1, source_target_pairs={{0,8},{4,12},{8,0},{12,4},{16,24},{20,28},{24,16},{28,20},{1,9},{5... | collective-permute-start | bytes 393224 | tf_op jit(solution)/shard_map/ppermute | solution.py:459
  14.9 8.7 %collective-permute-start.1 = (bf16[4,128,128]{2,1,0:T(8,128)(2,1)S(1)}, bf16[4,128,128]{2,1,0:T(8,128)(2,1)S(1)}, u32[]{:S(2)}, u32[]{:S(2)}) collective-permute-start(bf16[4,128,128]{2,1,0:T(8,128)(2,1)S(1)} %fusion.19), channel_id=1, source_target_pairs={{0,8},{4,12},{8,0},{12,4},{16,24},{20,28},{24,16},{28,20},{1,9},{5... | collective-permute-start | bytes 393224 | tf_op jit(solution)/shard_map/ppermute | solution.py:459
  18.0 7.0 %copy-start.22 = (bf16[4,128,128]{2,1,0:T(8,128)(2,1)}, bf16[4,128,128]{2,1,0:T(8,128)(2,1)S(1)}, u32[]{:S(2)}) copy-start(bf16[4,128,128]{2,1,0:T(8,128)(2,1)S(1)} %fusion.17.refs_4_) | copy-start | bytes 393220
  18.0 13.1 %collective-permute-start.5 = (bf16[4,128,128]{2,1,0:T(8,128)(2,1)S(1)}, bf16[4,128,128]{2,1,0:T(8,128)(2,1)S(1)}, u32[]{:S(2)}, u32[]{:S(2)}) collective-permute-start(bf16[4,128,128]{2,1,0:T(8,128)(2,1)S(1)} %fusion.17.refs_4_), channel_id=1, source_target_pairs={{0,16},{4,20},{8,24},{12,28},{16,0},{20,4},{24,8},{28,12},{1,17},{... | collective-permute-start | bytes 393224 | tf_op jit(solution)/shard_map/ppermute | solution.py:459
  21.9 7.6 %collective-permute-start.6 = (s32[8,128]{1,0:T(8,128)S(1)}, s32[8,128]{1,0:T(8,128)S(1)}, u32[]{:S(2)}, u32[]{:S(2)}) collective-permute-start(s32[8,128]{1,0:T(8,128)S(1)} %broadcast_in_dim.49), channel_id=1, source_target_pairs={{0,4},{4,0},{8,12},{12,8},{16,20},{20,16},{24,28},{28,24},{1,5},{5... | collective-permute-start | bytes 12296 | tf_op jit(solution)/shard_map/ppermute | solution.py:459
  24.5 6.6 %copy-start.18 = (bf16[4,128,128]{2,1,0:T(8,128)(2,1)S(1)}, bf16[4,128,128]{2,1,0:T(8,128)(2,1)}, u32[]{:S(2)}) copy-start(bf16[4,128,128]{2,1,0:T(8,128)(2,1)} %get-tuple-element.58) | copy-start | bytes 393220
  24.5 7.3 %collective-permute-start.2 = (bf16[4,128,128]{2,1,0:T(8,128)(2,1)S(1)}, bf16[4,128,128]{2,1,0:T(8,128)(2,1)S(1)}, u32[]{:S(2)}, u32[]{:S(2)}) collective-permute-start(bf16[4,128,128]{2,1,0:T(8,128)(2,1)S(1)} %fusion.12), channel_id=1, source_target_pairs={{0,16},{4,20},{8,24},{12,28},{16,0},{20,4},{24,8},{28,12},{1,17},{... | collective-permute-start | bytes 393224 | tf_op jit(solution)/shard_map/ppermute | solution.py:459
  29.5 8.6 %collective-permute-start.8 = (s32[8,128]{1,0:T(8,128)S(1)}, s32[8,128]{1,0:T(8,128)S(1)}, u32[]{:S(2)}, u32[]{:S(2)}) collective-permute-start(s32[8,128]{1,0:T(8,128)S(1)} %add.95), channel_id=1, source_target_pairs={{0,8},{4,12},{8,0},{12,4},{16,24},{20,28},{24,16},{28,20},{1,9},{5... | collective-permute-start | bytes 12296 | tf_op jit(solution)/shard_map/ppermute | solution.py:459
  31.2 2.2 %copy-start.21 = (bf16[4,128,128]{2,1,0:T(8,128)(2,1)}, bf16[4,128,128]{2,1,0:T(8,128)(2,1)S(1)}, u32[]{:S(2)}) copy-start(bf16[4,128,128]{2,1,0:T(8,128)(2,1)S(1)} %get-tuple-element.113.refs_4_) | copy-start | bytes 393220
  31.8 6.3 %copy-start.17 = (bf16[4,128,128]{2,1,0:T(8,128)(2,1)S(1)}, bf16[4,128,128]{2,1,0:T(8,128)(2,1)}, u32[]{:S(2)}) copy-start(bf16[4,128,128]{2,1,0:T(8,128)(2,1)} %get-tuple-element.56) | copy-start | bytes 393220
  31.8 6.4 %collective-permute-start.7 = (bf16[4,128,128]{2,1,0:T(8,128)(2,1)S(1)}, bf16[4,128,128]{2,1,0:T(8,128)(2,1)S(1)}, u32[]{:S(2)}, u32[]{:S(2)}) collective-permute-start(bf16[4,128,128]{2,1,0:T(8,128)(2,1)S(1)} %get-tuple-element.113.refs_4_), channel_id=1, source_target_pairs={{0,4},{4,0},{8,12},{12,8},{16,20},{20,16},{24,28},{28,24},{1,5},{5... | collective-permute-start | bytes 393224 | tf_op jit(solution)/shard_map/ppermute | solution.py:459
  33.4 7.5 %copy-start = (bf16[512,2048]{1,0:T(8,128)(2,1)S(1)}, bf16[512,2048]{1,0:T(8,128)(2,1)}, u32[]{:S(2)}) copy-start(bf16[512,2048]{1,0:T(8,128)(2,1)} %refs_1_.19) | copy-start | bytes 6291460
  33.4 7.5 %copy-start.3 = (f32[512,1024]{1,0:T(8,128)S(1)}, f32[512,1024]{1,0:T(8,128)}, u32[]{:S(2)}) copy-start(f32[512,1024]{1,0:T(8,128)} %shard_map.87.refs_5_.refs_2_) | copy-start | bytes 6291460
  38.3 5.1 %collective-permute-start.9 = (bf16[4,128,128]{2,1,0:T(8,128)(2,1)S(1)}, bf16[4,128,128]{2,1,0:T(8,128)(2,1)S(1)}, u32[]{:S(2)}, u32[]{:S(2)}) collective-permute-start(bf16[4,128,128]{2,1,0:T(8,128)(2,1)S(1)} %get-tuple-element.68), channel_id=1, source_target_pairs={{0,4},{4,0},{8,12},{12,8},{16,20},{20,16},{24,28},{28,24},{1,5},{5... | collective-permute-start | bytes 393224 | tf_op jit(solution)/shard_map/ppermute | solution.py:459
  38.8 4.5 %collective-permute-start.10 = (s32[8,128]{1,0:T(8,128)S(1)}, s32[8,128]{1,0:T(8,128)S(1)}, u32[]{:S(2)}, u32[]{:S(2)}) collective-permute-start(s32[8,128]{1,0:T(8,128)S(1)} %add.96), channel_id=1, source_target_pairs={{0,16},{4,20},{8,24},{12,28},{16,0},{20,4},{24,8},{28,12},{1,17},{... | collective-permute-start | bytes 12296 | tf_op jit(solution)/shard_map/ppermute | solution.py:459
  40.9 2.4 %copy-start.4 = (f32[512,1024]{1,0:T(8,128)S(1)}, f32[512,1024]{1,0:T(8,128)}, u32[]{:S(2)}) copy-start(f32[512,1024]{1,0:T(8,128)} %shard_map.88.refs_2_) | copy-start | bytes 6291460
  41.8 3.2 %collective-permute-start.11 = (bf16[512,1024]{1,0:T(8,128)(2,1)S(1)}, bf16[512,1024]{1,0:T(8,128)(2,1)}, u32[]{:S(2)}, u32[]{:S(2)}) collective-permute-start(bf16[512,1024]{1,0:T(8,128)(2,1)S(1)} %shard_map.89.refs_3_), channel_id=1, source_target_pairs={{0,1},{1,0},{2,3},{3,2},{4,5},{5,4},{6,7},{7,6},{8,9},{9,8},{10,11... | collective-permute-start | bytes 3145736 | tf_op jit(solution)/shard_map/ppermute | solution.py:459
  43.3 1.7 copy-start.13
  45.0 3.0 %collective-permute-start.12 = (bf16[512,1024]{1,0:T(8,128)(2,1)}, bf16[512,1024]{1,0:T(8,128)(2,1)}, u32[]{:S(2)}, u32[]{:S(2)}) collective-permute-start(bf16[512,1024]{1,0:T(8,128)(2,1)} %shard_map.90.refs_5_), channel_id=1, source_target_pairs={{0,1},{1,0},{2,3},{3,2},{4,5},{5,4},{6,7},{7,6},{8,9},{9,8},{10,11... | collective-permute-start | bytes 3145736 | tf_op jit(solution)/shard_map/ppermute | solution.py:459
  53.9 14.3 %collective-permute-start.14 = (bf16[512,512]{1,0:T(8,128)(2,1)}, bf16[512,512]{1,0:T(8,128)(2,1)}, u32[]{:S(2)}, u32[]{:S(2)}) collective-permute-start(bf16[512,512]{1,0:T(8,128)(2,1)} %shard_map.91.refs_9_), channel_id=1, source_target_pairs={{0,2},{1,3},{2,0},{3,1},{4,6},{5,7},{6,4},{7,5},{8,10},{9,11},{10,... | collective-permute-start | bytes 1572872 | tf_op jit(solution)/shard_map/ppermute | solution.py:602
  65.6 15.2 %collective-permute-start.15 = (bf16[512,512]{1,0:T(8,128)(2,1)S(1)}, bf16[512,512]{1,0:T(8,128)(2,1)S(1)}, u32[]{:S(2)}, u32[]{:S(2)}) collective-permute-start(bf16[512,512]{1,0:T(8,128)(2,1)S(1)} %shard_map.93.refs_9_), channel_id=1, source_target_pairs={{0,2},{1,3},{2,0},{3,1},{4,6},{5,7},{6,4},{7,5},{8,10},{9,11},{10,... | collective-permute-start | bytes 1572872 | tf_op jit(solution)/shard_map/ppermute | solution.py:602
  71.9 13.1 %collective-permute-start.16 = (bf16[512,256]{1,0:T(8,128)(2,1)S(1)}, bf16[512,256]{1,0:T(8,128)(2,1)S(1)}, u32[]{:S(2)}, u32[]{:S(2)}) collective-permute-start(bf16[512,256]{1,0:T(8,128)(2,1)S(1)} %shard_map.94.refs_9_), channel_id=1, source_target_pairs={{0,2},{1,3},{2,0},{3,1},{4,6},{5,7},{6,4},{7,5},{8,10},{9,11},{10,... | collective-permute-start | bytes 786440 | tf_op jit(solution)/shard_map/ppermute | solution.py:602
  80.7 1.3 copy-start.16
  83.4 2.6 %copy-start.14 = (bf16[4,128,128]{2,1,0:T(8,128)(2,1)S(1)}, bf16[4,128,128]{2,1,0:T(8,128)(2,1)}, u32[]{:S(2)}) copy-start(bf16[4,128,128]{2,1,0:T(8,128)(2,1)} %copy-done.13) | copy-start | bytes 393220
  83.4 2.6 %collective-permute-start.17 = (bf16[512,768]{1,0:T(8,128)(2,1)S(1)}, bf16[512,768]{1,0:T(8,128)(2,1)}, u32[]{:S(2)}, u32[]{:S(2)}) collective-permute-start(bf16[512,768]{1,0:T(8,128)(2,1)S(1)} %multiply_convert_fusion.refs_2_), channel_id=1, source_target_pairs={{0,1},{1,0},{2,3},{3,2},{4,5},{5,4},{6,7},{7,6},{8,9},{9,8},{10,11... | collective-permute-start | bytes 2359304 | tf_op jit(solution)/shard_map/ppermute | solution.py:459
  83.5 20.1 %collective-permute-start.19 = (bf16[512,768]{1,0:T(8,128)(2,1)S(1)}, bf16[512,768]{1,0:T(8,128)(2,1)}, u32[]{:S(2)}, u32[]{:S(2)}) collective-permute-start(bf16[512,768]{1,0:T(8,128)(2,1)S(1)} %multiply_convert_fusion.refs_2_), channel_id=1, source_target_pairs={{0,2},{1,3},{2,0},{3,1},{4,6},{5,7},{6,4},{7,5},{8,10},{9,11},{10,... | collective-permute-start | bytes 2359304 | tf_op jit(solution)/shard_map/ppermute | solution.py:602
  86.0 2.3 %collective-permute-start.18 = (bf16[512,512]{1,0:T(8,128)(2,1)}, bf16[512,512]{1,0:T(8,128)(2,1)}, u32[]{:S(2)}, u32[]{:S(2)}) collective-permute-start(bf16[512,512]{1,0:T(8,128)(2,1)} %multiply_convert_fusion.1.refs_3_), channel_id=1, source_target_pairs={{0,1},{1,0},{2,3},{3,2},{4,5},{5,4},{6,7},{7,6},{8,9},{9,8},{10,11... | collective-permute-start | bytes 1572872 | tf_op jit(solution)/shard_map/ppermute | solution.py:459
  86.0 12.3 %copy-start.5 = (bf16[8,128,128]{2,1,0:T(8,128)(2,1)}, bf16[8,128,128]{2,1,0:T(8,128)(2,1)S(1)}, u32[]{:S(2)}) copy-start(bf16[8,128,128]{2,1,0:T(8,128)(2,1)S(1)} %pad_maximum_fusion.refs_9_.refs_5_) | copy-start | bytes 786436
  86.1 12.3 %copy-start.10 = (bf16[8,128,128]{2,1,0:T(8,128)(2,1)}, bf16[8,128,128]{2,1,0:T(8,128)(2,1)S(1)}, u32[]{:S(2)}) copy-start(bf16[8,128,128]{2,1,0:T(8,128)(2,1)S(1)} %constant_dynamic-update-slice_fusion.refs_8_.refs_5_) | copy-start | bytes 786436
  103.6 2.6 %collective-permute-start.20 = (bf16[512,768]{1,0:T(8,128)(2,1)}, bf16[512,768]{1,0:T(8,128)(2,1)}, u32[]{:S(2)}, u32[]{:S(2)}) collective-permute-start(bf16[512,768]{1,0:T(8,128)(2,1)} %collective-permute-done.19.refs_3_), channel_id=1, source_target_pairs={{0,1},{1,0},{2,3},{3,2},{4,5},{5,4},{6,7},{7,6},{8,9},{9,8},{10,11... | collective-permute-start | bytes 2359304 | tf_op jit(solution)/shard_map/ppermute | solution.py:459
  103.6 14.5 %collective-permute-start.21 = (bf16[512,512]{1,0:T(8,128)(2,1)}, bf16[512,512]{1,0:T(8,128)(2,1)S(1)}, u32[]{:S(2)}, u32[]{:S(2)}) collective-permute-start(bf16[512,512]{1,0:T(8,128)(2,1)} %multiply_convert_fusion.1.refs_3_), channel_id=1, source_target_pairs={{0,2},{1,3},{2,0},{3,1},{4,6},{5,7},{6,4},{7,5},{8,10},{9,11},{10,... | collective-permute-start | bytes 1572872 | tf_op jit(solution)/shard_map/ppermute | solution.py:602
  118.1 1.9 %collective-permute-start.22 = (bf16[512,512]{1,0:T(8,128)(2,1)S(1)}, bf16[512,512]{1,0:T(8,128)(2,1)S(1)}, u32[]{:S(2)}, u32[]{:S(2)}) collective-permute-start(bf16[512,512]{1,0:T(8,128)(2,1)S(1)} %collective-permute-done.21.refs_5_), channel_id=1, source_target_pairs={{0,1},{1,0},{2,3},{3,2},{4,5},{5,4},{6,7},{7,6},{8,9},{9,8},{10,11... | collective-permute-start | bytes 1572872 | tf_op jit(solution)/shard_map/ppermute | solution.py:459
  124.8 8.4 %collective-permute-start.23 = (bf16[8,128,128]{2,1,0:T(8,128)(2,1)S(1)}, bf16[8,128,128]{2,1,0:T(8,128)(2,1)S(1)}, u32[]{:S(2)}, u32[]{:S(2)}) collective-permute-start(bf16[8,128,128]{2,1,0:T(8,128)(2,1)S(1)} %get-tuple-element.81.refs_9_), channel_id=1, source_target_pairs={{0,4},{4,0},{8,12},{12,8},{16,20},{20,16},{24,28},{28,24},{1,5},{5... | collective-permute-start | bytes 786440 | tf_op jit(solution)/shard_map/ppermute | solution.py:459
  131.2 3.0 %copy-start.8 = (bf16[8,128,128]{2,1,0:T(8,128)(2,1)}, bf16[8,128,128]{2,1,0:T(8,128)(2,1)S(1)}, u32[]{:S(2)}) copy-start(bf16[8,128,128]{2,1,0:T(8,128)(2,1)S(1)} %get-tuple-element.86.refs_7_) | copy-start | bytes 786436
  133.3 7.9 %collective-permute-start.24 = (bf16[8,128,128]{2,1,0:T(8,128)(2,1)S(1)}, bf16[8,128,128]{2,1,0:T(8,128)(2,1)S(1)}, u32[]{:S(2)}, u32[]{:S(2)}) collective-permute-start(bf16[8,128,128]{2,1,0:T(8,128)(2,1)S(1)} %fusion.6.refs_6_), channel_id=1, source_target_pairs={{0,8},{4,12},{8,0},{12,4},{16,24},{20,28},{24,16},{28,20},{1,9},{5... | collective-permute-start | bytes 786440 | tf_op jit(solution)/shard_map/ppermute | solution.py:459
  142.2 3.0 %copy-start.20 = (bf16[8,128,128]{2,1,0:T(8,128)(2,1)}, bf16[8,128,128]{2,1,0:T(8,128)(2,1)S(1)}, u32[]{:S(2)}) copy-start(bf16[8,128,128]{2,1,0:T(8,128)(2,1)S(1)} %fusion.4.refs_7_) | copy-start | bytes 786436
  142.2 15.2 %collective-permute-start.25 = (bf16[8,128,128]{2,1,0:T(8,128)(2,1)S(1)}, bf16[8,128,128]{2,1,0:T(8,128)(2,1)S(1)}, u32[]{:S(2)}, u32[]{:S(2)}) collective-permute-start(bf16[8,128,128]{2,1,0:T(8,128)(2,1)S(1)} %fusion.4.refs_7_), channel_id=1, source_target_pairs={{0,16},{4,20},{8,24},{12,28},{16,0},{20,4},{24,8},{28,12},{1,17},{... | collective-permute-start | bytes 786440 | tf_op jit(solution)/shard_map/ppermute | solution.py:459
  153.8 3.7 %copy-start.9 = (bf16[8,128,128]{2,1,0:T(8,128)(2,1)S(1)}, bf16[8,128,128]{2,1,0:T(8,128)(2,1)}, u32[]{:S(2)}) copy-start(bf16[8,128,128]{2,1,0:T(8,128)(2,1)} %copy-done.8) | copy-start | bytes 786436
  153.8 5.5 %copy-start.1 = (bf16[512,2048]{1,0:T(8,128)(2,1)S(1)}, bf16[512,2048]{1,0:T(8,128)(2,1)}, u32[]{:S(2)}) copy-start(bf16[512,2048]{1,0:T(8,128)(2,1)} %refs_1_.21) | copy-start | bytes 6291460
  153.8 5.5 %copy-start.2 = (bf16[512,2048]{1,0:T(8,128)(2,1)S(1)}, bf16[512,2048]{1,0:T(8,128)(2,1)}, u32[]{:S(2)}) copy-start(bf16[512,2048]{1,0:T(8,128)(2,1)} %refs_2_.17) | copy-start | bytes 6291460
  157.5 1.8 %copy-start.6 = (bf16[512,1024]{1,0:T(8,128)(2,1)S(1)}, bf16[512,1024]{1,0:T(8,128)(2,1)}, u32[]{:S(2)}) copy-start(bf16[512,1024]{1,0:T(8,128)(2,1)} %get-tuple-element.100.refs_4_) | copy-start | bytes 3145732
  157.7 7.0 %collective-permute-start.26 = (bf16[8,128,128]{2,1,0:T(8,128)(2,1)S(1)}, bf16[8,128,128]{2,1,0:T(8,128)(2,1)S(1)}, u32[]{:S(2)}, u32[]{:S(2)}) collective-permute-start(bf16[8,128,128]{2,1,0:T(8,128)(2,1)S(1)} %get-tuple-element.108), channel_id=1, source_target_pairs={{0,4},{4,0},{8,12},{12,8},{16,20},{20,16},{24,28},{28,24},{1,5},{5... | collective-permute-start | bytes 786440 | tf_op jit(solution)/shard_map/ppermute | solution.py:459
  161.2 3.6 %copy-start.11 = (bf16[512,1024]{1,0:T(8,128)(2,1)S(1)}, bf16[512,1024]{1,0:T(8,128)(2,1)}, u32[]{:S(2)}) copy-start(bf16[512,1024]{1,0:T(8,128)(2,1)} %get-tuple-element.98.refs_4_) | copy-start | bytes 3145732
  161.2 3.6 %copy-start.12 = (bf16[512,1024]{1,0:T(8,128)(2,1)S(1)}, bf16[512,1024]{1,0:T(8,128)(2,1)}, u32[]{:S(2)}) copy-start(bf16[512,1024]{1,0:T(8,128)(2,1)} %get-tuple-element.99.refs_5_) | copy-start | bytes 3145732
  (3 other events, 2.8 us)

commit v5 on v4

--- a/solution.py
+++ b/solution.py
@@ -73,6 +73,10 @@
     return lambda table, *args: kernel(*(table[n] for n, _ in at), *args, *after)
 
 
+def in_hbm(array):
+    return pltpu.with_memory_space_constraint(array, pltpu.HBM)
+
+
 def sds(shape, dtype):
     return jax.ShapeDtypeStruct(shape, dtype)
 
@@ -113,8 +117,8 @@
         2 * rows * DH * DH * heads * chunks,
         rows * DH * heads * chunks * 4,
         after=after,
-        vmem=58,
-    )(table, k, v)
+        vmem=30,
+    )(table, in_hbm(k), in_hbm(v))
 
 
 def intra_body(group, block, idx, q, k, v, out):
@@ -147,13 +151,14 @@
         at,
         (steps,),
         [blk, blk, blk],
-        pl.BlockSpec((rows, group * DH), lambda i, s: (0, i)),
-        sds((rows, half_heads * DH), F32),
+        [pl.BlockSpec((rows, group * DH), lambda i, s: (0, i))],
+        [pltpu.HBM((rows, half_heads * DH), F32)],
         4 * rows * (block + DH) * DH * half_heads,
         rows * DH * half_heads * 10,
         after=after,
-        vmem=58,
-    )(table, q, k, v)
+        vmem=30,
+        token=True,
+    )(table, in_hbm(q), in_hbm(k), in_hbm(v))
 
 
 def attn_body(heads, scale, idx, q, part, *refs):
@@ -167,7 +172,7 @@
                 out[:, c] = (scale * (part[:, c] + dot(q[:, c], state[i]))).astype(BF16)
 
 
-def attend(table, at, scale, q, part, states):
+def attend(table, at, scale, q, part, states, after=()):
     rows = q.shape[0]
     chunks, heads = len(states), states[0].shape[0]
     blk = pl.BlockSpec((rows, heads * DH), lambda i, s: (0, i))
@@ -184,6 +189,7 @@
         sds((rows, chunks * heads * DH), BF16),
         2 * rows * DH * DH * heads * chunks,
         rows * DH * heads * chunks * 8,
+        after=after,
     )(table, q, part, *states)
 
 
@@ -250,7 +256,7 @@
     in_specs, args = [], []
     if acc is not None:
         in_specs.append(pl.BlockSpec((rows, row_tile), lambda i, s: (0, i)))
-        args.append(pltpu.with_memory_space_constraint(acc, pltpu.HBM))
+        args.append(in_hbm(acc))
     total = 0
     for g, pieces in enumerate(groups):
         span = sum(piece.shape[1] for piece in pieces)
@@ -318,7 +324,7 @@
     wide = group * DH
     mine = pl.BlockSpec((rows, wide), lambda i, s: (0, s[0] * steps + i))
     in_specs, total = [pl.BlockSpec(memory_space=pltpu.HBM), mine], 0
-    args = [pltpu.with_memory_space_constraint(acc, pltpu.HBM), q]
+    args = [in_hbm(acc), q]
     for n, pieces in enumerate(groups):
         span = sum(piece.shape[1] for piece in pieces)
         total += span
@@ -395,7 +401,7 @@
     mine = pl.BlockSpec((rows, wide), lambda i, s: (0, s[0] * (half_heads // group) + first + i))
     own = pl.BlockSpec((rows, wide), lambda i, s: (0, first + i))
     extra = len(filled)
-    half = sds((rows, half_heads * DH), BF16)
+    half = pltpu.HBM((rows, half_heads * DH), BF16)
     return call(
         functools.partial(back_body, group, block, scale, extra),
         at,
@@ -409,14 +415,14 @@
         ]
         + [pl.BlockSpec(memory_space=pl.ANY)] * extra,
         [mine, own, own],
-        [sds((rows, width), F32), half, half],
+        [pltpu.HBM((rows, width), F32), half, half],
         2 * rows * DH * (5 * block + 4 * DH) * heads,
         rows * DH * heads * 20,
         {6 + n: n for n in range(extra)},
         after=after,
-        vmem=58,
+        vmem=30,
         token=True,
-    )(table, q, k, v, g, state, *filled)
+    )(table, in_hbm(q), in_hbm(k), in_hbm(v), in_hbm(g), state, *filled)
 
 
 def later_body(heads, scale, extra, idx, k, v, later, dk_in, dv_in, *refs):
@@ -429,7 +435,7 @@
 
 def add_later(table, at, scale, k, v, later, dk, dv, filled, half_heads, after):
     rows, width = k.shape
-    block = math.gcd(rows, 128)
+    block = math.gcd(rows, 256)
     wide = half_heads * DH
     mine = pl.BlockSpec((block, wide), lambda i, s: (i, s[0]))
     own = pl.BlockSpec((block, wide), lambda i, s: (i, 0))
@@ -544,8 +550,10 @@
 
     def intra_of(name, half):
         def run(after):
-            parts[name] = intra(table, [half], queries, keys, values, half_heads, after)
-            return [parts[name]]
+            parts[name], token = intra(
+                table, [half], queries, keys, values, half_heads, after
+            )
+            return [token]
 
         return run
 
@@ -574,7 +582,7 @@
         fill = {(last_step, 0): first_fill, (ctx_bits, 0): last_fill}
     else:
         fill = {(last_step, 0): last_fill}
-    before_mine, before_theirs, (*_, count) = scan_states(
+    before_mine, before_theirs, (*held, count) = scan_states(
         kv_theirs, kv_mine, ctx_bits, False, fill
     )
     count = count + swap(count, "ctx", last_step)
@@ -588,7 +596,7 @@
         attend(table, [mine_ix], scale, queries, parts["mine"], before_mine)
     )
     attn_theirs = both_cores(
-        attend(table, [theirs_ix], scale, queries, parts["theirs"], before_theirs)
+        attend(table, [theirs_ix], scale, queries, parts["theirs"], before_theirs, held)
     )
 
     def terms(by, lo, hi, after=()):

time: 169 us -> 164 us (0.970)
  other arithmetic: 8.54 us -> 3.92 us
  waiting for transfers between devices: 25.8 us -> 28.8 us
  Pallas kernels: 97.6 us -> 94.8 us
    convert_element_type x6, other arithmetic: 4.93 us -> 0.37 us  [scan_states(): other = beside(bit, [array.astype(BF16) for array in total])]
    ppermute x22, waiting for transfers between devices: 15.6 us -> 18.5 us  [swap(): return lax.ppermute(array, axis, [(i, i ^ 1 << bit) for i in range(size)])]
    pallas_call x20, Pallas kernels: 97.6 us -> 94.8 us  [call(): kernel(*(table[n] for n, _ in at), *args, *after)]
  transfers between devices with their start and end apart: 27 -> 27, of which waited for: 14 -> 15; matrix products, arithmetic and copies ran while one was open for 5% -> 3% of each run, Pallas kernels for 50% -> 50%
where the time goes in v5:
time: 164 us; the launch traced here: 163 us
  Pallas kernels  94.8 us (58%)
  starting transfers between devices  29.1 us (18%)
  waiting for transfers between devices  28.8 us (18%)
  local copies, waits for them, and re-layouts  4.65 us (3%)
  other arithmetic  3.92 us (2%)
  between operations  1.68 us (1%)
    pallas_call x20, Pallas kernels, call(): kernel(*(table[n] for n, _ in at), *args, *after)  94.8 us
    ppermute x22, starting transfers between devices, swap(): return lax.ppermute(array, axis, [(i, i ^ 1 << bit) for i in range(size)])  23.9 us
    ppermute x22, waiting for transfers between devices, swap(): return lax.ppermute(array, axis, [(i, i ^ 1 << bit) for i in range(size)])  18.5 us
    ppermute x5, waiting for transfers between devices, shift(): lax.ppermute(array, 'head', [(i, (i + 2 * by) % size) for i in range(size)])  10.2 us
    ppermute x5, starting transfers between devices, shift(): lax.ppermute(array, 'head', [(i, (i + 2 * by) % size) for i in range(size)])  5.2 us
  transfers between devices with their start and end apart: 27, of which 15 were waited for; matrix products, arithmetic and copies ran while one was open for 3% of the time, Pallas kernels for 50%

profile of v5, /device:TPU:0, one launch (start us, length us, event | category | flops | bytes accessed | tf_op | source)
XLA Modules:
  0.0 162.9 jit_solution(13278615689065457288)
XLA Ops:
  1.1 2.0 %shard_map.85 = (bf16[4,128,128]{2,1,0:T(8,128)(2,1)S(1)}, bf16[4,128,128]{2,1,0:T(8,128)(2,1)S(1)}) custom-call(s32[1]{0:T(128)} %bitcast.5.refs_0_.refs_1_, bf16[512,2048]{1,0:T(8,128)(2,1)} %refs_1_.21, bf16[512,2048]{1,0:T(8,128)(2,1)} %refs_2_.17), custom_call_target="tpu_custom_call" | custom-call | flops 1 | bytes 1 | tf_op jit(solution)/shard_map/pallas_call | solution.py:73
  3.1 2.6 %collective-permute-start.3 = (bf16[4,128,128]{2,1,0:T(8,128)(2,1)S(1)}, bf16[4,128,128]{2,1,0:T(8,128)(2,1)S(1)}, u32[]{:S(2)}, u32[]{:S(2)}) collective-permute-start(bf16[4,128,128]{2,1,0:T(8,128)(2,1)S(1)} %get-tuple-element.61.refs_3_), channel_id=1, source_target_pairs={{0,4},{4,0},{8,12},{12,8},{16,20},{20,16},{24,28},{28,24},{1,5},{5... | collective-permute-start | bytes 393224 | tf_op jit(solution)/shard_map/ppermute | solution.py:465
  5.8 2.0 %shard_map.86 = (bf16[4,128,128]{2,1,0:T(8,128)(2,1)S(1)}, bf16[4,128,128]{2,1,0:T(8,128)(2,1)S(1)}) custom-call(s32[1]{0:T(128)} %bitcast.refs_0_, bf16[512,2048]{1,0:T(8,128)(2,1)} %refs_1_.21, bf16[512,2048]{1,0:T(8,128)(2,1)} %refs_2_.17, bf16[4,128,128]{2,1,0:T(8,128)(2,1)S(1)} %get-tuple-element.61.refs_3_), custom_call_target="tpu_custom_call" | custom-call | flops 1 | bytes 1 | tf_op jit(solution)/shard_map/pallas_call | solution.py:73
  8.5 1.6 collective-permute-done.3
  10.1 2.1 %collective-permute-start.4 = (bf16[4,128,128]{2,1,0:T(8,128)(2,1)S(1)}, bf16[4,128,128]{2,1,0:T(8,128)(2,1)S(1)}, u32[]{:S(2)}, u32[]{:S(2)}) collective-permute-start(bf16[4,128,128]{2,1,0:T(8,128)(2,1)S(1)} %fusion.20), channel_id=1, source_target_pairs={{0,8},{4,12},{8,0},{12,4},{16,24},{20,28},{24,16},{28,20},{1,9},{5... | collective-permute-start | bytes 393224 | tf_op jit(solution)/shard_map/ppermute | solution.py:465
  12.7 1.9 %collective-permute-start.1 = (bf16[4,128,128]{2,1,0:T(8,128)(2,1)S(1)}, bf16[4,128,128]{2,1,0:T(8,128)(2,1)S(1)}, u32[]{:S(2)}, u32[]{:S(2)}) collective-permute-start(bf16[4,128,128]{2,1,0:T(8,128)(2,1)S(1)} %fusion.19), channel_id=1, source_target_pairs={{0,8},{4,12},{8,0},{12,4},{16,24},{20,28},{24,16},{28,20},{1,9},{5... | collective-permute-start | bytes 393224 | tf_op jit(solution)/shard_map/ppermute | solution.py:465
  15.3 3.3 %collective-permute-start.5 = (bf16[4,128,128]{2,1,0:T(8,128)(2,1)S(1)}, bf16[4,128,128]{2,1,0:T(8,128)(2,1)S(1)}, u32[]{:S(2)}, u32[]{:S(2)}) collective-permute-start(bf16[4,128,128]{2,1,0:T(8,128)(2,1)S(1)} %fusion.17.refs_4_), channel_id=1, source_target_pairs={{0,16},{4,20},{8,24},{12,28},{16,0},{20,4},{24,8},{28,12},{1,17},{... | collective-permute-start | bytes 393224 | tf_op jit(solution)/shard_map/ppermute | solution.py:465
  19.2 1.6 collective-permute-start.6
  20.9 1.2 collective-permute-start.2
  22.1 4.6 %shard_map.87 = (f32[512,1024]{1,0:T(8,128)}, f32[8,128]{1,0:T(8,128)S(1)}) custom-call(s32[1]{0:T(128)} %bitcast.refs_0_, bf16[512,2048]{1,0:T(8,128)(2,1)} %refs_1_.19, bf16[512,2048]{1,0:T(8,128)(2,1)} %refs_1_.21, bf16[512,2048]{1,0:T(8,128)(2,1)} %refs_2_.17, bf16[4,128,128]{2,1,0:T(8,128)(2,1)S(1)} %fusion.17.refs_4_), custom_call_target="tpu_custom_call" | custom-call | flops 1 | bytes 1 | tf_op jit(solution)/shard_map/pallas_call | solution.py:73
  26.7 1.6 collective-permute-start.8
  28.4 1.2 collective-permute-done.2
  29.6 1.7 %collective-permute-start.7 = (bf16[4,128,128]{2,1,0:T(8,128)(2,1)S(1)}, bf16[4,128,128]{2,1,0:T(8,128)(2,1)S(1)}, u32[]{:S(2)}, u32[]{:S(2)}) collective-permute-start(bf16[4,128,128]{2,1,0:T(8,128)(2,1)S(1)} %get-tuple-element.125.refs_4_), channel_id=1, source_target_pairs={{0,4},{4,0},{8,12},{12,8},{16,20},{20,16},{24,28},{28,24},{1,5},{5... | collective-permute-start | bytes 393224 | tf_op jit(solution)/shard_map/ppermute | solution.py:465
  31.3 4.6 %shard_map.88 = (f32[512,1024]{1,0:T(8,128)}, f32[8,128]{1,0:T(8,128)S(1)}) custom-call(s32[1]{0:T(128)} %bitcast.5.refs_0_.refs_1_, bf16[512,2048]{1,0:T(8,128)(2,1)} %refs_1_.19, bf16[512,2048]{1,0:T(8,128)(2,1)} %refs_1_.21, bf16[512,2048]{1,0:T(8,128)(2,1)} %refs_2_.17, bf16[4,128,128]{2,1,0:T(8,128)(2,1)S(1)} %get-tuple-element.125.refs_4_, ...), custom_call_target="tpu_custom_call" | custom-call | flops 1 | bytes 1 | tf_op jit(solution)/shard_map/pallas_call | solution.py:73
  37.1 1.6 %shard_map.89.refs_3_ = bf16[512,1024]{1,0:T(8,128)(2,1)} custom-call(s32[1]{0:T(128)} %bitcast.refs_0_, bf16[512,2048]{1,0:T(8,128)(2,1)S(1)} %copy-done, f32[512,1024]{1,0:T(8,128)S(1)} %copy-done.5, bf16[4,128,128]{2,1,0:T(8,128)(2,1)S(1)} %get-tuple-element.126.refs_3_, bf16[4,128,128]{2,1,0:T(8,128)(2,1)S(1)} %get-tuple-element.124.refs_4_), custom_call_target="tpu_custom_call" | custom-call | flops 1 | bytes 1 | tf_op jit(solution)/shard_map/pallas_call | solution.py:73
  38.8 2.3 %collective-permute-done.10 = s32[8,128]{1,0:T(8,128)S(1)} collective-permute-done((s32[8,128]{1,0:T(8,128)S(1)}, s32[8,128]{1,0:T(8,128)S(1)}, u32[]{:S(2)}, u32[]{:S(2)}) %collective-permute-start.10) | collective-permute-done | bytes 4128 | tf_op jit(solution)/shard_map/ppermute | solution.py:465
  42.2 2.7 %collective-permute-done.12.refs_6_ = bf16[512,1024]{1,0:T(8,128)(2,1)} collective-permute-done((bf16[512,1024]{1,0:T(8,128)(2,1)S(1)}, bf16[512,1024]{1,0:T(8,128)(2,1)}, u32[]{:S(2)}, u32[]{:S(2)}) %collective-permute-start.12) | collective-permute-done | bytes 1048608 | tf_op jit(solution)/shard_map/ppermute | solution.py:465
  44.9 5.8 %shard_map.91.refs_9_ = bf16[512,512]{1,0:T(8,128)(2,1)} custom-call(s32[1]{0:T(128)} %bitcast.refs_0_, s32[1]{0:T(128)} %bitcast.5.refs_0_.refs_1_, s32[1]{0:T(128)} %bitcast.1.refs_2_.refs_0_.refs_1_, bf16[512,1024]{1,0:T(8,128)(2,1)} %shard_map.89.refs_3_, bf16[512,1024]{1,0:T(8,128)(2,1)} %collective-permute-done.11.refs_4_, ...), custom_call_target="tpu_custom_call" | custom-call | flops 1 | bytes 1 | tf_op jit(solution)/shard_map/pallas_call | solution.py:73
  50.8 1.7 %collective-permute-start.14 = (bf16[512,512]{1,0:T(8,128)(2,1)}, bf16[512,512]{1,0:T(8,128)(2,1)}, u32[]{:S(2)}, u32[]{:S(2)}) collective-permute-start(bf16[512,512]{1,0:T(8,128)(2,1)} %shard_map.91.refs_9_), channel_id=1, source_target_pairs={{0,2},{1,3},{2,0},{3,1},{4,6},{5,7},{6,4},{7,5},{8,10},{9,11},{10,... | collective-permute-start | bytes 1572872 | tf_op jit(solution)/shard_map/ppermute | solution.py:610
  52.5 5.1 %shard_map.92.refs_9_ = bf16[512,512]{1,0:T(8,128)(2,1)S(1)} custom-call(s32[1]{0:T(128)} %bitcast.refs_0_, s32[1]{0:T(128)} %bitcast.5.refs_0_.refs_1_, s32[1]{0:T(128)} %bitcast.3.refs_2_.refs_0_, bf16[512,1024]{1,0:T(8,128)(2,1)} %shard_map.89.refs_3_, bf16[512,1024]{1,0:T(8,128)(2,1)} %collective-permute-done.11.refs_4_, ...), custom_call_target="tpu_custom_call" | custom-call | flops 1 | bytes 1 | tf_op jit(solution)/shard_map/pallas_call | solution.py:73
  57.6 5.1 %shard_map.93.refs_9_ = bf16[512,512]{1,0:T(8,128)(2,1)S(1)} custom-call(s32[1]{0:T(128)} %bitcast.refs_0_, s32[1]{0:T(128)} %bitcast.5.refs_0_.refs_1_, s32[1]{0:T(128)} %bitcast.1.refs_2_.refs_0_.refs_1_, bf16[512,1024]{1,0:T(8,128)(2,1)} %shard_map.89.refs_3_, bf16[512,1024]{1,0:T(8,128)(2,1)} %collective-permute-done.11.refs_4_, ...), custom_call_target="tpu_custom_call" | custom-call | flops 1 | bytes 1 | tf_op jit(solution)/shard_map/pallas_call | solution.py:73
  65.1 3.7 %shard_map.94.refs_9_ = bf16[512,256]{1,0:T(8,128)(2,1)S(1)} custom-call(s32[1]{0:T(128)} %bitcast.refs_0_, s32[1]{0:T(128)} %bitcast.5.refs_0_.refs_1_, s32[1]{0:T(128)} %bitcast.1.refs_2_.refs_0_.refs_1_, bf16[512,1024]{1,0:T(8,128)(2,1)} %shard_map.89.refs_3_, bf16[512,1024]{1,0:T(8,128)(2,1)} %collective-permute-done.11.refs_4_, ...), custom_call_target="tpu_custom_call" | custom-call | flops 1 | bytes 1 | tf_op jit(solution)/shard_map/pallas_call | solution.py:73
  68.8 2.5 %collective-permute-start.16 = (bf16[512,256]{1,0:T(8,128)(2,1)S(1)}, bf16[512,256]{1,0:T(8,128)(2,1)S(1)}, u32[]{:S(2)}, u32[]{:S(2)}) collective-permute-start(bf16[512,256]{1,0:T(8,128)(2,1)S(1)} %shard_map.94.refs_9_), channel_id=1, source_target_pairs={{0,2},{1,3},{2,0},{3,1},{4,6},{5,7},{6,4},{7,5},{8,10},{9,11},{10,... | collective-permute-start | bytes 786440 | tf_op jit(solution)/shard_map/ppermute | solution.py:610
  71.4 6.5 %shard_map.95 = bf16[512,768]{1,0:T(8,128)(2,1)S(1)} custom-call(s32[1]{0:T(128)} %bitcast.refs_0_, s32[1]{0:T(128)} %bitcast.5.refs_0_.refs_1_, s32[1]{0:T(128)} %bitcast.3.refs_2_.refs_0_, bf16[512,1024]{1,0:T(8,128)(2,1)} %shard_map.89.refs_3_, bf16[512,1024]{1,0:T(8,128)(2,1)} %collective-permute-done.11.refs_4_, ...), custom_call_target="tpu_custom_call" | custom-call | flops 1 | bytes 1 | tf_op jit(solution)/shard_map/pallas_call | solution.py:73
  77.9 1.2 copy-done.12
  79.2 1.4 multiply_convert_fusion.refs_2_
  80.9 1.1 collective-permute-done.16
  82.1 1.0 multiply_convert_fusion.1.refs_3_
  84.1 1.3 collective-permute-done.18.refs_6_
  85.3 10.1 %shard_map.96 = (f32[512,2048]{1,0:T(8,128)}, f32[8,128]{1,0:T(8,128)S(1)}) custom-call(s32[1]{0:T(128)} %bitcast.3.refs_2_.refs_0_, s32[1]{0:T(128)} %bitcast.4.refs_1_, bf16[512,768]{1,0:T(8,128)(2,1)S(1)} %multiply_convert_fusion.refs_2_, bf16[512,512]{1,0:T(8,128)(2,1)} %multiply_convert_fusion.1.refs_3_, bf16[2048,5120]{1,0:T(8,128)(2,1)} %refs_8_.3, ...), custom_call_target="tpu_custom_call" | custom-call | flops 1 | bytes 1 | tf_op jit(solution)/shard_map/pallas_call | solution.py:73
  95.5 5.2 %collective-permute-done.19.refs_3_ = bf16[512,768]{1,0:T(8,128)(2,1)} collective-permute-done((bf16[512,768]{1,0:T(8,128)(2,1)S(1)}, bf16[512,768]{1,0:T(8,128)(2,1)}, u32[]{:S(2)}, u32[]{:S(2)}) %collective-permute-start.19) | collective-permute-done | bytes 786464 | tf_op jit(solution)/shard_map/ppermute | solution.py:610
  101.0 2.4 %collective-permute-done.20.refs_5_ = bf16[512,768]{1,0:T(8,128)(2,1)} collective-permute-done((bf16[512,768]{1,0:T(8,128)(2,1)}, bf16[512,768]{1,0:T(8,128)(2,1)}, u32[]{:S(2)}, u32[]{:S(2)}) %collective-permute-start.20) | collective-permute-done | bytes 786464 | tf_op jit(solution)/shard_map/ppermute | solution.py:465
  103.3 8.9 %shard_map.97 = (f32[512,2048]{1,0:T(8,128)}, f32[8,128]{1,0:T(8,128)S(1)}) custom-call(s32[1]{0:T(128)} %bitcast.1.refs_2_.refs_0_.refs_1_, s32[1]{0:T(128)} %bitcast.2.refs_1_.refs_2_, f32[512,2048]{1,0:T(8,128)} %get-tuple-element.85.refs_2_, bf16[512,768]{1,0:T(8,128)(2,1)} %collective-permute-done.19.refs_3_, bf16[2048,5120]{1,0:T(8,128)(2,1)} %refs_8_.3, ...), custom_call_target="tpu_custom_call" | custom-call | flops 1 | bytes 1 | tf_op jit(solution)/shard_map/pallas_call | solution.py:73
  112.2 3.1 %collective-permute-done.21.refs_5_ = bf16[512,512]{1,0:T(8,128)(2,1)S(1)} collective-permute-done((bf16[512,512]{1,0:T(8,128)(2,1)}, bf16[512,512]{1,0:T(8,128)(2,1)S(1)}, u32[]{:S(2)}, u32[]{:S(2)}) %collective-permute-start.21) | collective-permute-done | bytes 524320 | tf_op jit(solution)/shard_map/ppermute | solution.py:610
  115.2 1.9 %collective-permute-done.22.refs_7_ = bf16[512,512]{1,0:T(8,128)(2,1)S(1)} collective-permute-done((bf16[512,512]{1,0:T(8,128)(2,1)S(1)}, bf16[512,512]{1,0:T(8,128)(2,1)S(1)}, u32[]{:S(2)}, u32[]{:S(2)}) %collective-permute-start.22) | collective-permute-done | bytes 524320 | tf_op jit(solution)/shard_map/ppermute | solution.py:465
  117.1 4.8 %shard_map.98 = (bf16[512,1024]{1,0:T(8,128)(2,1)}, bf16[8,128,128]{2,1,0:T(8,128)(2,1)S(1)}) custom-call(s32[1]{0:T(128)} %bitcast.5.refs_0_.refs_1_, s32[1]{0:T(128)} %bitcast.1.refs_2_.refs_0_.refs_1_, s32[1]{0:T(128)} %bitcast.2.refs_1_.refs_2_, f32[512,2048]{1,0:T(8,128)} %get-tuple-element.89.refs_3_, bf16[512,2048]{1,0:T(8,128)(2,1)S(1)} %copy-done, ...), custom_call_target="tpu_custom_call" | custom-call | flops 1 | bytes 1 | tf_op jit(solution)/shard_map/pallas_call | solution.py:73
  121.9 1.4 collective-permute-start.23
  123.3 4.8 %shard_map.99 = (bf16[512,1024]{1,0:T(8,128)(2,1)}, bf16[8,128,128]{2,1,0:T(8,128)(2,1)S(1)}) custom-call(s32[1]{0:T(128)} %bitcast.refs_0_, s32[1]{0:T(128)} %bitcast.1.refs_2_.refs_0_.refs_1_, s32[1]{0:T(128)} %bitcast.2.refs_1_.refs_2_, f32[512,2048]{1,0:T(8,128)} %get-tuple-element.89.refs_3_, bf16[512,2048]{1,0:T(8,128)(2,1)S(1)} %copy-done, ...), custom_call_target="tpu_custom_call" | custom-call | flops 1 | bytes 1 | tf_op jit(solution)/shard_map/pallas_call | solution.py:73
  128.2 2.2 %collective-permute-done.23 = bf16[8,128,128]{2,1,0:T(8,128)(2,1)S(1)} collective-permute-done((bf16[8,128,128]{2,1,0:T(8,128)(2,1)S(1)}, bf16[8,128,128]{2,1,0:T(8,128)(2,1)S(1)}, u32[]{:S(2)}, u32[]{:S(2)}) %collective-permute-start.23) | collective-permute-done | bytes 262176 | tf_op jit(solution)/shard_map/ppermute | solution.py:465
  131.3 6.9 %shard_map.100 = (f32[512,2048]{1,0:T(8,128)}, bf16[512,1024]{1,0:T(8,128)(2,1)}, bf16[512,1024]{1,0:T(8,128)(2,1)}, f32[8,128]{1,0:T(8,128)S(1)}) custom-call(s32[1]{0:T(128)} %bitcast.refs_0_, bf16[512,2048]{1,0:T(8,128)(2,1)} %refs_1_.19, bf16[512,2048]{1,0:T(8,128)(2,1)} %refs_1_.21, bf16[512,2048]{1,0:T(8,128)(2,1)} %refs_2_.17, ...), custom_call_target="tpu_custom_call" | custom-call | flops 1 | bytes 1 | tf_op jit(solution)/shard_map/pallas_call | solution.py:73
  138.3 2.5 %collective-permute-start.25 = (bf16[8,128,128]{2,1,0:T(8,128)(2,1)S(1)}, bf16[8,128,128]{2,1,0:T(8,128)(2,1)S(1)}, u32[]{:S(2)}, u32[]{:S(2)}) collective-permute-start(bf16[8,128,128]{2,1,0:T(8,128)(2,1)S(1)} %fusion.4.refs_7_), channel_id=1, source_target_pairs={{0,16},{4,20},{8,24},{12,28},{16,0},{20,4},{24,8},{28,12},{1,17},{... | collective-permute-start | bytes 786440 | tf_op jit(solution)/shard_map/ppermute | solution.py:465
  140.8 8.5 %shard_map.101 = (f32[512,2048]{1,0:T(8,128)}, bf16[512,1024]{1,0:T(8,128)(2,1)}, bf16[512,1024]{1,0:T(8,128)(2,1)}, f32[8,128]{1,0:T(8,128)S(1)}) custom-call(s32[1]{0:T(128)} %bitcast.5.refs_0_.refs_1_, bf16[512,2048]{1,0:T(8,128)(2,1)} %refs_1_.19, bf16[512,2048]{1,0:T(8,128)(2,1)} %refs_1_.21, ...), custom_call_target="tpu_custom_call", output_to_operand_aliasing={{0}: (6, {})} | custom-call | flops 1 | bytes 1 | tf_op jit(solution)/shard_map/pallas_call | solution.py:73
  149.3 3.7 %shard_map.102 = (f32[512,2048]{1,0:T(8,128)}, bf16[512,1024]{1,0:T(8,128)(2,1)}, bf16[512,1024]{1,0:T(8,128)(2,1)}, f32[8,128]{1,0:T(8,128)S(1)}) custom-call(s32[1]{0:T(128)} %bitcast.refs_0_, bf16[512,2048]{1,0:T(8,128)(2,1)} %refs_1_.19, bf16[512,2048]{1,0:T(8,128)(2,1)} %refs_1_.21, ...), custom_call_target="tpu_custom_call", output_to_operand_aliasing={{0}: (6, {}), {1}: (7, {}), {2}: (8, {})} | custom-call | flops 1 | bytes 1 | tf_op jit(solution)/shard_map/pallas_call | solution.py:73
  153.2 1.3 collective-permute-start.26
  154.6 1.2 copy-done.4
  155.8 2.7 %shard_map.103 = (f32[512,2048]{1,0:T(8,128)}, f32[512,2048]{1,0:T(8,128)}) custom-call(s32[1]{0:T(128)} %bitcast.refs_0_, bf16[512,2048]{1,0:T(8,128)(2,1)S(1)} %copy-done.1, bf16[512,2048]{1,0:T(8,128)(2,1)S(1)} %copy-done.2, bf16[8,128,128]{2,1,0:T(8,128)(2,1)S(1)} %get-tuple-element.119.refs_3_.refs_7_, bf16[512,1024]{1,0:T(8,128)(2,1)S(1)} %copy-done.3, ...), custom_call_target="tpu_custom_call" | custom-call | flops 1 | bytes 1 | tf_op jit(solution)/shard_map/pallas_call | solution.py:73
  158.4 1.8 %collective-permute-done.26.refs_3_ = bf16[8,128,128]{2,1,0:T(8,128)(2,1)S(1)} collective-permute-done((bf16[8,128,128]{2,1,0:T(8,128)(2,1)S(1)}, bf16[8,128,128]{2,1,0:T(8,128)(2,1)S(1)}, u32[]{:S(2)}, u32[]{:S(2)}) %collective-permute-start.26) | collective-permute-done | bytes 262176 | tf_op jit(solution)/shard_map/ppermute | solution.py:465
  160.2 2.7 %shard_map.104 = (f32[512,2048]{1,0:T(8,128)}, f32[512,2048]{1,0:T(8,128)}) custom-call(s32[1]{0:T(128)} %bitcast.5.refs_0_.refs_1_, bf16[512,2048]{1,0:T(8,128)(2,1)S(1)} %copy-done.1, bf16[512,2048]{1,0:T(8,128)(2,1)S(1)} %copy-done.2, bf16[8,128,128]{2,1,0:T(8,128)(2,1)S(1)} %collective-permute-done.26.refs_3_, ...), custom_call_target="tpu_custom_call", output_to_operand_aliasing={{0}: (6, {}), {1}: (7, {})} | custom-call | flops 1 | bytes 1 | tf_op jit(solution)/shard_map/pallas_call | solution.py:73
  (77 shorter events, 10.4 us)
Async XLA Ops:
  0.6 44.3 %collective-permute-start.13 = (bf16[2048,5120]{1,0:T(8,128)(2,1)}, bf16[2048,5120]{1,0:T(8,128)(2,1)}, u32[]{:S(2)}, u32[]{:S(2)}) collective-permute-start(bf16[2048,5120]{1,0:T(8,128)(2,1)} %refs_8_.3), channel_id=1, source_target_pairs={{0,1},{1,0},{2,3},{3,2},{4,5},{5,4},{6,7},{7,6},{8,9},{9,8},{10,11... | collective-permute-start | bytes 62914568 | tf_op jit(solution)/shard_map/ppermute | solution.py:465
  3.1 7.0 %collective-permute-start.3 = (bf16[4,128,128]{2,1,0:T(8,128)(2,1)S(1)}, bf16[4,128,128]{2,1,0:T(8,128)(2,1)S(1)}, u32[]{:S(2)}, u32[]{:S(2)}) collective-permute-start(bf16[4,128,128]{2,1,0:T(8,128)(2,1)S(1)} %get-tuple-element.61.refs_3_), channel_id=1, source_target_pairs={{0,4},{4,0},{8,12},{12,8},{16,20},{20,16},{24,28},{28,24},{1,5},{5... | collective-permute-start | bytes 393224 | tf_op jit(solution)/shard_map/ppermute | solution.py:465
  5.7 6.9 %collective-permute-start = (bf16[4,128,128]{2,1,0:T(8,128)(2,1)S(1)}, bf16[4,128,128]{2,1,0:T(8,128)(2,1)S(1)}, u32[]{:S(2)}, u32[]{:S(2)}) collective-permute-start(bf16[4,128,128]{2,1,0:T(8,128)(2,1)S(1)} %get-tuple-element.63), channel_id=1, source_target_pairs={{0,4},{4,0},{8,12},{12,8},{16,20},{20,16},{24,28},{28,24},{1,5},{5... | collective-permute-start | bytes 393224 | tf_op jit(solution)/shard_map/ppermute | solution.py:465
  5.8 2.0 %copy-start.13 = (s32[512]{0:T(512)S(1)}, s32[512]{0:T(512)}, u32[]{:S(2)}) copy-start(s32[512]{0:T(512)} %param.11) | copy-start | bytes 6148
  10.1 5.1 %collective-permute-start.4 = (bf16[4,128,128]{2,1,0:T(8,128)(2,1)S(1)}, bf16[4,128,128]{2,1,0:T(8,128)(2,1)S(1)}, u32[]{:S(2)}, u32[]{:S(2)}) collective-permute-start(bf16[4,128,128]{2,1,0:T(8,128)(2,1)S(1)} %fusion.20), channel_id=1, source_target_pairs={{0,8},{4,12},{8,0},{12,4},{16,24},{20,28},{24,16},{28,20},{1,9},{5... | collective-permute-start | bytes 393224 | tf_op jit(solution)/shard_map/ppermute | solution.py:465
  12.7 8.1 %collective-permute-start.1 = (bf16[4,128,128]{2,1,0:T(8,128)(2,1)S(1)}, bf16[4,128,128]{2,1,0:T(8,128)(2,1)S(1)}, u32[]{:S(2)}, u32[]{:S(2)}) collective-permute-start(bf16[4,128,128]{2,1,0:T(8,128)(2,1)S(1)} %fusion.19), channel_id=1, source_target_pairs={{0,8},{4,12},{8,0},{12,4},{16,24},{20,28},{24,16},{28,20},{1,9},{5... | collective-permute-start | bytes 393224 | tf_op jit(solution)/shard_map/ppermute | solution.py:465
  15.3 13.0 %collective-permute-start.5 = (bf16[4,128,128]{2,1,0:T(8,128)(2,1)S(1)}, bf16[4,128,128]{2,1,0:T(8,128)(2,1)S(1)}, u32[]{:S(2)}, u32[]{:S(2)}) collective-permute-start(bf16[4,128,128]{2,1,0:T(8,128)(2,1)S(1)} %fusion.17.refs_4_), channel_id=1, source_target_pairs={{0,16},{4,20},{8,24},{12,28},{16,0},{20,4},{24,8},{28,12},{1,17},{... | collective-permute-start | bytes 393224 | tf_op jit(solution)/shard_map/ppermute | solution.py:465
  19.2 7.4 %collective-permute-start.6 = (s32[8,128]{1,0:T(8,128)S(1)}, s32[8,128]{1,0:T(8,128)S(1)}, u32[]{:S(2)}, u32[]{:S(2)}) collective-permute-start(s32[8,128]{1,0:T(8,128)S(1)} %broadcast_in_dim.49), channel_id=1, source_target_pairs={{0,4},{4,0},{8,12},{12,8},{16,20},{20,16},{24,28},{28,24},{1,5},{5... | collective-permute-start | bytes 12296 | tf_op jit(solution)/shard_map/ppermute | solution.py:465
  20.9 8.7 %collective-permute-start.2 = (bf16[4,128,128]{2,1,0:T(8,128)(2,1)S(1)}, bf16[4,128,128]{2,1,0:T(8,128)(2,1)S(1)}, u32[]{:S(2)}, u32[]{:S(2)}) collective-permute-start(bf16[4,128,128]{2,1,0:T(8,128)(2,1)S(1)} %fusion.12), channel_id=1, source_target_pairs={{0,16},{4,20},{8,24},{12,28},{16,0},{20,4},{24,8},{28,12},{1,17},{... | collective-permute-start | bytes 393224 | tf_op jit(solution)/shard_map/ppermute | solution.py:465
  26.7 9.2 %collective-permute-start.8 = (s32[8,128]{1,0:T(8,128)S(1)}, s32[8,128]{1,0:T(8,128)S(1)}, u32[]{:S(2)}, u32[]{:S(2)}) collective-permute-start(s32[8,128]{1,0:T(8,128)S(1)} %add.95), channel_id=1, source_target_pairs={{0,8},{4,12},{8,0},{12,4},{16,24},{20,28},{24,16},{28,20},{1,9},{5... | collective-permute-start | bytes 12296 | tf_op jit(solution)/shard_map/ppermute | solution.py:465
  29.6 7.5 %copy-start = (bf16[512,2048]{1,0:T(8,128)(2,1)S(1)}, bf16[512,2048]{1,0:T(8,128)(2,1)}, u32[]{:S(2)}) copy-start(bf16[512,2048]{1,0:T(8,128)(2,1)} %refs_1_.19) | copy-start | bytes 6291460
  29.6 7.5 %copy-start.5 = (f32[512,1024]{1,0:T(8,128)S(1)}, f32[512,1024]{1,0:T(8,128)}, u32[]{:S(2)}) copy-start(f32[512,1024]{1,0:T(8,128)} %get-tuple-element.80.refs_2_) | copy-start | bytes 6291460
  29.6 6.4 %collective-permute-start.7 = (bf16[4,128,128]{2,1,0:T(8,128)(2,1)S(1)}, bf16[4,128,128]{2,1,0:T(8,128)(2,1)S(1)}, u32[]{:S(2)}, u32[]{:S(2)}) collective-permute-start(bf16[4,128,128]{2,1,0:T(8,128)(2,1)S(1)} %get-tuple-element.125.refs_4_), channel_id=1, source_target_pairs={{0,4},{4,0},{8,12},{12,8},{16,20},{20,16},{24,28},{28,24},{1,5},{5... | collective-permute-start | bytes 393224 | tf_op jit(solution)/shard_map/ppermute | solution.py:465
  36.0 5.0 %collective-permute-start.9 = (bf16[4,128,128]{2,1,0:T(8,128)(2,1)S(1)}, bf16[4,128,128]{2,1,0:T(8,128)(2,1)S(1)}, u32[]{:S(2)}, u32[]{:S(2)}) collective-permute-start(bf16[4,128,128]{2,1,0:T(8,128)(2,1)S(1)} %get-tuple-element.77), channel_id=1, source_target_pairs={{0,4},{4,0},{8,12},{12,8},{16,20},{20,16},{24,28},{28,24},{1,5},{5... | collective-permute-start | bytes 393224 | tf_op jit(solution)/shard_map/ppermute | solution.py:465
  36.6 4.5 %collective-permute-start.10 = (s32[8,128]{1,0:T(8,128)S(1)}, s32[8,128]{1,0:T(8,128)S(1)}, u32[]{:S(2)}, u32[]{:S(2)}) collective-permute-start(s32[8,128]{1,0:T(8,128)S(1)} %add.96), channel_id=1, source_target_pairs={{0,16},{4,20},{8,24},{12,28},{16,0},{20,4},{24,8},{28,12},{1,17},{... | collective-permute-start | bytes 12296 | tf_op jit(solution)/shard_map/ppermute | solution.py:465
  37.1 4.0 %copy-start.6 = (f32[512,1024]{1,0:T(8,128)S(1)}, f32[512,1024]{1,0:T(8,128)}, u32[]{:S(2)}) copy-start(f32[512,1024]{1,0:T(8,128)} %get-tuple-element.81.refs_2_) | copy-start | bytes 6291460
  38.8 3.4 %collective-permute-start.11 = (bf16[512,1024]{1,0:T(8,128)(2,1)}, bf16[512,1024]{1,0:T(8,128)(2,1)}, u32[]{:S(2)}, u32[]{:S(2)}) collective-permute-start(bf16[512,1024]{1,0:T(8,128)(2,1)} %shard_map.89.refs_3_), channel_id=1, source_target_pairs={{0,1},{1,0},{2,3},{3,2},{4,5},{5,4},{6,7},{7,6},{8,9},{9,8},{10,11... | collective-permute-start | bytes 3145736 | tf_op jit(solution)/shard_map/ppermute | solution.py:465
  41.1 1.0 copy-start.9
  42.1 2.9 %collective-permute-start.12 = (bf16[512,1024]{1,0:T(8,128)(2,1)S(1)}, bf16[512,1024]{1,0:T(8,128)(2,1)}, u32[]{:S(2)}, u32[]{:S(2)}) collective-permute-start(bf16[512,1024]{1,0:T(8,128)(2,1)S(1)} %shard_map.90.refs_5_), channel_id=1, source_target_pairs={{0,1},{1,0},{2,3},{3,2},{4,5},{5,4},{6,7},{7,6},{8,9},{9,8},{10,11... | collective-permute-start | bytes 3145736 | tf_op jit(solution)/shard_map/ppermute | solution.py:465
  50.8 14.3 %collective-permute-start.14 = (bf16[512,512]{1,0:T(8,128)(2,1)}, bf16[512,512]{1,0:T(8,128)(2,1)}, u32[]{:S(2)}, u32[]{:S(2)}) collective-permute-start(bf16[512,512]{1,0:T(8,128)(2,1)} %shard_map.91.refs_9_), channel_id=1, source_target_pairs={{0,2},{1,3},{2,0},{3,1},{4,6},{5,7},{6,4},{7,5},{8,10},{9,11},{10,... | collective-permute-start | bytes 1572872 | tf_op jit(solution)/shard_map/ppermute | solution.py:610
  62.7 15.2 %collective-permute-start.15 = (bf16[512,512]{1,0:T(8,128)(2,1)S(1)}, bf16[512,512]{1,0:T(8,128)(2,1)S(1)}, u32[]{:S(2)}, u32[]{:S(2)}) collective-permute-start(bf16[512,512]{1,0:T(8,128)(2,1)S(1)} %shard_map.93.refs_9_), channel_id=1, source_target_pairs={{0,2},{1,3},{2,0},{3,1},{4,6},{5,7},{6,4},{7,5},{8,10},{9,11},{10,... | collective-permute-start | bytes 1572872 | tf_op jit(solution)/shard_map/ppermute | solution.py:610
  68.8 13.3 %collective-permute-start.16 = (bf16[512,256]{1,0:T(8,128)(2,1)S(1)}, bf16[512,256]{1,0:T(8,128)(2,1)S(1)}, u32[]{:S(2)}, u32[]{:S(2)}) collective-permute-start(bf16[512,256]{1,0:T(8,128)(2,1)S(1)} %shard_map.94.refs_9_), channel_id=1, source_target_pairs={{0,2},{1,3},{2,0},{3,1},{4,6},{5,7},{6,4},{7,5},{8,10},{9,11},{10,... | collective-permute-start | bytes 786440 | tf_op jit(solution)/shard_map/ppermute | solution.py:610
  77.8 1.3 copy-start.12
  80.5 3.5 %collective-permute-start.17 = (bf16[512,768]{1,0:T(8,128)(2,1)S(1)}, bf16[512,768]{1,0:T(8,128)(2,1)}, u32[]{:S(2)}, u32[]{:S(2)}) collective-permute-start(bf16[512,768]{1,0:T(8,128)(2,1)S(1)} %multiply_convert_fusion.refs_2_), channel_id=1, source_target_pairs={{0,1},{1,0},{2,3},{3,2},{4,5},{5,4},{6,7},{7,6},{8,9},{9,8},{10,11... | collective-permute-start | bytes 2359304 | tf_op jit(solution)/shard_map/ppermute | solution.py:465
  80.6 20.1 %collective-permute-start.19 = (bf16[512,768]{1,0:T(8,128)(2,1)S(1)}, bf16[512,768]{1,0:T(8,128)(2,1)}, u32[]{:S(2)}, u32[]{:S(2)}) collective-permute-start(bf16[512,768]{1,0:T(8,128)(2,1)S(1)} %multiply_convert_fusion.refs_2_), channel_id=1, source_target_pairs={{0,2},{1,3},{2,0},{3,1},{4,6},{5,7},{6,4},{7,5},{8,10},{9,11},{10,... | collective-permute-start | bytes 2359304 | tf_op jit(solution)/shard_map/ppermute | solution.py:610
  83.1 2.3 %collective-permute-start.18 = (bf16[512,512]{1,0:T(8,128)(2,1)}, bf16[512,512]{1,0:T(8,128)(2,1)}, u32[]{:S(2)}, u32[]{:S(2)}) collective-permute-start(bf16[512,512]{1,0:T(8,128)(2,1)} %multiply_convert_fusion.1.refs_3_), channel_id=1, source_target_pairs={{0,1},{1,0},{2,3},{3,2},{4,5},{5,4},{6,7},{7,6},{8,9},{9,8},{10,11... | collective-permute-start | bytes 1572872 | tf_op jit(solution)/shard_map/ppermute | solution.py:465
  100.7 2.6 %collective-permute-start.20 = (bf16[512,768]{1,0:T(8,128)(2,1)}, bf16[512,768]{1,0:T(8,128)(2,1)}, u32[]{:S(2)}, u32[]{:S(2)}) collective-permute-start(bf16[512,768]{1,0:T(8,128)(2,1)} %collective-permute-done.19.refs_3_), channel_id=1, source_target_pairs={{0,1},{1,0},{2,3},{3,2},{4,5},{5,4},{6,7},{7,6},{8,9},{9,8},{10,11... | collective-permute-start | bytes 2359304 | tf_op jit(solution)/shard_map/ppermute | solution.py:465
  100.7 14.5 %collective-permute-start.21 = (bf16[512,512]{1,0:T(8,128)(2,1)}, bf16[512,512]{1,0:T(8,128)(2,1)S(1)}, u32[]{:S(2)}, u32[]{:S(2)}) collective-permute-start(bf16[512,512]{1,0:T(8,128)(2,1)} %multiply_convert_fusion.1.refs_3_), channel_id=1, source_target_pairs={{0,2},{1,3},{2,0},{3,1},{4,6},{5,7},{6,4},{7,5},{8,10},{9,11},{10,... | collective-permute-start | bytes 1572872 | tf_op jit(solution)/shard_map/ppermute | solution.py:610
  115.2 1.9 %collective-permute-start.22 = (bf16[512,512]{1,0:T(8,128)(2,1)S(1)}, bf16[512,512]{1,0:T(8,128)(2,1)S(1)}, u32[]{:S(2)}, u32[]{:S(2)}) collective-permute-start(bf16[512,512]{1,0:T(8,128)(2,1)S(1)} %collective-permute-done.21.refs_5_), channel_id=1, source_target_pairs={{0,1},{1,0},{2,3},{3,2},{4,5},{5,4},{6,7},{7,6},{8,9},{9,8},{10,11... | collective-permute-start | bytes 1572872 | tf_op jit(solution)/shard_map/ppermute | solution.py:465
  121.9 8.4 %collective-permute-start.23 = (bf16[8,128,128]{2,1,0:T(8,128)(2,1)S(1)}, bf16[8,128,128]{2,1,0:T(8,128)(2,1)S(1)}, u32[]{:S(2)}, u32[]{:S(2)}) collective-permute-start(bf16[8,128,128]{2,1,0:T(8,128)(2,1)S(1)} %get-tuple-element.93.refs_9_), channel_id=1, source_target_pairs={{0,4},{4,0},{8,12},{12,8},{16,20},{20,16},{24,28},{28,24},{1,5},{5... | collective-permute-start | bytes 786440 | tf_op jit(solution)/shard_map/ppermute | solution.py:465
  130.3 7.9 %copy-start.10 = (bf16[8,128,128]{2,1,0:T(8,128)(2,1)}, bf16[8,128,128]{2,1,0:T(8,128)(2,1)S(1)}, u32[]{:S(2)}) copy-start(bf16[8,128,128]{2,1,0:T(8,128)(2,1)S(1)} %collective-permute-done.23) | copy-start | bytes 786436
  130.4 7.8 %collective-permute-start.24 = (bf16[8,128,128]{2,1,0:T(8,128)(2,1)S(1)}, bf16[8,128,128]{2,1,0:T(8,128)(2,1)S(1)}, u32[]{:S(2)}, u32[]{:S(2)}) collective-permute-start(bf16[8,128,128]{2,1,0:T(8,128)(2,1)S(1)} %fusion.6.refs_6_), channel_id=1, source_target_pairs={{0,8},{4,12},{8,0},{12,4},{16,24},{20,28},{24,16},{28,20},{1,9},{5... | collective-permute-start | bytes 786440 | tf_op jit(solution)/shard_map/ppermute | solution.py:465
  138.3 14.7 %collective-permute-start.25 = (bf16[8,128,128]{2,1,0:T(8,128)(2,1)S(1)}, bf16[8,128,128]{2,1,0:T(8,128)(2,1)S(1)}, u32[]{:S(2)}, u32[]{:S(2)}) collective-permute-start(bf16[8,128,128]{2,1,0:T(8,128)(2,1)S(1)} %fusion.4.refs_7_), channel_id=1, source_target_pairs={{0,16},{4,20},{8,24},{12,28},{16,0},{20,4},{24,8},{28,12},{1,17},{... | collective-permute-start | bytes 786440 | tf_op jit(solution)/shard_map/ppermute | solution.py:465
  149.3 3.7 %copy-start.11 = (bf16[8,128,128]{2,1,0:T(8,128)(2,1)S(1)}, bf16[8,128,128]{2,1,0:T(8,128)(2,1)}, u32[]{:S(2)}) copy-start(bf16[8,128,128]{2,1,0:T(8,128)(2,1)} %copy-done.10) | copy-start | bytes 786436
  149.3 5.2 %copy-start.1 = (bf16[512,2048]{1,0:T(8,128)(2,1)S(1)}, bf16[512,2048]{1,0:T(8,128)(2,1)}, u32[]{:S(2)}) copy-start(bf16[512,2048]{1,0:T(8,128)(2,1)} %refs_1_.21) | copy-start | bytes 6291460
  149.3 5.2 %copy-start.2 = (bf16[512,2048]{1,0:T(8,128)(2,1)S(1)}, bf16[512,2048]{1,0:T(8,128)(2,1)}, u32[]{:S(2)}) copy-start(bf16[512,2048]{1,0:T(8,128)(2,1)} %refs_2_.17) | copy-start | bytes 6291460
  153.0 1.6 copy-start.3
  153.2 7.0 %collective-permute-start.26 = (bf16[8,128,128]{2,1,0:T(8,128)(2,1)S(1)}, bf16[8,128,128]{2,1,0:T(8,128)(2,1)S(1)}, u32[]{:S(2)}, u32[]{:S(2)}) collective-permute-start(bf16[8,128,128]{2,1,0:T(8,128)(2,1)S(1)} %get-tuple-element.120), channel_id=1, source_target_pairs={{0,4},{4,0},{8,12},{12,8},{16,20},{20,16},{24,28},{28,24},{1,5},{5... | collective-permute-start | bytes 786440 | tf_op jit(solution)/shard_map/ppermute | solution.py:465
  154.6 1.2 copy-start.4
  155.8 4.5 %copy-start.7 = (bf16[512,1024]{1,0:T(8,128)(2,1)S(1)}, bf16[512,1024]{1,0:T(8,128)(2,1)}, u32[]{:S(2)}) copy-start(bf16[512,1024]{1,0:T(8,128)(2,1)} %get-tuple-element.110.refs_4_) | copy-start | bytes 3145732
  155.8 4.5 %copy-start.8 = (bf16[512,1024]{1,0:T(8,128)(2,1)S(1)}, bf16[512,1024]{1,0:T(8,128)(2,1)}, u32[]{:S(2)}) copy-start(bf16[512,1024]{1,0:T(8,128)(2,1)} %get-tuple-element.111.refs_5_) | copy-start | bytes 3145732

commit v6 on v5

--- a/solution.py
+++ b/solution.py
@@ -693,14 +693,14 @@
 
     groups = half_heads // math.gcd(half_heads, 2)
     split = max(1, groups * 3 // 4)
-    order = [("mine", 0, split), ("theirs", 0, groups), ("mine", split, groups)]
+    order = [("mine", split, groups), ("mine", 0, split), ("theirs", 0, groups)]
 
     def beside_backward(step):
         def run(after):
             if step == 0:
-                return [r_mine]
-            todo = order[: step if step < 3 else 0]
-            del order[: len(todo)]
+                after = [r_mine]
+            todo = order[:1]
+            del order[:1]
             for name, lo, hi in todo:
                 if lo < hi:
                     after = back(name, lo, hi, after)

time: 164 us -> 165 us (level)
  waiting for transfers between devices: 28.8 us -> 32.4 us
    ppermute x22, waiting for transfers between devices: 18.5 us -> 22.1 us  [swap(): return lax.ppermute(array, axis, [(i, i ^ 1 << bit) for i in range(size)])]
  transfers between devices with their start and end apart: 27 -> 27, of which waited for: 15 -> 16; matrix products, arithmetic and copies ran while one was open for 3% -> 3% of each run, Pallas kernels for 50% -> 50%
where the time goes in v6:
time: 165 us; the launch traced here: 164 us
  Pallas kernels  94.9 us (58%)
  waiting for transfers between devices  32.4 us (20%)
  starting transfers between devices  28.1 us (17%)
  other arithmetic  3.91 us (2%)
  local copies, waits for them, and re-layouts  3.43 us (2%)
  between operations  1.68 us (1%)
    pallas_call x20, Pallas kernels, call(): kernel(*(table[n] for n, _ in at), *args, *after)  94.9 us
    ppermute x22, starting transfers between devices, swap(): return lax.ppermute(array, axis, [(i, i ^ 1 << bit) for i in range(size)])  22.9 us
    ppermute x22, waiting for transfers between devices, swap(): return lax.ppermute(array, axis, [(i, i ^ 1 << bit) for i in range(size)])  22.1 us
    ppermute x5, waiting for transfers between devices, shift(): lax.ppermute(array, 'head', [(i, (i + 2 * by) % size) for i in range(size)])  10.2 us
    ppermute x5, starting transfers between devices, shift(): lax.ppermute(array, 'head', [(i, (i + 2 * by) % size) for i in range(size)])  5.2 us
  transfers between devices with their start and end apart: 27, of which 16 were waited for; matrix products, arithmetic and copies ran while one was open for 3% of the time, Pallas kernels for 50%

profile of v6, /device:TPU:0, one launch (start us, length us, event | category | flops | bytes accessed | tf_op | source)
XLA Modules:
  0.0 164.3 jit_solution(15194602088307953827)
XLA Ops:
  1.1 2.0 %shard_map.85 = (bf16[4,128,128]{2,1,0:T(8,128)(2,1)S(1)}, bf16[4,128,128]{2,1,0:T(8,128)(2,1)S(1)}) custom-call(s32[1]{0:T(128)} %bitcast.refs_0_.refs_1_, bf16[512,2048]{1,0:T(8,128)(2,1)} %refs_1_.21, bf16[512,2048]{1,0:T(8,128)(2,1)} %refs_2_.17), custom_call_target="tpu_custom_call" | custom-call | flops 1 | bytes 1 | tf_op jit(solution)/shard_map/pallas_call | solution.py:73
  3.1 2.6 %collective-permute-start.3 = (bf16[4,128,128]{2,1,0:T(8,128)(2,1)S(1)}, bf16[4,128,128]{2,1,0:T(8,128)(2,1)S(1)}, u32[]{:S(2)}, u32[]{:S(2)}) collective-permute-start(bf16[4,128,128]{2,1,0:T(8,128)(2,1)S(1)} %get-tuple-element.61.refs_3_), channel_id=1, source_target_pairs={{0,4},{4,0},{8,12},{12,8},{16,20},{20,16},{24,28},{28,24},{1,5},{5... | collective-permute-start | bytes 393224 | tf_op jit(solution)/shard_map/ppermute | solution.py:465
  5.8 2.0 %shard_map.86 = (bf16[4,128,128]{2,1,0:T(8,128)(2,1)S(1)}, bf16[4,128,128]{2,1,0:T(8,128)(2,1)S(1)}) custom-call(s32[1]{0:T(128)} %bitcast.5.refs_0_, bf16[512,2048]{1,0:T(8,128)(2,1)} %refs_1_.21, bf16[512,2048]{1,0:T(8,128)(2,1)} %refs_2_.17, bf16[4,128,128]{2,1,0:T(8,128)(2,1)S(1)} %get-tuple-element.61.refs_3_), custom_call_target="tpu_custom_call" | custom-call | flops 1 | bytes 1 | tf_op jit(solution)/shard_map/pallas_call | solution.py:73
  8.5 1.6 collective-permute-done.3
  10.1 2.1 %collective-permute-start.4 = (bf16[4,128,128]{2,1,0:T(8,128)(2,1)S(1)}, bf16[4,128,128]{2,1,0:T(8,128)(2,1)S(1)}, u32[]{:S(2)}, u32[]{:S(2)}) collective-permute-start(bf16[4,128,128]{2,1,0:T(8,128)(2,1)S(1)} %fusion.20), channel_id=1, source_target_pairs={{0,8},{4,12},{8,0},{12,4},{16,24},{20,28},{24,16},{28,20},{1,9},{5... | collective-permute-start | bytes 393224 | tf_op jit(solution)/shard_map/ppermute | solution.py:465
  12.7 1.9 %collective-permute-start.1 = (bf16[4,128,128]{2,1,0:T(8,128)(2,1)S(1)}, bf16[4,128,128]{2,1,0:T(8,128)(2,1)S(1)}, u32[]{:S(2)}, u32[]{:S(2)}) collective-permute-start(bf16[4,128,128]{2,1,0:T(8,128)(2,1)S(1)} %fusion.19), channel_id=1, source_target_pairs={{0,8},{4,12},{8,0},{12,4},{16,24},{20,28},{24,16},{28,20},{1,9},{5... | collective-permute-start | bytes 393224 | tf_op jit(solution)/shard_map/ppermute | solution.py:465
  15.3 3.3 %collective-permute-start.5 = (bf16[4,128,128]{2,1,0:T(8,128)(2,1)S(1)}, bf16[4,128,128]{2,1,0:T(8,128)(2,1)S(1)}, u32[]{:S(2)}, u32[]{:S(2)}) collective-permute-start(bf16[4,128,128]{2,1,0:T(8,128)(2,1)S(1)} %fusion.17.refs_4_), channel_id=1, source_target_pairs={{0,16},{4,20},{8,24},{12,28},{16,0},{20,4},{24,8},{28,12},{1,17},{... | collective-permute-start | bytes 393224 | tf_op jit(solution)/shard_map/ppermute | solution.py:465
  19.2 1.6 collective-permute-start.6
  20.9 1.2 collective-permute-start.2
  22.1 4.6 %shard_map.87 = (f32[512,1024]{1,0:T(8,128)}, f32[8,128]{1,0:T(8,128)S(1)}) custom-call(s32[1]{0:T(128)} %bitcast.5.refs_0_, bf16[512,2048]{1,0:T(8,128)(2,1)} %refs_1_.19, bf16[512,2048]{1,0:T(8,128)(2,1)} %refs_1_.21, bf16[512,2048]{1,0:T(8,128)(2,1)} %refs_2_.17, bf16[4,128,128]{2,1,0:T(8,128)(2,1)S(1)} %fusion.17.refs_4_), custom_call_target="tpu_custom_call" | custom-call | flops 1 | bytes 1 | tf_op jit(solution)/shard_map/pallas_call | solution.py:73
  26.7 1.6 collective-permute-start.8
  28.4 1.2 collective-permute-done.2
  29.6 1.7 %collective-permute-start.7 = (bf16[4,128,128]{2,1,0:T(8,128)(2,1)S(1)}, bf16[4,128,128]{2,1,0:T(8,128)(2,1)S(1)}, u32[]{:S(2)}, u32[]{:S(2)}) collective-permute-start(bf16[4,128,128]{2,1,0:T(8,128)(2,1)S(1)} %get-tuple-element.125.refs_4_), channel_id=1, source_target_pairs={{0,4},{4,0},{8,12},{12,8},{16,20},{20,16},{24,28},{28,24},{1,5},{5... | collective-permute-start | bytes 393224 | tf_op jit(solution)/shard_map/ppermute | solution.py:465
  31.3 4.6 %shard_map.88 = (f32[512,1024]{1,0:T(8,128)}, f32[8,128]{1,0:T(8,128)S(1)}) custom-call(s32[1]{0:T(128)} %bitcast.refs_0_.refs_1_, bf16[512,2048]{1,0:T(8,128)(2,1)} %refs_1_.19, bf16[512,2048]{1,0:T(8,128)(2,1)} %refs_1_.21, bf16[512,2048]{1,0:T(8,128)(2,1)} %refs_2_.17, bf16[4,128,128]{2,1,0:T(8,128)(2,1)S(1)} %get-tuple-element.125.refs_4_, ...), custom_call_target="tpu_custom_call" | custom-call | flops 1 | bytes 1 | tf_op jit(solution)/shard_map/pallas_call | solution.py:73
  37.1 1.6 %shard_map.89.refs_3_ = bf16[512,1024]{1,0:T(8,128)(2,1)} custom-call(s32[1]{0:T(128)} %bitcast.5.refs_0_, bf16[512,2048]{1,0:T(8,128)(2,1)S(1)} %copy-done, f32[512,1024]{1,0:T(8,128)S(1)} %copy-done.5, bf16[4,128,128]{2,1,0:T(8,128)(2,1)S(1)} %get-tuple-element.126.refs_3_, bf16[4,128,128]{2,1,0:T(8,128)(2,1)S(1)} %get-tuple-element.124.refs_4_), custom_call_target="tpu_custom_call" | custom-call | flops 1 | bytes 1 | tf_op jit(solution)/shard_map/pallas_call | solution.py:73
  38.8 2.3 %collective-permute-done.10 = s32[8,128]{1,0:T(8,128)S(1)} collective-permute-done((s32[8,128]{1,0:T(8,128)S(1)}, s32[8,128]{1,0:T(8,128)S(1)}, u32[]{:S(2)}, u32[]{:S(2)}) %collective-permute-start.10) | collective-permute-done | bytes 4128 | tf_op jit(solution)/shard_map/ppermute | solution.py:465
  41.1 1.0 shard_map.90.refs_5_
  42.2 2.7 %collective-permute-done.12.refs_6_ = bf16[512,1024]{1,0:T(8,128)(2,1)} collective-permute-done((bf16[512,1024]{1,0:T(8,128)(2,1)S(1)}, bf16[512,1024]{1,0:T(8,128)(2,1)}, u32[]{:S(2)}, u32[]{:S(2)}) %collective-permute-start.12) | collective-permute-done | bytes 1048608 | tf_op jit(solution)/shard_map/ppermute | solution.py:465
  44.9 5.8 %shard_map.91.refs_9_ = bf16[512,512]{1,0:T(8,128)(2,1)} custom-call(s32[1]{0:T(128)} %bitcast.5.refs_0_, s32[1]{0:T(128)} %bitcast.refs_0_.refs_1_, s32[1]{0:T(128)} %bitcast.1.refs_2_.refs_0_.refs_1_, bf16[512,1024]{1,0:T(8,128)(2,1)} %shard_map.89.refs_3_, bf16[512,1024]{1,0:T(8,128)(2,1)} %collective-permute-done.11.refs_4_, ...), custom_call_target="tpu_custom_call" | custom-call | flops 1 | bytes 1 | tf_op jit(solution)/shard_map/pallas_call | solution.py:73
  50.8 1.7 %collective-permute-start.14 = (bf16[512,512]{1,0:T(8,128)(2,1)}, bf16[512,512]{1,0:T(8,128)(2,1)}, u32[]{:S(2)}, u32[]{:S(2)}) collective-permute-start(bf16[512,512]{1,0:T(8,128)(2,1)} %shard_map.91.refs_9_), channel_id=1, source_target_pairs={{0,2},{1,3},{2,0},{3,1},{4,6},{5,7},{6,4},{7,5},{8,10},{9,11},{10,... | collective-permute-start | bytes 1572872 | tf_op jit(solution)/shard_map/ppermute | solution.py:610
  52.5 5.1 %shard_map.92.refs_9_ = bf16[512,512]{1,0:T(8,128)(2,1)S(1)} custom-call(s32[1]{0:T(128)} %bitcast.5.refs_0_, s32[1]{0:T(128)} %bitcast.refs_0_.refs_1_, s32[1]{0:T(128)} %bitcast.3.refs_2_.refs_0_, bf16[512,1024]{1,0:T(8,128)(2,1)} %shard_map.89.refs_3_, bf16[512,1024]{1,0:T(8,128)(2,1)} %collective-permute-done.11.refs_4_, ...), custom_call_target="tpu_custom_call" | custom-call | flops 1 | bytes 1 | tf_op jit(solution)/shard_map/pallas_call | solution.py:73
  57.6 5.1 %shard_map.93.refs_9_ = bf16[512,512]{1,0:T(8,128)(2,1)S(1)} custom-call(s32[1]{0:T(128)} %bitcast.5.refs_0_, s32[1]{0:T(128)} %bitcast.refs_0_.refs_1_, s32[1]{0:T(128)} %bitcast.1.refs_2_.refs_0_.refs_1_, bf16[512,1024]{1,0:T(8,128)(2,1)} %shard_map.89.refs_3_, bf16[512,1024]{1,0:T(8,128)(2,1)} %collective-permute-done.11.refs_4_, ...), custom_call_target="tpu_custom_call" | custom-call | flops 1 | bytes 1 | tf_op jit(solution)/shard_map/pallas_call | solution.py:73
  65.1 3.7 %shard_map.94.refs_9_ = bf16[512,256]{1,0:T(8,128)(2,1)S(1)} custom-call(s32[1]{0:T(128)} %bitcast.5.refs_0_, s32[1]{0:T(128)} %bitcast.refs_0_.refs_1_, s32[1]{0:T(128)} %bitcast.1.refs_2_.refs_0_.refs_1_, bf16[512,1024]{1,0:T(8,128)(2,1)} %shard_map.89.refs_3_, bf16[512,1024]{1,0:T(8,128)(2,1)} %collective-permute-done.11.refs_4_, ...), custom_call_target="tpu_custom_call" | custom-call | flops 1 | bytes 1 | tf_op jit(solution)/shard_map/pallas_call | solution.py:73
  68.8 2.5 %collective-permute-start.16 = (bf16[512,256]{1,0:T(8,128)(2,1)S(1)}, bf16[512,256]{1,0:T(8,128)(2,1)S(1)}, u32[]{:S(2)}, u32[]{:S(2)}) collective-permute-start(bf16[512,256]{1,0:T(8,128)(2,1)S(1)} %shard_map.94.refs_9_), channel_id=1, source_target_pairs={{0,2},{1,3},{2,0},{3,1},{4,6},{5,7},{6,4},{7,5},{8,10},{9,11},{10,... | collective-permute-start | bytes 786440 | tf_op jit(solution)/shard_map/ppermute | solution.py:610
  71.4 6.5 %shard_map.95 = bf16[512,768]{1,0:T(8,128)(2,1)S(1)} custom-call(s32[1]{0:T(128)} %bitcast.5.refs_0_, s32[1]{0:T(128)} %bitcast.refs_0_.refs_1_, s32[1]{0:T(128)} %bitcast.3.refs_2_.refs_0_, bf16[512,1024]{1,0:T(8,128)(2,1)} %shard_map.89.refs_3_, bf16[512,1024]{1,0:T(8,128)(2,1)} %collective-permute-done.11.refs_4_, ...), custom_call_target="tpu_custom_call" | custom-call | flops 1 | bytes 1 | tf_op jit(solution)/shard_map/pallas_call | solution.py:73
  77.9 1.2 copy-done.12
  79.2 1.4 multiply_convert_fusion.refs_2_
  80.9 1.1 collective-permute-done.16
  82.1 1.0 multiply_convert_fusion.1.refs_3_
  83.1 0.9 constant_dynamic-update-slice_fusion.refs_8_.refs_5_
  84.1 1.3 collective-permute-done.18.refs_6_
  85.3 10.1 %shard_map.96 = (f32[512,2048]{1,0:T(8,128)}, f32[8,128]{1,0:T(8,128)S(1)}) custom-call(s32[1]{0:T(128)} %bitcast.3.refs_2_.refs_0_, s32[1]{0:T(128)} %bitcast.4.refs_1_, bf16[512,768]{1,0:T(8,128)(2,1)S(1)} %multiply_convert_fusion.refs_2_, bf16[512,512]{1,0:T(8,128)(2,1)} %multiply_convert_fusion.1.refs_3_, bf16[2048,5120]{1,0:T(8,128)(2,1)} %refs_8_.3, ...), custom_call_target="tpu_custom_call" | custom-call | flops 1 | bytes 1 | tf_op jit(solution)/shard_map/pallas_call | solution.py:73
  95.5 5.2 %collective-permute-done.19.refs_3_ = bf16[512,768]{1,0:T(8,128)(2,1)} collective-permute-done((bf16[512,768]{1,0:T(8,128)(2,1)S(1)}, bf16[512,768]{1,0:T(8,128)(2,1)}, u32[]{:S(2)}, u32[]{:S(2)}) %collective-permute-start.19) | collective-permute-done | bytes 786464 | tf_op jit(solution)/shard_map/ppermute | solution.py:610
  101.0 2.4 %collective-permute-done.20.refs_5_ = bf16[512,768]{1,0:T(8,128)(2,1)} collective-permute-done((bf16[512,768]{1,0:T(8,128)(2,1)}, bf16[512,768]{1,0:T(8,128)(2,1)}, u32[]{:S(2)}, u32[]{:S(2)}) %collective-permute-start.20) | collective-permute-done | bytes 786464 | tf_op jit(solution)/shard_map/ppermute | solution.py:465
  103.3 8.9 %shard_map.97 = (f32[512,2048]{1,0:T(8,128)}, f32[8,128]{1,0:T(8,128)S(1)}) custom-call(s32[1]{0:T(128)} %bitcast.1.refs_2_.refs_0_.refs_1_, s32[1]{0:T(128)} %bitcast.2.refs_1_.refs_2_, f32[512,2048]{1,0:T(8,128)} %get-tuple-element.85.refs_2_, bf16[512,768]{1,0:T(8,128)(2,1)} %collective-permute-done.19.refs_3_, bf16[2048,5120]{1,0:T(8,128)(2,1)} %refs_8_.3, ...), custom_call_target="tpu_custom_call" | custom-call | flops 1 | bytes 1 | tf_op jit(solution)/shard_map/pallas_call | solution.py:73
  112.2 3.1 %collective-permute-done.21.refs_5_ = bf16[512,512]{1,0:T(8,128)(2,1)S(1)} collective-permute-done((bf16[512,512]{1,0:T(8,128)(2,1)}, bf16[512,512]{1,0:T(8,128)(2,1)S(1)}, u32[]{:S(2)}, u32[]{:S(2)}) %collective-permute-start.21) | collective-permute-done | bytes 524320 | tf_op jit(solution)/shard_map/ppermute | solution.py:610
  115.2 1.9 %collective-permute-done.22.refs_7_ = bf16[512,512]{1,0:T(8,128)(2,1)S(1)} collective-permute-done((bf16[512,512]{1,0:T(8,128)(2,1)S(1)}, bf16[512,512]{1,0:T(8,128)(2,1)S(1)}, u32[]{:S(2)}, u32[]{:S(2)}) %collective-permute-start.22) | collective-permute-done | bytes 524320 | tf_op jit(solution)/shard_map/ppermute | solution.py:465
  117.1 4.8 %shard_map.98 = (bf16[512,1024]{1,0:T(8,128)(2,1)}, bf16[8,128,128]{2,1,0:T(8,128)(2,1)S(1)}) custom-call(s32[1]{0:T(128)} %bitcast.refs_0_.refs_1_, s32[1]{0:T(128)} %bitcast.1.refs_2_.refs_0_.refs_1_, s32[1]{0:T(128)} %bitcast.2.refs_1_.refs_2_, f32[512,2048]{1,0:T(8,128)} %get-tuple-element.89.refs_3_, bf16[512,2048]{1,0:T(8,128)(2,1)S(1)} %copy-done, ...), custom_call_target="tpu_custom_call" | custom-call | flops 1 | bytes 1 | tf_op jit(solution)/shard_map/pallas_call | solution.py:73
  121.9 1.4 collective-permute-start.23
  123.3 4.8 %shard_map.99 = (bf16[512,1024]{1,0:T(8,128)(2,1)}, bf16[8,128,128]{2,1,0:T(8,128)(2,1)S(1)}) custom-call(s32[1]{0:T(128)} %bitcast.5.refs_0_, s32[1]{0:T(128)} %bitcast.1.refs_2_.refs_0_.refs_1_, s32[1]{0:T(128)} %bitcast.2.refs_1_.refs_2_, f32[512,2048]{1,0:T(8,128)} %get-tuple-element.89.refs_3_, bf16[512,2048]{1,0:T(8,128)(2,1)S(1)} %copy-done, ...), custom_call_target="tpu_custom_call" | custom-call | flops 1 | bytes 1 | tf_op jit(solution)/shard_map/pallas_call | solution.py:73
  128.2 3.5 %shard_map.100 = (f32[512,2048]{1,0:T(8,128)}, bf16[512,1024]{1,0:T(8,128)(2,1)}, bf16[512,1024]{1,0:T(8,128)(2,1)}, f32[8,128]{1,0:T(8,128)S(1)}) custom-call(s32[1]{0:T(128)} %bitcast.5.refs_0_, bf16[512,2048]{1,0:T(8,128)(2,1)} %refs_1_.19, bf16[512,2048]{1,0:T(8,128)(2,1)} %refs_1_.21, bf16[512,2048]{1,0:T(8,128)(2,1)} %refs_2_.17, ...), custom_call_target="tpu_custom_call" | custom-call | flops 1 | bytes 1 | tf_op jit(solution)/shard_map/pallas_call | solution.py:73
  132.5 6.9 %shard_map.101 = (f32[512,2048]{1,0:T(8,128)}, bf16[512,1024]{1,0:T(8,128)(2,1)}, bf16[512,1024]{1,0:T(8,128)(2,1)}, f32[8,128]{1,0:T(8,128)S(1)}) custom-call(s32[1]{0:T(128)} %bitcast.5.refs_0_, bf16[512,2048]{1,0:T(8,128)(2,1)} %refs_1_.19, bf16[512,2048]{1,0:T(8,128)(2,1)} %refs_1_.21, ...), custom_call_target="tpu_custom_call", output_to_operand_aliasing={{0}: (6, {}), {1}: (7, {}), {2}: (8, {})} | custom-call | flops 1 | bytes 1 | tf_op jit(solution)/shard_map/pallas_call | solution.py:73
  140.0 2.0 %collective-permute-start.25 = (bf16[8,128,128]{2,1,0:T(8,128)(2,1)S(1)}, bf16[8,128,128]{2,1,0:T(8,128)(2,1)S(1)}, u32[]{:S(2)}, u32[]{:S(2)}) collective-permute-start(bf16[8,128,128]{2,1,0:T(8,128)(2,1)S(1)} %fusion.4.refs_7_), channel_id=1, source_target_pairs={{0,16},{4,20},{8,24},{12,28},{16,0},{20,4},{24,8},{28,12},{1,17},{... | collective-permute-start | bytes 786440 | tf_op jit(solution)/shard_map/ppermute | solution.py:465
  142.0 8.7 %shard_map.102 = (f32[512,2048]{1,0:T(8,128)}, bf16[512,1024]{1,0:T(8,128)(2,1)}, bf16[512,1024]{1,0:T(8,128)(2,1)}, f32[8,128]{1,0:T(8,128)S(1)}) custom-call(s32[1]{0:T(128)} %bitcast.refs_0_.refs_1_, bf16[512,2048]{1,0:T(8,128)(2,1)} %refs_1_.19, bf16[512,2048]{1,0:T(8,128)(2,1)} %refs_1_.21, ...), custom_call_target="tpu_custom_call", output_to_operand_aliasing={{0}: (6, {})} | custom-call | flops 1 | bytes 1 | tf_op jit(solution)/shard_map/pallas_call | solution.py:73
  150.7 3.2 %collective-permute-done.25 = bf16[8,128,128]{2,1,0:T(8,128)(2,1)S(1)} collective-permute-done((bf16[8,128,128]{2,1,0:T(8,128)(2,1)S(1)}, bf16[8,128,128]{2,1,0:T(8,128)(2,1)S(1)}, u32[]{:S(2)}, u32[]{:S(2)}) %collective-permute-start.25) | collective-permute-done | bytes 262176 | tf_op jit(solution)/shard_map/ppermute | solution.py:465
  155.0 2.7 %shard_map.103 = (f32[512,2048]{1,0:T(8,128)}, f32[512,2048]{1,0:T(8,128)}) custom-call(s32[1]{0:T(128)} %bitcast.5.refs_0_, bf16[512,2048]{1,0:T(8,128)(2,1)S(1)} %copy-done.1, bf16[512,2048]{1,0:T(8,128)(2,1)S(1)} %copy-done.2, bf16[8,128,128]{2,1,0:T(8,128)(2,1)S(1)} %get-tuple-element.119.refs_3_.refs_7_, bf16[512,1024]{1,0:T(8,128)(2,1)S(1)} %copy-done.3, ...), custom_call_target="tpu_custom_call" | custom-call | flops 1 | bytes 1 | tf_op jit(solution)/shard_map/pallas_call | solution.py:73
  157.7 3.9 %collective-permute-done.26.refs_3_ = bf16[8,128,128]{2,1,0:T(8,128)(2,1)S(1)} collective-permute-done((bf16[8,128,128]{2,1,0:T(8,128)(2,1)S(1)}, bf16[8,128,128]{2,1,0:T(8,128)(2,1)S(1)}, u32[]{:S(2)}, u32[]{:S(2)}) %collective-permute-start.26) | collective-permute-done | bytes 262176 | tf_op jit(solution)/shard_map/ppermute | solution.py:465
  161.6 2.7 %shard_map.104 = (f32[512,2048]{1,0:T(8,128)}, f32[512,2048]{1,0:T(8,128)}) custom-call(s32[1]{0:T(128)} %bitcast.refs_0_.refs_1_, bf16[512,2048]{1,0:T(8,128)(2,1)S(1)} %copy-done.1, bf16[512,2048]{1,0:T(8,128)(2,1)S(1)} %copy-done.2, bf16[8,128,128]{2,1,0:T(8,128)(2,1)S(1)} %collective-permute-done.26.refs_3_, ...), custom_call_target="tpu_custom_call", output_to_operand_aliasing={{0}: (6, {}), {1}: (7, {})} | custom-call | flops 1 | bytes 1 | tf_op jit(solution)/shard_map/pallas_call | solution.py:73
  (77 shorter events, 9.7 us)
Async XLA Ops:
  0.6 44.3 %collective-permute-start.13 = (bf16[2048,5120]{1,0:T(8,128)(2,1)}, bf16[2048,5120]{1,0:T(8,128)(2,1)}, u32[]{:S(2)}, u32[]{:S(2)}) collective-permute-start(bf16[2048,5120]{1,0:T(8,128)(2,1)} %refs_8_.3), channel_id=1, source_target_pairs={{0,1},{1,0},{2,3},{3,2},{4,5},{5,4},{6,7},{7,6},{8,9},{9,8},{10,11... | collective-permute-start | bytes 62914568 | tf_op jit(solution)/shard_map/ppermute | solution.py:465
  3.1 7.0 %collective-permute-start.3 = (bf16[4,128,128]{2,1,0:T(8,128)(2,1)S(1)}, bf16[4,128,128]{2,1,0:T(8,128)(2,1)S(1)}, u32[]{:S(2)}, u32[]{:S(2)}) collective-permute-start(bf16[4,128,128]{2,1,0:T(8,128)(2,1)S(1)} %get-tuple-element.61.refs_3_), channel_id=1, source_target_pairs={{0,4},{4,0},{8,12},{12,8},{16,20},{20,16},{24,28},{28,24},{1,5},{5... | collective-permute-start | bytes 393224 | tf_op jit(solution)/shard_map/ppermute | solution.py:465
  5.7 6.9 %collective-permute-start = (bf16[4,128,128]{2,1,0:T(8,128)(2,1)S(1)}, bf16[4,128,128]{2,1,0:T(8,128)(2,1)S(1)}, u32[]{:S(2)}, u32[]{:S(2)}) collective-permute-start(bf16[4,128,128]{2,1,0:T(8,128)(2,1)S(1)} %get-tuple-element.63), channel_id=1, source_target_pairs={{0,4},{4,0},{8,12},{12,8},{16,20},{20,16},{24,28},{28,24},{1,5},{5... | collective-permute-start | bytes 393224 | tf_op jit(solution)/shard_map/ppermute | solution.py:465
  5.8 2.0 %copy-start.13 = (s32[512]{0:T(512)S(1)}, s32[512]{0:T(512)}, u32[]{:S(2)}) copy-start(s32[512]{0:T(512)} %param.11) | copy-start | bytes 6148
  10.1 5.1 %collective-permute-start.4 = (bf16[4,128,128]{2,1,0:T(8,128)(2,1)S(1)}, bf16[4,128,128]{2,1,0:T(8,128)(2,1)S(1)}, u32[]{:S(2)}, u32[]{:S(2)}) collective-permute-start(bf16[4,128,128]{2,1,0:T(8,128)(2,1)S(1)} %fusion.20), channel_id=1, source_target_pairs={{0,8},{4,12},{8,0},{12,4},{16,24},{20,28},{24,16},{28,20},{1,9},{5... | collective-permute-start | bytes 393224 | tf_op jit(solution)/shard_map/ppermute | solution.py:465
  12.7 8.1 %collective-permute-start.1 = (bf16[4,128,128]{2,1,0:T(8,128)(2,1)S(1)}, bf16[4,128,128]{2,1,0:T(8,128)(2,1)S(1)}, u32[]{:S(2)}, u32[]{:S(2)}) collective-permute-start(bf16[4,128,128]{2,1,0:T(8,128)(2,1)S(1)} %fusion.19), channel_id=1, source_target_pairs={{0,8},{4,12},{8,0},{12,4},{16,24},{20,28},{24,16},{28,20},{1,9},{5... | collective-permute-start | bytes 393224 | tf_op jit(solution)/shard_map/ppermute | solution.py:465
  15.3 13.0 %collective-permute-start.5 = (bf16[4,128,128]{2,1,0:T(8,128)(2,1)S(1)}, bf16[4,128,128]{2,1,0:T(8,128)(2,1)S(1)}, u32[]{:S(2)}, u32[]{:S(2)}) collective-permute-start(bf16[4,128,128]{2,1,0:T(8,128)(2,1)S(1)} %fusion.17.refs_4_), channel_id=1, source_target_pairs={{0,16},{4,20},{8,24},{12,28},{16,0},{20,4},{24,8},{28,12},{1,17},{... | collective-permute-start | bytes 393224 | tf_op jit(solution)/shard_map/ppermute | solution.py:465
  19.2 7.4 %collective-permute-start.6 = (s32[8,128]{1,0:T(8,128)S(1)}, s32[8,128]{1,0:T(8,128)S(1)}, u32[]{:S(2)}, u32[]{:S(2)}) collective-permute-start(s32[8,128]{1,0:T(8,128)S(1)} %broadcast_in_dim.49), channel_id=1, source_target_pairs={{0,4},{4,0},{8,12},{12,8},{16,20},{20,16},{24,28},{28,24},{1,5},{5... | collective-permute-start | bytes 12296 | tf_op jit(solution)/shard_map/ppermute | solution.py:465
  20.9 8.7 %collective-permute-start.2 = (bf16[4,128,128]{2,1,0:T(8,128)(2,1)S(1)}, bf16[4,128,128]{2,1,0:T(8,128)(2,1)S(1)}, u32[]{:S(2)}, u32[]{:S(2)}) collective-permute-start(bf16[4,128,128]{2,1,0:T(8,128)(2,1)S(1)} %fusion.12), channel_id=1, source_target_pairs={{0,16},{4,20},{8,24},{12,28},{16,0},{20,4},{24,8},{28,12},{1,17},{... | collective-permute-start | bytes 393224 | tf_op jit(solution)/shard_map/ppermute | solution.py:465
  26.7 9.2 %collective-permute-start.8 = (s32[8,128]{1,0:T(8,128)S(1)}, s32[8,128]{1,0:T(8,128)S(1)}, u32[]{:S(2)}, u32[]{:S(2)}) collective-permute-start(s32[8,128]{1,0:T(8,128)S(1)} %add.95), channel_id=1, source_target_pairs={{0,8},{4,12},{8,0},{12,4},{16,24},{20,28},{24,16},{28,20},{1,9},{5... | collective-permute-start | bytes 12296 | tf_op jit(solution)/shard_map/ppermute | solution.py:465
  29.6 7.5 %copy-start = (bf16[512,2048]{1,0:T(8,128)(2,1)S(1)}, bf16[512,2048]{1,0:T(8,128)(2,1)}, u32[]{:S(2)}) copy-start(bf16[512,2048]{1,0:T(8,128)(2,1)} %refs_1_.19) | copy-start | bytes 6291460
  29.6 7.5 %copy-start.5 = (f32[512,1024]{1,0:T(8,128)S(1)}, f32[512,1024]{1,0:T(8,128)}, u32[]{:S(2)}) copy-start(f32[512,1024]{1,0:T(8,128)} %get-tuple-element.80.refs_2_) | copy-start | bytes 6291460
  29.6 6.4 %collective-permute-start.7 = (bf16[4,128,128]{2,1,0:T(8,128)(2,1)S(1)}, bf16[4,128,128]{2,1,0:T(8,128)(2,1)S(1)}, u32[]{:S(2)}, u32[]{:S(2)}) collective-permute-start(bf16[4,128,128]{2,1,0:T(8,128)(2,1)S(1)} %get-tuple-element.125.refs_4_), channel_id=1, source_target_pairs={{0,4},{4,0},{8,12},{12,8},{16,20},{20,16},{24,28},{28,24},{1,5},{5... | collective-permute-start | bytes 393224 | tf_op jit(solution)/shard_map/ppermute | solution.py:465
  36.0 5.0 %collective-permute-start.9 = (bf16[4,128,128]{2,1,0:T(8,128)(2,1)S(1)}, bf16[4,128,128]{2,1,0:T(8,128)(2,1)S(1)}, u32[]{:S(2)}, u32[]{:S(2)}) collective-permute-start(bf16[4,128,128]{2,1,0:T(8,128)(2,1)S(1)} %get-tuple-element.77), channel_id=1, source_target_pairs={{0,4},{4,0},{8,12},{12,8},{16,20},{20,16},{24,28},{28,24},{1,5},{5... | collective-permute-start | bytes 393224 | tf_op jit(solution)/shard_map/ppermute | solution.py:465
  36.6 4.5 %collective-permute-start.10 = (s32[8,128]{1,0:T(8,128)S(1)}, s32[8,128]{1,0:T(8,128)S(1)}, u32[]{:S(2)}, u32[]{:S(2)}) collective-permute-start(s32[8,128]{1,0:T(8,128)S(1)} %add.96), channel_id=1, source_target_pairs={{0,16},{4,20},{8,24},{12,28},{16,0},{20,4},{24,8},{28,12},{1,17},{... | collective-permute-start | bytes 12296 | tf_op jit(solution)/shard_map/ppermute | solution.py:465
  37.1 4.0 %copy-start.6 = (f32[512,1024]{1,0:T(8,128)S(1)}, f32[512,1024]{1,0:T(8,128)}, u32[]{:S(2)}) copy-start(f32[512,1024]{1,0:T(8,128)} %get-tuple-element.81.refs_2_) | copy-start | bytes 6291460
  38.8 3.4 %collective-permute-start.11 = (bf16[512,1024]{1,0:T(8,128)(2,1)}, bf16[512,1024]{1,0:T(8,128)(2,1)}, u32[]{:S(2)}, u32[]{:S(2)}) collective-permute-start(bf16[512,1024]{1,0:T(8,128)(2,1)} %shard_map.89.refs_3_), channel_id=1, source_target_pairs={{0,1},{1,0},{2,3},{3,2},{4,5},{5,4},{6,7},{7,6},{8,9},{9,8},{10,11... | collective-permute-start | bytes 3145736 | tf_op jit(solution)/shard_map/ppermute | solution.py:465
  41.1 1.0 copy-start.9
  42.1 2.9 %collective-permute-start.12 = (bf16[512,1024]{1,0:T(8,128)(2,1)S(1)}, bf16[512,1024]{1,0:T(8,128)(2,1)}, u32[]{:S(2)}, u32[]{:S(2)}) collective-permute-start(bf16[512,1024]{1,0:T(8,128)(2,1)S(1)} %shard_map.90.refs_5_), channel_id=1, source_target_pairs={{0,1},{1,0},{2,3},{3,2},{4,5},{5,4},{6,7},{7,6},{8,9},{9,8},{10,11... | collective-permute-start | bytes 3145736 | tf_op jit(solution)/shard_map/ppermute | solution.py:465
  50.8 14.3 %collective-permute-start.14 = (bf16[512,512]{1,0:T(8,128)(2,1)}, bf16[512,512]{1,0:T(8,128)(2,1)}, u32[]{:S(2)}, u32[]{:S(2)}) collective-permute-start(bf16[512,512]{1,0:T(8,128)(2,1)} %shard_map.91.refs_9_), channel_id=1, source_target_pairs={{0,2},{1,3},{2,0},{3,1},{4,6},{5,7},{6,4},{7,5},{8,10},{9,11},{10,... | collective-permute-start | bytes 1572872 | tf_op jit(solution)/shard_map/ppermute | solution.py:610
  62.7 15.2 %collective-permute-start.15 = (bf16[512,512]{1,0:T(8,128)(2,1)S(1)}, bf16[512,512]{1,0:T(8,128)(2,1)S(1)}, u32[]{:S(2)}, u32[]{:S(2)}) collective-permute-start(bf16[512,512]{1,0:T(8,128)(2,1)S(1)} %shard_map.93.refs_9_), channel_id=1, source_target_pairs={{0,2},{1,3},{2,0},{3,1},{4,6},{5,7},{6,4},{7,5},{8,10},{9,11},{10,... | collective-permute-start | bytes 1572872 | tf_op jit(solution)/shard_map/ppermute | solution.py:610
  68.8 13.3 %collective-permute-start.16 = (bf16[512,256]{1,0:T(8,128)(2,1)S(1)}, bf16[512,256]{1,0:T(8,128)(2,1)S(1)}, u32[]{:S(2)}, u32[]{:S(2)}) collective-permute-start(bf16[512,256]{1,0:T(8,128)(2,1)S(1)} %shard_map.94.refs_9_), channel_id=1, source_target_pairs={{0,2},{1,3},{2,0},{3,1},{4,6},{5,7},{6,4},{7,5},{8,10},{9,11},{10,... | collective-permute-start | bytes 786440 | tf_op jit(solution)/shard_map/ppermute | solution.py:610
  77.8 1.3 copy-start.12
  80.5 3.5 %collective-permute-start.17 = (bf16[512,768]{1,0:T(8,128)(2,1)S(1)}, bf16[512,768]{1,0:T(8,128)(2,1)}, u32[]{:S(2)}, u32[]{:S(2)}) collective-permute-start(bf16[512,768]{1,0:T(8,128)(2,1)S(1)} %multiply_convert_fusion.refs_2_), channel_id=1, source_target_pairs={{0,1},{1,0},{2,3},{3,2},{4,5},{5,4},{6,7},{7,6},{8,9},{9,8},{10,11... | collective-permute-start | bytes 2359304 | tf_op jit(solution)/shard_map/ppermute | solution.py:465
  80.6 20.1 %collective-permute-start.19 = (bf16[512,768]{1,0:T(8,128)(2,1)S(1)}, bf16[512,768]{1,0:T(8,128)(2,1)}, u32[]{:S(2)}, u32[]{:S(2)}) collective-permute-start(bf16[512,768]{1,0:T(8,128)(2,1)S(1)} %multiply_convert_fusion.refs_2_), channel_id=1, source_target_pairs={{0,2},{1,3},{2,0},{3,1},{4,6},{5,7},{6,4},{7,5},{8,10},{9,11},{10,... | collective-permute-start | bytes 2359304 | tf_op jit(solution)/shard_map/ppermute | solution.py:610
  83.1 2.3 %collective-permute-start.18 = (bf16[512,512]{1,0:T(8,128)(2,1)}, bf16[512,512]{1,0:T(8,128)(2,1)}, u32[]{:S(2)}, u32[]{:S(2)}) collective-permute-start(bf16[512,512]{1,0:T(8,128)(2,1)} %multiply_convert_fusion.1.refs_3_), channel_id=1, source_target_pairs={{0,1},{1,0},{2,3},{3,2},{4,5},{5,4},{6,7},{7,6},{8,9},{9,8},{10,11... | collective-permute-start | bytes 1572872 | tf_op jit(solution)/shard_map/ppermute | solution.py:465
  100.7 2.6 %collective-permute-start.20 = (bf16[512,768]{1,0:T(8,128)(2,1)}, bf16[512,768]{1,0:T(8,128)(2,1)}, u32[]{:S(2)}, u32[]{:S(2)}) collective-permute-start(bf16[512,768]{1,0:T(8,128)(2,1)} %collective-permute-done.19.refs_3_), channel_id=1, source_target_pairs={{0,1},{1,0},{2,3},{3,2},{4,5},{5,4},{6,7},{7,6},{8,9},{9,8},{10,11... | collective-permute-start | bytes 2359304 | tf_op jit(solution)/shard_map/ppermute | solution.py:465
  100.7 14.5 %collective-permute-start.21 = (bf16[512,512]{1,0:T(8,128)(2,1)}, bf16[512,512]{1,0:T(8,128)(2,1)S(1)}, u32[]{:S(2)}, u32[]{:S(2)}) collective-permute-start(bf16[512,512]{1,0:T(8,128)(2,1)} %multiply_convert_fusion.1.refs_3_), channel_id=1, source_target_pairs={{0,2},{1,3},{2,0},{3,1},{4,6},{5,7},{6,4},{7,5},{8,10},{9,11},{10,... | collective-permute-start | bytes 1572872 | tf_op jit(solution)/shard_map/ppermute | solution.py:610
  115.2 1.9 %collective-permute-start.22 = (bf16[512,512]{1,0:T(8,128)(2,1)S(1)}, bf16[512,512]{1,0:T(8,128)(2,1)S(1)}, u32[]{:S(2)}, u32[]{:S(2)}) collective-permute-start(bf16[512,512]{1,0:T(8,128)(2,1)S(1)} %collective-permute-done.21.refs_5_), channel_id=1, source_target_pairs={{0,1},{1,0},{2,3},{3,2},{4,5},{5,4},{6,7},{7,6},{8,9},{9,8},{10,11... | collective-permute-start | bytes 1572872 | tf_op jit(solution)/shard_map/ppermute | solution.py:465
  121.9 9.7 %collective-permute-start.23 = (bf16[8,128,128]{2,1,0:T(8,128)(2,1)S(1)}, bf16[8,128,128]{2,1,0:T(8,128)(2,1)S(1)}, u32[]{:S(2)}, u32[]{:S(2)}) collective-permute-start(bf16[8,128,128]{2,1,0:T(8,128)(2,1)S(1)} %get-tuple-element.94.refs_9_), channel_id=1, source_target_pairs={{0,4},{4,0},{8,12},{12,8},{16,20},{20,16},{24,28},{28,24},{1,5},{5... | collective-permute-start | bytes 786440 | tf_op jit(solution)/shard_map/ppermute | solution.py:465
  131.6 8.2 %copy-start.10 = (bf16[8,128,128]{2,1,0:T(8,128)(2,1)}, bf16[8,128,128]{2,1,0:T(8,128)(2,1)S(1)}, u32[]{:S(2)}) copy-start(bf16[8,128,128]{2,1,0:T(8,128)(2,1)S(1)} %collective-permute-done.23) | copy-start | bytes 786436
  131.7 8.1 %collective-permute-start.24 = (bf16[8,128,128]{2,1,0:T(8,128)(2,1)S(1)}, bf16[8,128,128]{2,1,0:T(8,128)(2,1)S(1)}, u32[]{:S(2)}, u32[]{:S(2)}) collective-permute-start(bf16[8,128,128]{2,1,0:T(8,128)(2,1)S(1)} %fusion.6.refs_9_), channel_id=1, source_target_pairs={{0,8},{4,12},{8,0},{12,4},{16,24},{20,28},{24,16},{28,20},{1,9},{5... | collective-permute-start | bytes 786440 | tf_op jit(solution)/shard_map/ppermute | solution.py:465
  140.0 13.9 %collective-permute-start.25 = (bf16[8,128,128]{2,1,0:T(8,128)(2,1)S(1)}, bf16[8,128,128]{2,1,0:T(8,128)(2,1)S(1)}, u32[]{:S(2)}, u32[]{:S(2)}) collective-permute-start(bf16[8,128,128]{2,1,0:T(8,128)(2,1)S(1)} %fusion.4.refs_7_), channel_id=1, source_target_pairs={{0,16},{4,20},{8,24},{12,28},{16,0},{20,4},{24,8},{28,12},{1,17},{... | collective-permute-start | bytes 786440 | tf_op jit(solution)/shard_map/ppermute | solution.py:465
  142.0 11.9 %copy-start.11 = (bf16[8,128,128]{2,1,0:T(8,128)(2,1)S(1)}, bf16[8,128,128]{2,1,0:T(8,128)(2,1)}, u32[]{:S(2)}) copy-start(bf16[8,128,128]{2,1,0:T(8,128)(2,1)} %copy-done.10) | copy-start | bytes 786436
  142.0 13.0 %copy-start.1 = (bf16[512,2048]{1,0:T(8,128)(2,1)S(1)}, bf16[512,2048]{1,0:T(8,128)(2,1)}, u32[]{:S(2)}) copy-start(bf16[512,2048]{1,0:T(8,128)(2,1)} %refs_1_.21) | copy-start | bytes 6291460
  142.0 13.0 %copy-start.2 = (bf16[512,2048]{1,0:T(8,128)(2,1)S(1)}, bf16[512,2048]{1,0:T(8,128)(2,1)}, u32[]{:S(2)}) copy-start(bf16[512,2048]{1,0:T(8,128)(2,1)} %refs_2_.17) | copy-start | bytes 6291460
  142.0 13.0 %copy-start.4 = (bf16[512,1024]{1,0:T(8,128)(2,1)S(1)}, bf16[512,1024]{1,0:T(8,128)(2,1)}, u32[]{:S(2)}) copy-start(bf16[512,1024]{1,0:T(8,128)(2,1)} %get-tuple-element.113.refs_5_) | copy-start | bytes 3145732
  150.7 4.3 %copy-start.3 = (bf16[512,1024]{1,0:T(8,128)(2,1)S(1)}, bf16[512,1024]{1,0:T(8,128)(2,1)}, u32[]{:S(2)}) copy-start(bf16[512,1024]{1,0:T(8,128)(2,1)} %get-tuple-element.112.refs_4_) | copy-start | bytes 3145732
  154.1 7.5 %collective-permute-start.26 = (bf16[8,128,128]{2,1,0:T(8,128)(2,1)S(1)}, bf16[8,128,128]{2,1,0:T(8,128)(2,1)S(1)}, u32[]{:S(2)}, u32[]{:S(2)}) collective-permute-start(bf16[8,128,128]{2,1,0:T(8,128)(2,1)S(1)} %get-tuple-element.120), channel_id=1, source_target_pairs={{0,4},{4,0},{8,12},{12,8},{16,20},{20,16},{24,28},{28,24},{1,5},{5... | collective-permute-start | bytes 786440 | tf_op jit(solution)/shard_map/ppermute | solution.py:465
  155.0 6.7 %copy-start.7 = (bf16[512,1024]{1,0:T(8,128)(2,1)S(1)}, bf16[512,1024]{1,0:T(8,128)(2,1)}, u32[]{:S(2)}) copy-start(bf16[512,1024]{1,0:T(8,128)(2,1)} %get-tuple-element.110.refs_4_) | copy-start | bytes 3145732
  155.0 6.6 %copy-start.8 = (bf16[512,1024]{1,0:T(8,128)(2,1)S(1)}, bf16[512,1024]{1,0:T(8,128)(2,1)}, u32[]{:S(2)}) copy-start(bf16[512,1024]{1,0:T(8,128)(2,1)} %get-tuple-element.111.refs_5_) | copy-start | bytes 3145732
